TPU v7x, 32 devices: a whole 2x2x4 slice. The times are simulated.
32 devices in a mesh: groups: 2 (over x), seq: 16 (over z, y, core).
Axes of the slice: x: 2, y: 2, z: 4, core: 2. Of those that a mesh axis runs over, the one named last changes fastest.
Arguments:
- queries: bfloat16 [8192, 1280], P(('groups', 'seq')), parts along dimension 0, may hold values from -6 to 6
- keys: bfloat16 [8192, 1280], P(('groups', 'seq')), parts along dimension 0, may hold values from -6 to 6
- values: bfloat16 [8192, 1280], P(('groups', 'seq')), parts along dimension 0, may hold values from -6 to 6
- cotangent: bfloat16 [8192, 1280], P(('groups', 'seq')), parts along dimension 0, may hold values from -6 to 6
- local_blocks: int32 [64, 3], P('groups'), parts along dimension 0, may hold values from -1 to 31, as said below
- far_blocks: int32 [64, 4], P('groups'), parts along dimension 0, may hold values from -1 to 29, as said below
- counts: int32 [64], P('groups'), parts along dimension 0, may hold values from 2 to 128
Outputs:
- attended: bfloat16 [8192, 1280], P(('groups', 'seq')), parts along dimension 0
- grad_queries: bfloat16 [8192, 1280], P(('groups', 'seq')), parts along dimension 0
- grad_keys: bfloat16 [8192, 1280], P(('groups', 'seq')), parts along dimension 0
- grad_values: bfloat16 [8192, 1280], P(('groups', 'seq')), parts along dimension 0
There are 2 independent parts, one for each index of `groups`. A program takes and returns all parts, laid end to end along the dimension named above; each array names one. Nothing has to cross between parts.
Inputs may be any that keep to these rules, and one draw needn't show every extreme that they name: `local_blocks`: row b holds block b itself first, then 3 - 1 distinct blocks whose index differs from b by 1 to 2, or -1 where such a block lies outside the sequence. `far_blocks`: each entry of row b is -1 or a block whose index lies in [(b // 2 - k) * 2, (b // 2 - k + 1) * 2) for some k from 1 to 2; it is -1 exactly where that range would start below 0. Entries may repeat.
All inputs are finite; a program needn't handle non-finite values.
Results may differ from a plain program's by a relative error of at most 0.027.
Values may be sent and summed in bfloat16 or wider, within the bound.
No kernel may reach another device: no remote copies, remote signals or barrier semaphores. Data moves between devices by JAX's collectives and lax.ppermute only.
A program may use at most 128 MiB of HBM per device.

v0:
```python
import math

import jax
import jax.numpy as jnp
from jax import lax
from jax.experimental import pallas as pl
from jax.experimental.pallas import tpu as pltpu
from jax.sharding import PartitionSpec as P

HEADS = 16
BLK = 128
PLANE = 4
CHUNKS = (2, 2)
FAR_UP = 2
WINDOW = 4
CHAIN = PLANE + FAR_UP + 1
F32 = jnp.float32
BF16 = jnp.bfloat16
ANY = pl.BlockSpec(memory_space=pl.ANY)
SMEM = pl.BlockSpec(memory_space=pltpu.SMEM)
VMEM = pl.BlockSpec(memory_space=pltpu.VMEM)


def params(mib=48):
    return pltpu.CompilerParams(vmem_limit_bytes=mib << 20)


def run_copies(copies):
    for copy in copies:
        copy.start()
    for copy in copies:
        copy.wait()


def prep_kernel(head_size, roles, *refs):
    inputs = refs[:4]
    outs = refs[4 : 4 + PLANE * len(CHUNKS)]
    turned, sems = refs[4 + PLANE * len(CHUNKS) :]
    for index, ref in enumerate(inputs):
        turned[index] = ref[...].T
    place = roles[0]
    copies = []
    per_device = HEADS // PLANE
    first = 0
    for chunk, heads in enumerate(CHUNKS):
        for hop in range(PLANE):
            group = place ^ hop
            row = pl.multiple_of((group * per_device + first) * head_size, 16)
            number = chunk * PLANE + hop
            copies.append(
                pltpu.make_async_copy(
                    turned.at[:, pl.ds(row, heads * head_size)], outs[number], sems.at[number]
                )
            )
        first += heads
    run_copies(copies)


def limits_kernel(roles, local_blocks, far_blocks, counts, out):
    blocks = counts.shape[0]
    first = roles[1] * (PLANE * 2)
    for query in range(PLANE * 2):
        listed = [local_blocks[first + query, s] for s in range(local_blocks.shape[1])]
        listed += [far_blocks[first + query, s] for s in range(far_blocks.shape[1])]
        for slot in range(WINDOW * 2):
            key = first - 2 * FAR_UP + (query // 2) * 2 + slot
            found = listed[0] == key
            for entry in listed[1:]:
                found = found | (entry == key)
            inside = (key >= 0) & (key < blocks)
            count = counts[jnp.clip(key, 0, blocks - 1)]
            out[query * WINDOW * 2 + slot] = jnp.where(found & inside, count, 0)


def pack_kernel(roles, *refs):
    pieces = refs[:PLANE]
    even, odd = refs[PLANE : PLANE + 2]
    plane, sems = refs[PLANE + 2 :]
    place, parity = roles[0], roles[2]
    run_copies(
        [
            pltpu.make_async_copy(
                pieces[hop].at[pl.ds(0, 2)], plane.at[place ^ hop], sems.at[hop]
            )
            for hop in range(PLANE)
        ]
    )
    run_copies(
        [
            pltpu.make_async_copy(plane.at[pl.ds(2 - 2 * parity, 2)], even, sems.at[0]),
            pltpu.make_async_copy(plane.at[pl.ds(2 * parity, 2)], odd, sems.at[1]),
        ]
    )


def dot(a, b, left, right):
    return lax.dot_general(a, b, (((left,), (right,)), ((), ())), preferred_element_type=F32)


def main_kernel(head_size, heads, roles, limits, *refs):
    pieces = refs[:PLANE]
    even_in, odd_in = refs[PLANE : PLANE + 2]
    rest = refs[PLANE + 2 :]
    outs = rest[:PLANE]
    local_out, even_out, odd_out = rest[PLANE : PLANE + 3]
    chain, query, result, key_sums, sums, sems = rest[PLANE + 3 :]
    place, parity = roles[0], roles[2]
    copies = []
    for hop in range(PLANE):
        unit = place ^ hop
        copies.append(
            pltpu.make_async_copy(
                pieces[hop].at[pl.ds(0, 2)], chain.at[FAR_UP + unit], sems.at[2 * hop]
            )
        )
        copies.append(
            pltpu.make_async_copy(
                pieces[hop].at[pl.ds(2, 2)], query.at[unit], sems.at[2 * hop + 1]
            )
        )
    above = FAR_UP + PLANE
    copies.append(
        pltpu.make_async_copy(
            even_in, chain.at[pl.ds((1 - parity) * above, 2)], sems.at[2 * PLANE]
        )
    )
    copies.append(
        pltpu.make_async_copy(odd_in, chain.at[pl.ds(parity * above, 2)], sems.at[2 * PLANE + 1])
    )
    for copy in copies:
        copy.start()
    key_sums[...] = jnp.zeros_like(key_sums)
    for copy in copies:
        copy.wait()

    scale = 1.0 / math.sqrt(head_size)
    rate = scale * math.log2(math.e)
    tokens = 2 * BLK
    row = lax.broadcasted_iota(jnp.int32, (BLK, tokens), 0)
    lane = lax.broadcasted_iota(jnp.int32, (1, tokens), 1)

    def step(index, carry):
        head, unit = index // PLANE, index % PLANE
        query_t = query[unit, 0, head]
        grad_t = query[unit, 1, head]
        scores = []
        peak = jnp.full((1, tokens), -1e30, F32)
        for k in range(WINDOW):
            tile = dot(chain[unit + k, 0, head], query_t, 0, 0)
            for half in range(2):
                slot = 2 * k + half
                base = unit * 2 * WINDOW * 2 + slot
                limit = jnp.where(lane < BLK, limits[base], limits[base + WINDOW * 2])
                part = jnp.where(row < limit, tile[half * BLK : (half + 1) * BLK], -1e30)
                peak = jnp.maximum(peak, jnp.max(part, axis=0, keepdims=True))
                scores.append(part)
        total = jnp.zeros((1, tokens), F32)
        powers = []
        for part in scores:
            power = jnp.exp2((part - peak) * rate)
            total = total + jnp.sum(power, axis=0, keepdims=True)
            powers.append(power)
        powers = [
            jnp.concatenate(powers[2 * k : 2 * k + 2], axis=0) for k in range(WINDOW)
        ]
        weights = [power.astype(BF16) for power in powers]
        inverse = 1.0 / total
        out_t = dot(chain[unit, 1, head], weights[0], 1, 0)
        for k in range(1, WINDOW):
            out_t = out_t + dot(chain[unit + k, 1, head], weights[k], 1, 0)
        attended = (out_t * inverse).astype(BF16)
        grad_wide = grad_t.astype(F32)
        delta = jnp.sum(grad_wide * attended.astype(F32), axis=0, keepdims=True) * inverse
        grad_scaled = (grad_wide * inverse).astype(BF16)
        query_grad = jnp.zeros((head_size, tokens), F32)
        for k in range(WINDOW):
            grad_chance = dot(chain[unit + k, 1, head], grad_scaled, 0, 0)
            grad_scores = (powers[k] * (grad_chance - delta)).astype(BF16)
            query_grad = query_grad + dot(chain[unit + k, 0, head], grad_scores, 1, 0)
            key_sums[unit + k, 0, head] += dot(query_t, grad_scores, 1, 1)
            key_sums[unit + k, 1, head] += dot(grad_scaled, weights[k], 1, 1)
        result[unit, 0, head] = attended
        result[unit, 1, head] = (query_grad * scale).astype(BF16)
        return carry

    lax.fori_loop(0, heads * PLANE, step, 0)
    for unit in range(CHAIN + 1):
        sums[unit, 0] = (key_sums[unit, 0] * scale).astype(BF16)
        sums[unit, 1] = key_sums[unit, 1].astype(BF16)
    copies = [
        pltpu.make_async_copy(result.at[place ^ hop], outs[hop], sems.at[hop])
        for hop in range(PLANE)
    ]
    copies.append(
        pltpu.make_async_copy(sums.at[pl.ds(FAR_UP, PLANE)], local_out, sems.at[PLANE])
    )
    copies.append(
        pltpu.make_async_copy(
            sums.at[pl.ds((1 - parity) * above, 2)], even_out, sems.at[PLANE + 1]
        )
    )
    copies.append(
        pltpu.make_async_copy(sums.at[pl.ds(parity * above, 2)], odd_out, sems.at[PLANE + 2])
    )
    run_copies(copies)


def join_kernel(roles, local, even_in, odd_in, *refs):
    outs = refs[:PLANE]
    held, sems = refs[PLANE:]
    place, parity = roles[0], roles[2]
    below_ok, above_ok = roles[3], roles[4]
    held[...] = local[...]

    def take(below, above):
        @pl.when(below_ok == 1)
        def _():
            held[0] = (held[0].astype(F32) + below[0].astype(F32)).astype(BF16)

        @pl.when(above_ok == 1)
        def _():
            for unit in range(2):
                held[2 + unit] = (held[2 + unit].astype(F32) + above[unit].astype(F32)).astype(
                    BF16
                )

    @pl.when(parity == 0)
    def _():
        take(odd_in, even_in)

    @pl.when(parity == 1)
    def _():
        take(even_in, odd_in)

    run_copies(
        [
            pltpu.make_async_copy(held.at[place ^ hop], outs[hop], sems.at[hop])
            for hop in range(PLANE)
        ]
    )


def finish_kernel(head_size, roles, *refs):
    count = PLANE * len(CHUNKS)
    pieces = refs[:count]
    first_out, second_out, turned, sems = refs[count:]
    place = roles[0]
    per_device = HEADS // PLANE
    copies = []
    first = 0
    for chunk, heads in enumerate(CHUNKS):
        for hop in range(PLANE):
            group = place ^ hop
            row = pl.multiple_of((group * per_device + first) * head_size, 16)
            number = chunk * PLANE + hop
            copies.append(
                pltpu.make_async_copy(
                    pieces[number], turned.at[:, pl.ds(row, heads * head_size)], sems.at[number]
                )
            )
        first += heads
    run_copies(copies)
    first_out[...] = turned[0].T
    second_out[...] = turned[1].T


def body(queries, keys, values, cotangent, local_blocks, far_blocks, counts):
    tokens, width = queries.shape
    head_size = width // HEADS
    size = lax.axis_size("seq")
    planes = size // PLANE
    device = lax.axis_index("seq")
    level = device // PLANE
    roles = jnp.stack(
        [
            device % PLANE,
            level,
            level % 2,
            (level > 0).astype(jnp.int32),
            (level < planes - 1).astype(jnp.int32),
        ]
    ).astype(jnp.int32)

    def swap(array, hop):
        pairs = [(i, (i // PLANE) * PLANE + ((i % PLANE) ^ hop)) for i in range(size)]
        return lax.ppermute(array, "seq", pairs)

    def level_swap(array, odd):
        pairs = []
        for i in range(size):
            z = i // PLANE
            other = z + 1 if z % 2 == odd else z - 1
            pairs.append((i, i + (other - z) * PLANE if 0 <= other < planes else i))
        return lax.ppermute(array, "seq", pairs)

    def piece(tensors, heads):
        return jax.ShapeDtypeStruct((tensors, heads * head_size, tokens), BF16)

    pieces = pl.pallas_call(
        lambda *refs: prep_kernel(head_size, *refs),
        out_shape=[piece(4, heads) for heads in CHUNKS for _ in range(PLANE)],
        in_specs=[SMEM] + [VMEM] * 4,
        out_specs=[ANY] * (PLANE * len(CHUNKS)),
        scratch_shapes=[
            pltpu.VMEM((4, width, tokens), BF16),
            pltpu.SemaphoreType.DMA((PLANE * len(CHUNKS),)),
        ],
        compiler_params=params(),
    )(roles, keys, values, queries, cotangent)
    limits = pl.pallas_call(
        limits_kernel,
        out_shape=jax.ShapeDtypeStruct((PLANE * 2 * WINDOW * 2,), jnp.int32),
        in_specs=[SMEM] * 4,
        out_specs=SMEM,
    )(roles, local_blocks, far_blocks, counts)

    query_pieces = []
    key_pieces = []
    for chunk, heads in enumerate(CHUNKS):
        own = pieces[chunk * PLANE]
        held = [own] + [swap(pieces[chunk * PLANE + hop], hop) for hop in range(1, PLANE)]
        pair = jax.ShapeDtypeStruct((2, 2, heads * head_size, tokens), BF16)
        even, odd = pl.pallas_call(
            pack_kernel,
            out_shape=[pair, pair],
            in_specs=[SMEM] + [ANY] * PLANE,
            out_specs=[ANY, ANY],
            scratch_shapes=[
                pltpu.VMEM((PLANE, 2, heads * head_size, tokens), BF16),
                pltpu.SemaphoreType.DMA((PLANE,)),
            ],
            compiler_params=params(),
        )(roles, *held)
        even, odd = level_swap(even, 0), level_swap(odd, 1)
        shape = (heads, head_size, tokens)
        results = pl.pallas_call(
            lambda *refs, heads=heads: main_kernel(head_size, heads, *refs),
            out_shape=[jax.ShapeDtypeStruct((2,) + shape, BF16)] * PLANE
            + [jax.ShapeDtypeStruct((PLANE, 2) + shape, BF16)]
            + [jax.ShapeDtypeStruct((2, 2) + shape, BF16)] * 2,
            in_specs=[SMEM, SMEM] + [ANY] * (PLANE + 2),
            out_specs=[ANY] * (PLANE + 3),
            scratch_shapes=[
                pltpu.VMEM((CHAIN + 1, 2) + shape, BF16),
                pltpu.VMEM((PLANE, 2) + shape, BF16),
                pltpu.VMEM((PLANE, 2) + shape, BF16),
                pltpu.VMEM((CHAIN + 1, 2) + shape, F32),
                pltpu.VMEM((CHAIN + 1, 2) + shape, BF16),
                pltpu.SemaphoreType.DMA((2 * PLANE + 2,)),
            ],
            compiler_params=params(),
        )(
            roles,
            limits,
            *[part.reshape((4,) + shape) for part in held],
            even.reshape((2, 2) + shape),
            odd.reshape((2, 2) + shape),
        )
        flat = (2, heads * head_size, tokens)
        out = [part.reshape(flat) for part in results[:PLANE]]
        query_pieces += [out[0]] + [swap(out[hop], hop) for hop in range(1, PLANE)]
        local, even, odd = results[PLANE:]
        even, odd = level_swap(even, 0), level_swap(odd, 1)
        back = pl.pallas_call(
            join_kernel,
            out_shape=[piece(2, heads)] * PLANE,
            in_specs=[SMEM] + [VMEM] * 3,
            out_specs=[ANY] * PLANE,
            scratch_shapes=[
                pltpu.VMEM((PLANE,) + flat, BF16),
                pltpu.SemaphoreType.DMA((PLANE,)),
            ],
            compiler_params=params(),
        )(roles, local.reshape((PLANE,) + flat), even.reshape((2,) + flat), odd.reshape((2,) + flat))
        key_pieces += [back[0]] + [swap(back[hop], hop) for hop in range(1, PLANE)]

    def finish(parts):
        return pl.pallas_call(
            lambda *refs: finish_kernel(head_size, *refs),
            out_shape=[jax.ShapeDtypeStruct((tokens, width), BF16)] * 2,
            in_specs=[SMEM] + [ANY] * len(parts),
            out_specs=[VMEM, VMEM],
            scratch_shapes=[
                pltpu.VMEM((2, width, tokens), BF16),
                pltpu.SemaphoreType.DMA((len(parts),)),
            ],
            compiler_params=params(),
        )(roles, *parts)

    attended, query_grad = finish(query_pieces)
    key_grad, value_grad = finish(key_pieces)
    return attended, query_grad, key_grad, value_grad


def solution(mesh):
    rows = P(("groups", "seq"), None)
    return jax.shard_map(
        body,
        mesh=mesh,
        in_specs=(rows, rows, rows, rows, P("groups", None), P("groups", None), P("groups")),
        out_specs=(rows, rows, rows, rows),
        check_vma=False,
    )
```

profile of v0, /device:TPU:0, one launch (start us, length us, event | category | flops | bytes accessed | tf_op | source)
XLA Modules:
  0.0 124.2 jit_solution(18434597124982850045)
XLA Ops:
  5.1 1.7 %shard_map.103 = (bf16[4,160,256]{2,1,0:T(8,128)(2,1)S(1)}, bf16[4,160,256]{2,1,0:T(8,128)(2,1)S(1)}, bf16[4,160,256]{2,1,0:T(8,128)(2,1)S(1)}, bf16[4,160,256]{...) custom-call(s32[5]{0:T(128)S(1)} %stack.31.roles.refs_0_, ...), custom_call_target="tpu_custom_call" | custom-call | tf_op jit(solution)/shard_map/pallas_call | solution.py:299
  7.3 2.6 %collective-permute-start.9 = (bf16[4,160,256]{2,1,0:T(8,128)(2,1)S(1)}, bf16[4,160,256]{2,1,0:T(8,128)(2,1)S(1)}, u32[]{:S(2)}, u32[]{:S(2)}) collective-permute-start(bf16[4,160,256]{2,1,0:T(8,128)(2,1)S(1)} %get-tuple-element.54), channel_id=1, source_target_pairs={{0,2},{1,3},{2,0},{3,1},{4,6},{5,7},{6,4},{7,5},{8,10},{9,11},{10,... | collective-permute-start | bytes 983048 | tf_op jit(solution)/shard_map/ppermute | solution.py:286
  10.1 1.9 %collective-permute-start.1 = (bf16[4,160,256]{2,1,0:T(8,128)(2,1)S(1)}, bf16[4,160,256]{2,1,0:T(8,128)(2,1)S(1)}, u32[]{:S(2)}, u32[]{:S(2)}) collective-permute-start(bf16[4,160,256]{2,1,0:T(8,128)(2,1)S(1)} %get-tuple-element.44), channel_id=1, source_target_pairs={{0,2},{1,3},{2,0},{3,1},{4,6},{5,7},{6,4},{7,5},{8,10},{9,11},{10,... | collective-permute-start | bytes 983048 | tf_op jit(solution)/shard_map/ppermute | solution.py:286
  12.1 6.4 %collective-permute-done.9.refs_2_ = bf16[4,160,256]{2,1,0:T(8,128)(2,1)S(1)} collective-permute-done((bf16[4,160,256]{2,1,0:T(8,128)(2,1)S(1)}, bf16[4,160,256]{2,1,0:T(8,128)(2,1)S(1)}, u32[]{:S(2)}, u32[]{:S(2)}) %collective-permute-start.9) | collective-permute-done | bytes 327712 | tf_op jit(solution)/shard_map/ppermute | solution.py:286
  18.5 6.5 %collective-permute-done.10.refs_3_ = bf16[4,160,256]{2,1,0:T(8,128)(2,1)S(1)} collective-permute-done((bf16[4,160,256]{2,1,0:T(8,128)(2,1)S(1)}, bf16[4,160,256]{2,1,0:T(8,128)(2,1)S(1)}, u32[]{:S(2)}, u32[]{:S(2)}) %collective-permute-start.10) | collective-permute-done | bytes 327712 | tf_op jit(solution)/shard_map/ppermute | solution.py:286
  25.0 2.3 %shard_map.106 = (bf16[2,2,160,256]{3,2,1,0:T(8,128)(2,1)}, bf16[2,2,160,256]{3,2,1,0:T(8,128)(2,1)}) custom-call(s32[5]{0:T(128)S(1)} %stack.31.roles.refs_0_, bf16[4,160,256]{2,1,0:T(8,128)(2,1)S(1)} %get-tuple-element.52.refs_0_, bf16[4,160,256]{2,1,0:T(8,128)(2,1)S(1)} %collective-permute-done.8.refs_1_, ...), custom_call_target="tpu_custom_call" | custom-call | tf_op jit(solution)/shard_map/pallas_call | solution.py:323
  27.2 1.7 %collective-permute-start.11 = (bf16[2,2,160,256]{3,2,1,0:T(8,128)(2,1)}, bf16[2,2,160,256]{3,2,1,0:T(8,128)(2,1)}, u32[]{:S(2)}, u32[]{:S(2)}) collective-permute-start(bf16[2,2,160,256]{3,2,1,0:T(8,128)(2,1)} %get-tuple-element.56), channel_id=1, source_target_pairs={{0,4},{1,5},{2,6},{3,7},{4,0},{5,1},{6,2},{7,3},{8,12},{9,13},{10,... | collective-permute-start | bytes 983048 | tf_op jit(solution)/shard_map/ppermute | solution.py:294
  28.9 3.9 %collective-permute-start.12 = (bf16[2,2,160,256]{3,2,1,0:T(8,128)(2,1)}, bf16[2,2,160,256]{3,2,1,0:T(8,128)(2,1)}, u32[]{:S(2)}, u32[]{:S(2)}) collective-permute-start(bf16[2,2,160,256]{3,2,1,0:T(8,128)(2,1)} %get-tuple-element.57), channel_id=1, source_target_pairs={{0,0},{1,1},{2,2},{3,3},{4,8},{5,9},{6,10},{7,11},{8,4},{9,5},{10,... | collective-permute-start | bytes 983048 | tf_op jit(solution)/shard_map/ppermute | solution.py:294
  32.8 6.2 %collective-permute-done.2.refs_3_ = bf16[4,160,256]{2,1,0:T(8,128)(2,1)S(1)} collective-permute-done((bf16[4,160,256]{2,1,0:T(8,128)(2,1)S(1)}, bf16[4,160,256]{2,1,0:T(8,128)(2,1)S(1)}, u32[]{:S(2)}, u32[]{:S(2)}) %collective-permute-start.2) | collective-permute-done | bytes 327712 | tf_op jit(solution)/shard_map/ppermute | solution.py:286
  39.0 2.3 %shard_map.104 = (bf16[2,2,160,256]{3,2,1,0:T(8,128)(2,1)}, bf16[2,2,160,256]{3,2,1,0:T(8,128)(2,1)}) custom-call(s32[5]{0:T(128)S(1)} %stack.31.roles.refs_0_, bf16[4,160,256]{2,1,0:T(8,128)(2,1)S(1)} %get-tuple-element.42.refs_0_, bf16[4,160,256]{2,1,0:T(8,128)(2,1)S(1)} %collective-permute-done.refs_1_, ...), custom_call_target="tpu_custom_call" | custom-call | tf_op jit(solution)/shard_map/pallas_call | solution.py:323
  41.3 1.7 %collective-permute-start.3 = (bf16[2,2,160,256]{3,2,1,0:T(8,128)(2,1)}, bf16[2,2,160,256]{3,2,1,0:T(8,128)(2,1)S(1)}, u32[]{:S(2)}, u32[]{:S(2)}) collective-permute-start(bf16[2,2,160,256]{3,2,1,0:T(8,128)(2,1)} %get-tuple-element.46), channel_id=1, source_target_pairs={{0,4},{1,5},{2,6},{3,7},{4,0},{5,1},{6,2},{7,3},{8,12},{9,13},{10,... | collective-permute-start | bytes 983048 | tf_op jit(solution)/shard_map/ppermute | solution.py:294
  43.0 1.8 %collective-permute-start.4 = (bf16[2,2,160,256]{3,2,1,0:T(8,128)(2,1)}, bf16[2,2,160,256]{3,2,1,0:T(8,128)(2,1)S(1)}, u32[]{:S(2)}, u32[]{:S(2)}) collective-permute-start(bf16[2,2,160,256]{3,2,1,0:T(8,128)(2,1)} %get-tuple-element.47), channel_id=1, source_target_pairs={{0,0},{1,1},{2,2},{3,3},{4,8},{5,9},{6,10},{7,11},{8,4},{9,5},{10,... | collective-permute-start | bytes 983048 | tf_op jit(solution)/shard_map/ppermute | solution.py:294
  46.1 2.1 %shard_map.102.refs_1_ = s32[64]{0:T(128)} custom-call(s32[5]{0:T(128)} %copy-done.4, s32[32,3]{1,0:T(8,128)} %copy.11.local_blocks, s32[32,4]{1,0:T(8,128)} %copy.12.far_blocks, s32[32]{0:T(128)} %counts.1), custom_call_target="tpu_custom_call" | custom-call | tf_op jit(solution)/shard_map/pallas_call | solution.py:310
  48.9 18.0 %shard_map.107 = (bf16[2,2,80,256]{3,2,1,0:T(8,128)(2,1)S(1)}, bf16[2,2,80,256]{3,2,1,0:T(8,128)(2,1)S(1)}, bf16[2,2,80,256]{3,2,1,0:T(8,128)(2,1)S(1)}, bf16[2,...) custom-call(s32[5]{0:T(128)S(1)} %copy-done.5, ...), custom_call_target="tpu_custom_call" | custom-call | tf_op jit(solution)/shard_map/pallas_call | solution.py:336
  67.0 3.5 %collective-permute-start.21 = (bf16[2,2,2,80,256]{4,3,2,1,0:T(8,128)(2,1)S(1)}, bf16[2,2,2,80,256]{4,3,2,1,0:T(8,128)(2,1)S(1)}, u32[]{:S(2)}, u32[]{:S(2)}) collective-permute-start(bf16[2,2,2,80,256]{4,3,2,1,0:T(8,128)(2,1)S(1)} %get-tuple-element.72), channel_id=1, source_target_pairs={{0,4},{1,5},{2,6},{3,7},{4,0},{5,1},{6,2},{7,3},{8,12},{9,13},{10,... | collective-permute-start | bytes 983048 | tf_op jit(solution)/shard_map/ppermute | solution.py:294
  71.2 17.4 %shard_map.105 = (bf16[2,2,80,256]{3,2,1,0:T(8,128)(2,1)S(1)}, bf16[2,2,80,256]{3,2,1,0:T(8,128)(2,1)S(1)}, bf16[2,2,80,256]{3,2,1,0:T(8,128)(2,1)S(1)}, bf16[2,...) custom-call(s32[5]{0:T(128)S(1)} %copy-done.5, ...), custom_call_target="tpu_custom_call" | custom-call | tf_op jit(solution)/shard_map/pallas_call | solution.py:336
  94.7 3.2 %collective-permute-done.14.refs_7_ = bf16[2,160,256]{2,1,0:T(8,128)(2,1)S(1)} collective-permute-done((bf16[2,160,256]{2,1,0:T(8,128)(2,1)S(1)}, bf16[2,160,256]{2,1,0:T(8,128)(2,1)S(1)}, u32[]{:S(2)}, u32[]{:S(2)}) %collective-permute-start.14) | collective-permute-done | bytes 163872 | tf_op jit(solution)/shard_map/ppermute | solution.py:286
  103.2 1.8 %collective-permute-done.6.refs_3_ = bf16[2,160,256]{2,1,0:T(8,128)(2,1)S(1)} collective-permute-done((bf16[2,160,256]{2,1,0:T(8,128)(2,1)S(1)}, bf16[2,160,256]{2,1,0:T(8,128)(2,1)S(1)}, u32[]{:S(2)}, u32[]{:S(2)}) %collective-permute-start.6) | collective-permute-done | bytes 163872 | tf_op jit(solution)/shard_map/ppermute | solution.py:286
  105.0 2.5 %collective-permute-done.7.refs_4_ = bf16[2,160,256]{2,1,0:T(8,128)(2,1)S(1)} collective-permute-done((bf16[2,160,256]{2,1,0:T(8,128)(2,1)S(1)}, bf16[2,160,256]{2,1,0:T(8,128)(2,1)S(1)}, u32[]{:S(2)}, u32[]{:S(2)}) %collective-permute-start.7) | collective-permute-done | bytes 163872 | tf_op jit(solution)/shard_map/ppermute | solution.py:286
  109.7 2.8 %shard_map.108 = (bf16[256,1280]{1,0:T(8,128)(2,1)}, bf16[256,1280]{1,0:T(8,128)(2,1)}) custom-call(s32[5]{0:T(128)S(1)} %copy-done.5, bf16[2,160,256]{2,1,0:T(8,128)(2,1)S(1)} %bitcast.48, bf16[2,160,256]{2,1,0:T(8,128)(2,1)S(1)} %collective-permute-done.5.refs_2_, bf16[2,160,256]{2,1,0:T(8,128)(2,1)S(1)} %collective-permute-done.6.refs_3_, ...), custom_call_target="tpu_custom_call" | custom-call | tf_op jit(solution)/shard_map/pallas_call | solution.py:378
  112.5 2.1 %collective-permute-done.25.refs_8_ = bf16[2,160,256]{2,1,0:T(8,128)(2,1)S(1)} collective-permute-done((bf16[2,160,256]{2,1,0:T(8,128)(2,1)S(1)}, bf16[2,160,256]{2,1,0:T(8,128)(2,1)S(1)}, u32[]{:S(2)}, u32[]{:S(2)}) %collective-permute-start.25) | collective-permute-done | bytes 163872 | tf_op jit(solution)/shard_map/ppermute | solution.py:286
  114.6 4.5 %collective-permute-done.19.refs_3_ = bf16[2,160,256]{2,1,0:T(8,128)(2,1)S(1)} collective-permute-done((bf16[2,160,256]{2,1,0:T(8,128)(2,1)S(1)}, bf16[2,160,256]{2,1,0:T(8,128)(2,1)S(1)}, u32[]{:S(2)}, u32[]{:S(2)}) %collective-permute-start.19) | collective-permute-done | bytes 163872 | tf_op jit(solution)/shard_map/ppermute | solution.py:286
  119.1 2.4 %collective-permute-done.20.refs_4_ = bf16[2,160,256]{2,1,0:T(8,128)(2,1)S(1)} collective-permute-done((bf16[2,160,256]{2,1,0:T(8,128)(2,1)S(1)}, bf16[2,160,256]{2,1,0:T(8,128)(2,1)S(1)}, u32[]{:S(2)}, u32[]{:S(2)}) %collective-permute-start.20) | collective-permute-done | bytes 163872 | tf_op jit(solution)/shard_map/ppermute | solution.py:286
  121.4 2.8 %shard_map.111 = (bf16[256,1280]{1,0:T(8,128)(2,1)}, bf16[256,1280]{1,0:T(8,128)(2,1)}) custom-call(s32[5]{0:T(128)S(1)} %copy-done.5, bf16[2,160,256]{2,1,0:T(8,128)(2,1)S(1)} %get-tuple-element.67.refs_1_, bf16[2,160,256]{2,1,0:T(8,128)(2,1)S(1)} %collective-permute-done.18.refs_2_, bf16[2,160,256]{2,1,0:T(8,128)(2,1)S(1)} %collective-permute-done.19.refs_3_, ...), custom_call_target="tpu_custom_call" | custom-call | tf_op jit(solution)/shard_map/pallas_call | solution.py:378
  (59 shorter events, 21.4 us)
Async XLA Ops:
  7.3 11.2 %collective-permute-start.9 = (bf16[4,160,256]{2,1,0:T(8,128)(2,1)S(1)}, bf16[4,160,256]{2,1,0:T(8,128)(2,1)S(1)}, u32[]{:S(2)}, u32[]{:S(2)}) collective-permute-start(bf16[4,160,256]{2,1,0:T(8,128)(2,1)S(1)} %get-tuple-element.54), channel_id=1, source_target_pairs={{0,2},{1,3},{2,0},{3,1},{4,6},{5,7},{6,4},{7,5},{8,10},{9,11},{10,... | collective-permute-start | bytes 983048 | tf_op jit(solution)/shard_map/ppermute | solution.py:286
  9.9 15.1 %collective-permute-start.10 = (bf16[4,160,256]{2,1,0:T(8,128)(2,1)S(1)}, bf16[4,160,256]{2,1,0:T(8,128)(2,1)S(1)}, u32[]{:S(2)}, u32[]{:S(2)}) collective-permute-start(bf16[4,160,256]{2,1,0:T(8,128)(2,1)S(1)} %get-tuple-element.55), channel_id=1, source_target_pairs={{0,3},{1,2},{2,1},{3,0},{4,7},{5,6},{6,5},{7,4},{8,11},{9,10},{10,... | collective-permute-start | bytes 983048 | tf_op jit(solution)/shard_map/ppermute | solution.py:286
  10.0 22.8 %collective-permute-start = (bf16[4,160,256]{2,1,0:T(8,128)(2,1)S(1)}, bf16[4,160,256]{2,1,0:T(8,128)(2,1)S(1)}, u32[]{:S(2)}, u32[]{:S(2)}) collective-permute-start(bf16[4,160,256]{2,1,0:T(8,128)(2,1)S(1)} %get-tuple-element.43), channel_id=1, source_target_pairs={{0,1},{1,0},{2,3},{3,2},{4,5},{5,4},{6,7},{7,6},{8,9},{9,8},{10,11... | collective-permute-start | bytes 983048 | tf_op jit(solution)/shard_map/ppermute | solution.py:286
  10.1 22.7 %collective-permute-start.1 = (bf16[4,160,256]{2,1,0:T(8,128)(2,1)S(1)}, bf16[4,160,256]{2,1,0:T(8,128)(2,1)S(1)}, u32[]{:S(2)}, u32[]{:S(2)}) collective-permute-start(bf16[4,160,256]{2,1,0:T(8,128)(2,1)S(1)} %get-tuple-element.44), channel_id=1, source_target_pairs={{0,2},{1,3},{2,0},{3,1},{4,6},{5,7},{6,4},{7,5},{8,10},{9,11},{10,... | collective-permute-start | bytes 983048 | tf_op jit(solution)/shard_map/ppermute | solution.py:286
  12.0 27.0 %collective-permute-start.2 = (bf16[4,160,256]{2,1,0:T(8,128)(2,1)S(1)}, bf16[4,160,256]{2,1,0:T(8,128)(2,1)S(1)}, u32[]{:S(2)}, u32[]{:S(2)}) collective-permute-start(bf16[4,160,256]{2,1,0:T(8,128)(2,1)S(1)} %get-tuple-element.45), channel_id=1, source_target_pairs={{0,3},{1,2},{2,1},{3,0},{4,7},{5,6},{6,5},{7,4},{8,11},{9,10},{10,... | collective-permute-start | bytes 983048 | tf_op jit(solution)/shard_map/ppermute | solution.py:286
  27.2 21.0 %collective-permute-start.11 = (bf16[2,2,160,256]{3,2,1,0:T(8,128)(2,1)}, bf16[2,2,160,256]{3,2,1,0:T(8,128)(2,1)}, u32[]{:S(2)}, u32[]{:S(2)}) collective-permute-start(bf16[2,2,160,256]{3,2,1,0:T(8,128)(2,1)} %get-tuple-element.56), channel_id=1, source_target_pairs={{0,4},{1,5},{2,6},{3,7},{4,0},{5,1},{6,2},{7,3},{8,12},{9,13},{10,... | collective-permute-start | bytes 983048 | tf_op jit(solution)/shard_map/ppermute | solution.py:294
  28.9 19.3 %collective-permute-start.12 = (bf16[2,2,160,256]{3,2,1,0:T(8,128)(2,1)}, bf16[2,2,160,256]{3,2,1,0:T(8,128)(2,1)}, u32[]{:S(2)}, u32[]{:S(2)}) collective-permute-start(bf16[2,2,160,256]{3,2,1,0:T(8,128)(2,1)} %get-tuple-element.57), channel_id=1, source_target_pairs={{0,0},{1,1},{2,2},{3,3},{4,8},{5,9},{6,10},{7,11},{8,4},{9,5},{10,... | collective-permute-start | bytes 983048 | tf_op jit(solution)/shard_map/ppermute | solution.py:294
  41.3 29.9 %collective-permute-start.3 = (bf16[2,2,160,256]{3,2,1,0:T(8,128)(2,1)}, bf16[2,2,160,256]{3,2,1,0:T(8,128)(2,1)S(1)}, u32[]{:S(2)}, u32[]{:S(2)}) collective-permute-start(bf16[2,2,160,256]{3,2,1,0:T(8,128)(2,1)} %get-tuple-element.46), channel_id=1, source_target_pairs={{0,4},{1,5},{2,6},{3,7},{4,0},{5,1},{6,2},{7,3},{8,12},{9,13},{10,... | collective-permute-start | bytes 983048 | tf_op jit(solution)/shard_map/ppermute | solution.py:294
  43.0 28.2 %collective-permute-start.4 = (bf16[2,2,160,256]{3,2,1,0:T(8,128)(2,1)}, bf16[2,2,160,256]{3,2,1,0:T(8,128)(2,1)S(1)}, u32[]{:S(2)}, u32[]{:S(2)}) collective-permute-start(bf16[2,2,160,256]{3,2,1,0:T(8,128)(2,1)} %get-tuple-element.47), channel_id=1, source_target_pairs={{0,0},{1,1},{2,2},{3,3},{4,8},{5,9},{6,10},{7,11},{8,4},{9,5},{10,... | collective-permute-start | bytes 983048 | tf_op jit(solution)/shard_map/ppermute | solution.py:294
  67.0 23.8 %collective-permute-start.21 = (bf16[2,2,2,80,256]{4,3,2,1,0:T(8,128)(2,1)S(1)}, bf16[2,2,2,80,256]{4,3,2,1,0:T(8,128)(2,1)S(1)}, u32[]{:S(2)}, u32[]{:S(2)}) collective-permute-start(bf16[2,2,2,80,256]{4,3,2,1,0:T(8,128)(2,1)S(1)} %get-tuple-element.72), channel_id=1, source_target_pairs={{0,4},{1,5},{2,6},{3,7},{4,0},{5,1},{6,2},{7,3},{8,12},{9,13},{10,... | collective-permute-start | bytes 983048 | tf_op jit(solution)/shard_map/ppermute | solution.py:294
  70.5 21.9 %collective-permute-start.22 = (bf16[2,2,2,80,256]{4,3,2,1,0:T(8,128)(2,1)S(1)}, bf16[2,2,2,80,256]{4,3,2,1,0:T(8,128)(2,1)S(1)}, u32[]{:S(2)}, u32[]{:S(2)}) collective-permute-start(bf16[2,2,2,80,256]{4,3,2,1,0:T(8,128)(2,1)S(1)} %get-tuple-element.73), channel_id=1, source_target_pairs={{0,0},{1,1},{2,2},{3,3},{4,8},{5,9},{6,10},{7,11},{8,4},{9,5},{10,... | collective-permute-start | bytes 983048 | tf_op jit(solution)/shard_map/ppermute | solution.py:294
  88.6 10.8 %collective-permute-start.16 = (bf16[2,2,2,80,256]{4,3,2,1,0:T(8,128)(2,1)S(1)}, bf16[2,2,2,80,256]{4,3,2,1,0:T(8,128)(2,1)S(1)}, u32[]{:S(2)}, u32[]{:S(2)}) collective-permute-start(bf16[2,2,2,80,256]{4,3,2,1,0:T(8,128)(2,1)S(1)} %get-tuple-element.65), channel_id=1, source_target_pairs={{0,4},{1,5},{2,6},{3,7},{4,0},{5,1},{6,2},{7,3},{8,12},{9,13},{10,... | collective-permute-start | bytes 983048 | tf_op jit(solution)/shard_map/ppermute | solution.py:294
  90.0 9.4 %collective-permute-start.17 = (bf16[2,2,2,80,256]{4,3,2,1,0:T(8,128)(2,1)S(1)}, bf16[2,2,2,80,256]{4,3,2,1,0:T(8,128)(2,1)S(1)}, u32[]{:S(2)}, u32[]{:S(2)}) collective-permute-start(bf16[2,2,2,80,256]{4,3,2,1,0:T(8,128)(2,1)S(1)} %get-tuple-element.66), channel_id=1, source_target_pairs={{0,0},{1,1},{2,2},{3,3},{4,8},{5,9},{6,10},{7,11},{8,4},{9,5},{10,... | collective-permute-start | bytes 983048 | tf_op jit(solution)/shard_map/ppermute | solution.py:294
  90.8 7.1 %collective-permute-start.14 = (bf16[2,160,256]{2,1,0:T(8,128)(2,1)S(1)}, bf16[2,160,256]{2,1,0:T(8,128)(2,1)S(1)}, u32[]{:S(2)}, u32[]{:S(2)}) collective-permute-start(bf16[2,160,256]{2,1,0:T(8,128)(2,1)S(1)} %bitcast.53), channel_id=1, source_target_pairs={{0,2},{1,3},{2,0},{3,1},{4,6},{5,7},{6,4},{7,5},{8,10},{9,11},{10,... | collective-permute-start | bytes 491528 | tf_op jit(solution)/shard_map/ppermute | solution.py:286
  92.4 9.2 %collective-permute-start.15 = (bf16[2,160,256]{2,1,0:T(8,128)(2,1)S(1)}, bf16[2,160,256]{2,1,0:T(8,128)(2,1)S(1)}, u32[]{:S(2)}, u32[]{:S(2)}) collective-permute-start(bf16[2,160,256]{2,1,0:T(8,128)(2,1)S(1)} %bitcast.49), channel_id=1, source_target_pairs={{0,3},{1,2},{2,1},{3,0},{4,7},{5,6},{6,5},{7,4},{8,11},{9,10},{10,... | collective-permute-start | bytes 491528 | tf_op jit(solution)/shard_map/ppermute | solution.py:286
  94.2 9.0 %collective-permute-start.5 = (bf16[2,160,256]{2,1,0:T(8,128)(2,1)S(1)}, bf16[2,160,256]{2,1,0:T(8,128)(2,1)S(1)}, u32[]{:S(2)}, u32[]{:S(2)}) collective-permute-start(bf16[2,160,256]{2,1,0:T(8,128)(2,1)S(1)} %bitcast.52), channel_id=1, source_target_pairs={{0,1},{1,0},{2,3},{3,2},{4,5},{5,4},{6,7},{7,6},{8,9},{9,8},{10,11... | collective-permute-start | bytes 491528 | tf_op jit(solution)/shard_map/ppermute | solution.py:286
  97.9 7.1 %collective-permute-start.6 = (bf16[2,160,256]{2,1,0:T(8,128)(2,1)S(1)}, bf16[2,160,256]{2,1,0:T(8,128)(2,1)S(1)}, u32[]{:S(2)}, u32[]{:S(2)}) collective-permute-start(bf16[2,160,256]{2,1,0:T(8,128)(2,1)S(1)} %bitcast.51), channel_id=1, source_target_pairs={{0,2},{1,3},{2,0},{3,1},{4,6},{5,7},{6,4},{7,5},{8,10},{9,11},{10,... | collective-permute-start | bytes 491528 | tf_op jit(solution)/shard_map/ppermute | solution.py:286
  99.4 8.2 %collective-permute-start.7 = (bf16[2,160,256]{2,1,0:T(8,128)(2,1)S(1)}, bf16[2,160,256]{2,1,0:T(8,128)(2,1)S(1)}, u32[]{:S(2)}, u32[]{:S(2)}) collective-permute-start(bf16[2,160,256]{2,1,0:T(8,128)(2,1)S(1)} %bitcast.50), channel_id=1, source_target_pairs={{0,3},{1,2},{2,1},{3,0},{4,7},{5,6},{6,5},{7,4},{8,11},{9,10},{10,... | collective-permute-start | bytes 491528 | tf_op jit(solution)/shard_map/ppermute | solution.py:286
  99.4 9.5 %collective-permute-start.23 = (bf16[2,160,256]{2,1,0:T(8,128)(2,1)S(1)}, bf16[2,160,256]{2,1,0:T(8,128)(2,1)S(1)}, u32[]{:S(2)}, u32[]{:S(2)}) collective-permute-start(bf16[2,160,256]{2,1,0:T(8,128)(2,1)S(1)} %get-tuple-element.75), channel_id=1, source_target_pairs={{0,1},{1,0},{2,3},{3,2},{4,5},{5,4},{6,7},{7,6},{8,9},{9,8},{10,11... | collective-permute-start | bytes 491528 | tf_op jit(solution)/shard_map/ppermute | solution.py:286
  101.6 10.9 %collective-permute-start.24 = (bf16[2,160,256]{2,1,0:T(8,128)(2,1)S(1)}, bf16[2,160,256]{2,1,0:T(8,128)(2,1)S(1)}, u32[]{:S(2)}, u32[]{:S(2)}) collective-permute-start(bf16[2,160,256]{2,1,0:T(8,128)(2,1)S(1)} %get-tuple-element.76), channel_id=1, source_target_pairs={{0,2},{1,3},{2,0},{3,1},{4,6},{5,7},{6,4},{7,5},{8,10},{9,11},{10,... | collective-permute-start | bytes 491528 | tf_op jit(solution)/shard_map/ppermute | solution.py:286
  103.2 11.4 %collective-permute-start.25 = (bf16[2,160,256]{2,1,0:T(8,128)(2,1)S(1)}, bf16[2,160,256]{2,1,0:T(8,128)(2,1)S(1)}, u32[]{:S(2)}, u32[]{:S(2)}) collective-permute-start(bf16[2,160,256]{2,1,0:T(8,128)(2,1)S(1)} %get-tuple-element.77), channel_id=1, source_target_pairs={{0,3},{1,2},{2,1},{3,0},{4,7},{5,6},{6,5},{7,4},{8,11},{9,10},{10,... | collective-permute-start | bytes 491528 | tf_op jit(solution)/shard_map/ppermute | solution.py:286
  105.0 9.6 %collective-permute-start.18 = (bf16[2,160,256]{2,1,0:T(8,128)(2,1)S(1)}, bf16[2,160,256]{2,1,0:T(8,128)(2,1)S(1)}, u32[]{:S(2)}, u32[]{:S(2)}) collective-permute-start(bf16[2,160,256]{2,1,0:T(8,128)(2,1)S(1)} %get-tuple-element.68), channel_id=1, source_target_pairs={{0,1},{1,0},{2,3},{3,2},{4,5},{5,4},{6,7},{7,6},{8,9},{9,8},{10,11... | collective-permute-start | bytes 491528 | tf_op jit(solution)/shard_map/ppermute | solution.py:286
  107.6 11.5 %collective-permute-start.19 = (bf16[2,160,256]{2,1,0:T(8,128)(2,1)S(1)}, bf16[2,160,256]{2,1,0:T(8,128)(2,1)S(1)}, u32[]{:S(2)}, u32[]{:S(2)}) collective-permute-start(bf16[2,160,256]{2,1,0:T(8,128)(2,1)S(1)} %get-tuple-element.69), channel_id=1, source_target_pairs={{0,2},{1,3},{2,0},{3,1},{4,6},{5,7},{6,4},{7,5},{8,10},{9,11},{10,... | collective-permute-start | bytes 491528 | tf_op jit(solution)/shard_map/ppermute | solution.py:286
  108.9 12.5 %collective-permute-start.20 = (bf16[2,160,256]{2,1,0:T(8,128)(2,1)S(1)}, bf16[2,160,256]{2,1,0:T(8,128)(2,1)S(1)}, u32[]{:S(2)}, u32[]{:S(2)}) collective-permute-start(bf16[2,160,256]{2,1,0:T(8,128)(2,1)S(1)} %get-tuple-element.70), channel_id=1, source_target_pairs={{0,3},{1,2},{2,1},{3,0},{4,7},{5,6},{6,5},{7,4},{8,11},{9,10},{10,... | collective-permute-start | bytes 491528 | tf_op jit(solution)/shard_map/ppermute | solution.py:286
  (11 other events, 54.2 us)
where the time goes:
time: 126 us; the launch traced here: 124 us
  Pallas kernels  52.4 us (42%)
  waiting for transfers between devices  35.7 us (28%)
  starting transfers between devices  28.8 us (23%)
  local copies, waits for them, and re-layouts  6.47 us (5%)
    ppermute x18, waiting for transfers between devices, swap(): return lax.ppermute(array, 'seq', pairs)  35.7 us
    pallas_call x2, Pallas kernels, body(): pl.pallas_call(lambda *refs, heads=heads: main_kernel(head_size, heads, *...  35.4 us
    ppermute x8, starting transfers between devices, level_swap(): return lax.ppermute(array, 'seq', pairs)  15.3 us
    ppermute x18, starting transfers between devices, swap(): return lax.ppermute(array, 'seq', pairs)  13.5 us
    unnamed x20, local copies, waits for them, and re-layouts  6.39 us
    pallas_call x2, Pallas kernels, finish(): pl.pallas_call(lambda *refs: finish_kernel(head_size, *refs), out_shape=[...  5.55 us
    pallas_call x2, Pallas kernels, body(): pl.pallas_call(pack_kernel, out_shape=[pair, pair], in_specs=[SMEM] + [AN...  4.52 us
    pallas_call x2, Pallas kernels, body(): pl.pallas_call(join_kernel, out_shape=[piece(2, heads)] * PLANE, in_specs...  3.12 us
  transfers between devices with their start and end apart: 26, of which 9 were waited for; matrix products, arithmetic and copies ran while one was open for 1% of the time, Pallas kernels for 39%

commit v1 on v0

--- a/solution.py
+++ b/solution.py
@@ -21,8 +21,14 @@
 VMEM = pl.BlockSpec(memory_space=pltpu.VMEM)
 
 
-def params(mib=48):
+def params(mib=60):
     return pltpu.CompilerParams(vmem_limit_bytes=mib << 20)
+
+
+def cost(microseconds):
+    return pl.CostEstimate(
+        flops=microseconds * 1_000_000_000, bytes_accessed=1_000_000, transcendentals=0
+    )
 
 
 def run_copies(copies):
@@ -32,12 +38,19 @@
         copy.wait()
 
 
-def prep_kernel(head_size, roles, *refs):
-    inputs = refs[:4]
-    outs = refs[4 : 4 + PLANE * len(CHUNKS)]
-    turned, sems = refs[4 + PLANE * len(CHUNKS) :]
-    for index, ref in enumerate(inputs):
-        turned[index] = ref[...].T
+def prep_kernel(head_size, roles, first_in, second_in, *refs):
+    count = PLANE * len(CHUNKS)
+    outs = refs[:count]
+    rows, turned, in_sems, sems = refs[count:]
+    loads = [
+        pltpu.make_async_copy(ref, rows.at[index], in_sems.at[index])
+        for index, ref in enumerate((first_in, second_in))
+    ]
+    for load in loads:
+        load.start()
+    for index, load in enumerate(loads):
+        load.wait()
+        turned[index] = rows[index].T
     place = roles[0]
     copies = []
     per_device = HEADS // PLANE
@@ -80,7 +93,7 @@
     run_copies(
         [
             pltpu.make_async_copy(
-                pieces[hop].at[pl.ds(0, 2)], plane.at[place ^ hop], sems.at[hop]
+                pieces[hop], plane.at[place ^ hop], sems.at[hop]
             )
             for hop in range(PLANE)
         ]
@@ -98,25 +111,29 @@
 
 
 def main_kernel(head_size, heads, roles, limits, *refs):
-    pieces = refs[:PLANE]
-    even_in, odd_in = refs[PLANE : PLANE + 2]
-    rest = refs[PLANE + 2 :]
+    key_pieces = refs[:PLANE]
+    query_pieces = refs[PLANE : 2 * PLANE]
+    even_in, odd_in = refs[2 * PLANE : 2 * PLANE + 2]
+    rest = refs[2 * PLANE + 2 :]
     outs = rest[:PLANE]
     local_out, even_out, odd_out = rest[PLANE : PLANE + 3]
-    chain, query, result, key_sums, sums, sems = rest[PLANE + 3 :]
+    chain, query, result, key_sums, sums = rest[PLANE + 3 : PLANE + 8]
+    scores, grads, peaks, weights, sems = (
+        rest[PLANE + 8 : PLANE + 10],
+        rest[PLANE + 10 : PLANE + 12],
+        rest[PLANE + 12 : PLANE + 14],
+        rest[PLANE + 14],
+        rest[PLANE + 15],
+    )
     place, parity = roles[0], roles[2]
     copies = []
     for hop in range(PLANE):
         unit = place ^ hop
         copies.append(
-            pltpu.make_async_copy(
-                pieces[hop].at[pl.ds(0, 2)], chain.at[FAR_UP + unit], sems.at[2 * hop]
-            )
+            pltpu.make_async_copy(key_pieces[hop], chain.at[FAR_UP + unit], sems.at[2 * hop])
         )
         copies.append(
-            pltpu.make_async_copy(
-                pieces[hop].at[pl.ds(2, 2)], query.at[unit], sems.at[2 * hop + 1]
-            )
+            pltpu.make_async_copy(query_pieces[hop], query.at[unit], sems.at[2 * hop + 1])
         )
     above = FAR_UP + PLANE
     copies.append(
@@ -138,71 +155,98 @@
     tokens = 2 * BLK
     row = lax.broadcasted_iota(jnp.int32, (BLK, tokens), 0)
     lane = lax.broadcasted_iota(jnp.int32, (1, tokens), 1)
-
-    def step(index, carry):
+    steps = heads * PLANE
+
+    def score(index, slot, k, peak):
         head, unit = index // PLANE, index % PLANE
+        tile = dot(chain[unit + k, 0, head], query[unit, 0, head], 0, 0)
+        for half in range(2):
+            place_in = 2 * k + half
+            base = unit * 2 * WINDOW * 2 + place_in
+            limit = jnp.where(lane < BLK, limits[base], limits[base + WINDOW * 2])
+            part = jnp.where(row < limit, tile[half * BLK : (half + 1) * BLK], -1e30)
+            top = jnp.max(part.reshape(BLK // 8, 8, tokens), axis=0)
+            peak = top if peak is None else jnp.maximum(peak, top)
+            scores[slot][place_in * BLK : (place_in + 1) * BLK] = part
+        return peak
+
+    def keep_peak(slot, peak):
+        peak = jnp.max(peak, axis=0, keepdims=True)
+        peaks[slot][...] = jnp.broadcast_to(peak, (8, tokens))
+
+    def grad(index, slot, k):
+        head, unit = index // PLANE, index % PLANE
+        grads[slot][k * tokens : (k + 1) * tokens] = dot(
+            chain[unit + k, 1, head], query[unit, 1, head], 0, 0
+        )
+
+    def step(index, now, later):
+        head, unit = index // PLANE, index % PLANE
+        after = jnp.minimum(index + 1, steps - 1)
         query_t = query[unit, 0, head]
-        grad_t = query[unit, 1, head]
-        scores = []
-        peak = jnp.full((1, tokens), -1e30, F32)
+        grad_wide = query[unit, 1, head].astype(F32)
+        peak = peaks[now][0:1]
+        total = out_t = later_peak = query_grad = None
         for k in range(WINDOW):
-            tile = dot(chain[unit + k, 0, head], query_t, 0, 0)
-            for half in range(2):
-                slot = 2 * k + half
-                base = unit * 2 * WINDOW * 2 + slot
-                limit = jnp.where(lane < BLK, limits[base], limits[base + WINDOW * 2])
-                part = jnp.where(row < limit, tile[half * BLK : (half + 1) * BLK], -1e30)
-                peak = jnp.maximum(peak, jnp.max(part, axis=0, keepdims=True))
-                scores.append(part)
-        total = jnp.zeros((1, tokens), F32)
-        powers = []
-        for part in scores:
-            power = jnp.exp2((part - peak) * rate)
-            total = total + jnp.sum(power, axis=0, keepdims=True)
-            powers.append(power)
-        powers = [
-            jnp.concatenate(powers[2 * k : 2 * k + 2], axis=0) for k in range(WINDOW)
-        ]
-        weights = [power.astype(BF16) for power in powers]
-        inverse = 1.0 / total
-        out_t = dot(chain[unit, 1, head], weights[0], 1, 0)
-        for k in range(1, WINDOW):
-            out_t = out_t + dot(chain[unit + k, 1, head], weights[k], 1, 0)
+            span = slice(k * tokens, (k + 1) * tokens)
+            power = jnp.exp2((scores[now][span] - peak) * rate)
+            part = jnp.sum(power.reshape(tokens // 8, 8, tokens), axis=0)
+            total = part if k == 0 else total + part
+            weight = power.astype(BF16)
+            weights[span] = weight
+            part = dot(chain[unit + k, 1, head], weight, 1, 0)
+            out_t = part if k == 0 else out_t + part
+            later_peak = score(after, later, k, later_peak)
+        keep_peak(later, later_peak)
+        inverse = 1.0 / jnp.sum(total, axis=0, keepdims=True)
         attended = (out_t * inverse).astype(BF16)
-        grad_wide = grad_t.astype(F32)
-        delta = jnp.sum(grad_wide * attended.astype(F32), axis=0, keepdims=True) * inverse
+        delta = jnp.sum(grad_wide * attended.astype(F32), axis=0, keepdims=True)
         grad_scaled = (grad_wide * inverse).astype(BF16)
-        query_grad = jnp.zeros((head_size, tokens), F32)
+        query_scaled = (query_t.astype(F32) * inverse).astype(BF16)
         for k in range(WINDOW):
-            grad_chance = dot(chain[unit + k, 1, head], grad_scaled, 0, 0)
-            grad_scores = (powers[k] * (grad_chance - delta)).astype(BF16)
-            query_grad = query_grad + dot(chain[unit + k, 0, head], grad_scores, 1, 0)
-            key_sums[unit + k, 0, head] += dot(query_t, grad_scores, 1, 1)
-            key_sums[unit + k, 1, head] += dot(grad_scaled, weights[k], 1, 1)
+            span = slice(k * tokens, (k + 1) * tokens)
+            weight = weights[span]
+            grad_scores = weight * (grads[now][span] - delta).astype(BF16)
+            part = dot(chain[unit + k, 0, head], grad_scores, 1, 0)
+            query_grad = part if k == 0 else query_grad + part
+            key_sums[unit + k, 0, head] += dot(query_scaled, grad_scores, 1, 1)
+            key_sums[unit + k, 1, head] += dot(grad_scaled, weight, 1, 1)
+            grad(after, later, k)
         result[unit, 0, head] = attended
-        result[unit, 1, head] = (query_grad * scale).astype(BF16)
+        result[unit, 1, head] = (query_grad * (inverse * scale)).astype(BF16)
+
+    first_peak = None
+    for k in range(WINDOW):
+        first_peak = score(0, 0, k, first_peak)
+        grad(0, 0, k)
+    keep_peak(0, first_peak)
+
+    def two_steps(index, carry):
+        step(2 * index, 0, 1)
+        step(2 * index + 1, 1, 0)
         return carry
 
-    lax.fori_loop(0, heads * PLANE, step, 0)
-    for unit in range(CHAIN + 1):
-        sums[unit, 0] = (key_sums[unit, 0] * scale).astype(BF16)
-        sums[unit, 1] = key_sums[unit, 1].astype(BF16)
+    lax.fori_loop(0, steps // 2, two_steps, 0)
     copies = [
         pltpu.make_async_copy(result.at[place ^ hop], outs[hop], sems.at[hop])
         for hop in range(PLANE)
     ]
-    copies.append(
-        pltpu.make_async_copy(sums.at[pl.ds(FAR_UP, PLANE)], local_out, sems.at[PLANE])
-    )
-    copies.append(
+    for copy in copies:
+        copy.start()
+    for unit in range(CHAIN + 1):
+        sums[unit, 0] = (key_sums[unit, 0] * scale).astype(BF16)
+        sums[unit, 1] = key_sums[unit, 1].astype(BF16)
+    more = [
+        pltpu.make_async_copy(sums.at[pl.ds(FAR_UP, PLANE)], local_out, sems.at[PLANE]),
         pltpu.make_async_copy(
             sums.at[pl.ds((1 - parity) * above, 2)], even_out, sems.at[PLANE + 1]
-        )
-    )
-    copies.append(
-        pltpu.make_async_copy(sums.at[pl.ds(parity * above, 2)], odd_out, sems.at[PLANE + 2])
-    )
-    run_copies(copies)
+        ),
+        pltpu.make_async_copy(sums.at[pl.ds(parity * above, 2)], odd_out, sems.at[PLANE + 2]),
+    ]
+    for copy in more:
+        copy.start()
+    for copy in copies + more:
+        copy.wait()
 
 
 def join_kernel(roles, local, even_in, odd_in, *refs):
@@ -293,20 +337,34 @@
             pairs.append((i, i + (other - z) * PLANE if 0 <= other < planes else i))
         return lax.ppermute(array, "seq", pairs)
 
-    def piece(tensors, heads):
-        return jax.ShapeDtypeStruct((tensors, heads * head_size, tokens), BF16)
-
-    pieces = pl.pallas_call(
-        lambda *refs: prep_kernel(head_size, *refs),
-        out_shape=[piece(4, heads) for heads in CHUNKS for _ in range(PLANE)],
-        in_specs=[SMEM] + [VMEM] * 4,
-        out_specs=[ANY] * (PLANE * len(CHUNKS)),
-        scratch_shapes=[
-            pltpu.VMEM((4, width, tokens), BF16),
-            pltpu.SemaphoreType.DMA((PLANE * len(CHUNKS),)),
-        ],
-        compiler_params=params(),
-    )(roles, keys, values, queries, cotangent)
+    def piece(heads):
+        return jax.ShapeDtypeStruct((2, heads * head_size, tokens), BF16)
+
+    def prep(first, second):
+        return pl.pallas_call(
+            lambda *refs: prep_kernel(head_size, *refs),
+            out_shape=[piece(heads) for heads in CHUNKS for _ in range(PLANE)],
+            in_specs=[SMEM, ANY, ANY],
+            out_specs=[ANY] * (PLANE * len(CHUNKS)),
+            scratch_shapes=[
+                pltpu.VMEM((2, tokens, width), BF16),
+                pltpu.VMEM((2, width, tokens), BF16),
+                pltpu.SemaphoreType.DMA((2,)),
+                pltpu.SemaphoreType.DMA((PLANE * len(CHUNKS),)),
+            ],
+            compiler_params=params(),
+            cost_estimate=cost(3),
+        )(roles, first, second)
+
+    def spread(parts):
+        return [
+            [parts[chunk * PLANE]]
+            + [swap(parts[chunk * PLANE + hop], hop) for hop in range(1, PLANE)]
+            for chunk in range(len(CHUNKS))
+        ]
+
+    key_held = spread(prep(keys, values))
+    query_held = spread(prep(queries, cotangent))
     limits = pl.pallas_call(
         limits_kernel,
         out_shape=jax.ShapeDtypeStruct((PLANE * 2 * WINDOW * 2,), jnp.int32),
@@ -316,9 +374,9 @@
 
     query_pieces = []
     key_pieces = []
+    halos = []
     for chunk, heads in enumerate(CHUNKS):
-        own = pieces[chunk * PLANE]
-        held = [own] + [swap(pieces[chunk * PLANE + hop], hop) for hop in range(1, PLANE)]
+        held = key_held[chunk]
         pair = jax.ShapeDtypeStruct((2, 2, heads * head_size, tokens), BF16)
         even, odd = pl.pallas_call(
             pack_kernel,
@@ -331,14 +389,17 @@
             ],
             compiler_params=params(),
         )(roles, *held)
-        even, odd = level_swap(even, 0), level_swap(odd, 1)
+        halos.append((level_swap(even, 0), level_swap(odd, 1)))
+
+    for chunk, heads in enumerate(CHUNKS):
+        even, odd = halos[chunk]
         shape = (heads, head_size, tokens)
         results = pl.pallas_call(
             lambda *refs, heads=heads: main_kernel(head_size, heads, *refs),
             out_shape=[jax.ShapeDtypeStruct((2,) + shape, BF16)] * PLANE
             + [jax.ShapeDtypeStruct((PLANE, 2) + shape, BF16)]
             + [jax.ShapeDtypeStruct((2, 2) + shape, BF16)] * 2,
-            in_specs=[SMEM, SMEM] + [ANY] * (PLANE + 2),
+            in_specs=[SMEM, SMEM] + [ANY] * (2 * PLANE + 2),
             out_specs=[ANY] * (PLANE + 3),
             scratch_shapes=[
                 pltpu.VMEM((CHAIN + 1, 2) + shape, BF16),
@@ -346,13 +407,21 @@
                 pltpu.VMEM((PLANE, 2) + shape, BF16),
                 pltpu.VMEM((CHAIN + 1, 2) + shape, F32),
                 pltpu.VMEM((CHAIN + 1, 2) + shape, BF16),
+                pltpu.VMEM((WINDOW * tokens, tokens), F32),
+                pltpu.VMEM((WINDOW * tokens, tokens), F32),
+                pltpu.VMEM((WINDOW * tokens, tokens), F32),
+                pltpu.VMEM((WINDOW * tokens, tokens), F32),
+                pltpu.VMEM((8, tokens), F32),
+                pltpu.VMEM((8, tokens), F32),
+                pltpu.VMEM((WINDOW * tokens, tokens), BF16),
                 pltpu.SemaphoreType.DMA((2 * PLANE + 2,)),
             ],
             compiler_params=params(),
+            cost_estimate=cost(6 * heads),
         )(
             roles,
             limits,
-            *[part.reshape((4,) + shape) for part in held],
+            *[part.reshape((2,) + shape) for part in key_held[chunk] + query_held[chunk]],
             even.reshape((2, 2) + shape),
             odd.reshape((2, 2) + shape),
         )
@@ -363,7 +432,7 @@
         even, odd = level_swap(even, 0), level_swap(odd, 1)
         back = pl.pallas_call(
             join_kernel,
-            out_shape=[piece(2, heads)] * PLANE,
+            out_shape=[piece(heads)] * PLANE,
             in_specs=[SMEM] + [VMEM] * 3,
             out_specs=[ANY] * PLANE,
             scratch_shapes=[

time: 126 us -> 109 us (0.87); the launches traced: 124 us -> 109 us
  waiting for transfers between devices: 35.7 us -> 19.6 us
  starting transfers between devices: 28.8 us -> 33.5 us
  Pallas kernels: 52.4 us -> 50.1 us
  local copies, waits for them, and re-layouts: 6.47 us -> 4.35 us
    ppermute x18 -> x24, waiting for transfers between devices: 35.7 us -> 19.6 us  [swap(): return lax.ppermute(array, 'seq', pairs)]
    pallas_call x2, Pallas kernels: 35.4 us -> 24.3 us  [body(): pl.pallas_call(lambda *refs, heads=heads: main_kernel(head_size, heads, *...]
    pallas_call x3 -> x4, Pallas kernels: 4.79 us -> 11.4 us  [the longest x2 6.7 us: prep(): pl.pallas_call(lambda *refs: prep_kernel(head_size, *refs), out_shape=[pi...]
    ppermute x18 -> x24, starting transfers between devices: 13.5 us -> 19.1 us  [swap(): return lax.ppermute(array, 'seq', pairs)]
    unnamed x20 -> x92, local copies, waits for them, and re-layouts: 6.39 us -> 3.67 us
  transfers between devices with their start and end apart: 26 -> 32, of which waited for: 9 -> 8; matrix products, arithmetic and copies ran while one was open for 1% -> 1% of each run, Pallas kernels for 39% -> 40%
where the time goes in v1:
time: 109 us
  Pallas kernels  50.1 us (46%)
  starting transfers between devices  33.5 us (31%)
  waiting for transfers between devices  19.6 us (18%)
  local copies, waits for them, and re-layouts  4.35 us (4%)
  between operations  1.12 us (1%)
    pallas_call x2, Pallas kernels, body(): pl.pallas_call(lambda *refs, heads=heads: main_kernel(head_size, heads, *...  24.3 us
    ppermute x24, waiting for transfers between devices, swap(): return lax.ppermute(array, 'seq', pairs)  19.6 us
    ppermute x24, starting transfers between devices, swap(): return lax.ppermute(array, 'seq', pairs)  19.1 us
    ppermute x8, starting transfers between devices, level_swap(): return lax.ppermute(array, 'seq', pairs)  14.4 us
    pallas_call x2, Pallas kernels, finish(): pl.pallas_call(lambda *refs: finish_kernel(head_size, *refs), out_shape=[...  6.8 us
    pallas_call x2, Pallas kernels, prep(): pl.pallas_call(lambda *refs: prep_kernel(head_size, *refs), out_shape=[pi...  6.7 us
    pallas_call x2, Pallas kernels, body(): pl.pallas_call(pack_kernel, out_shape=[pair, pair], in_specs=[SMEM] + [AN...  5.5 us
    pallas_call x2, Pallas kernels, body(): pl.pallas_call(join_kernel, out_shape=[piece(heads)] * PLANE, in_specs=[S...  4.71 us
  transfers between devices with their start and end apart: 32, of which 8 were waited for; matrix products, arithmetic and copies ran while one was open for 1% of the time, Pallas kernels for 40%

profile of v1, /device:TPU:0, one launch (start us, length us, event | category | flops | bytes accessed | tf_op | source)
XLA Modules:
  0.0 108.7 jit_solution(3182761949220667687)
XLA Ops:
  1.3 3.3 %shard_map.103 = (bf16[2,160,256]{2,1,0:T(8,128)(2,1)}, bf16[2,160,256]{2,1,0:T(8,128)(2,1)}, bf16[2,160,256]{2,1,0:T(8,128)(2,1)}, bf16[2,160,256]{2,1,0:T(8,12...) custom-call(s32[5]{0:T(128)} %stack.31.roles.refs_0_, ...), custom_call_target="tpu_custom_call" | custom-call | flops 3000000000 | bytes 1000000 | tf_op jit(solution)/shard_map/pallas_call | solution.py:344
  5.2 2.6 %collective-permute-start.12 = (bf16[2,160,256]{2,1,0:T(8,128)(2,1)}, bf16[2,160,256]{2,1,0:T(8,128)(2,1)S(1)}, u32[]{:S(2)}, u32[]{:S(2)}) collective-permute-start(bf16[2,160,256]{2,1,0:T(8,128)(2,1)} %get-tuple-element.66), channel_id=1, source_target_pairs={{0,2},{1,3},{2,0},{3,1},{4,6},{5,7},{6,4},{7,5},{8,10},{9,11},{10,... | collective-permute-start | bytes 491528 | tf_op jit(solution)/shard_map/ppermute | solution.py:330
  8.0 1.9 %collective-permute-start.1 = (bf16[2,160,256]{2,1,0:T(8,128)(2,1)}, bf16[2,160,256]{2,1,0:T(8,128)(2,1)S(1)}, u32[]{:S(2)}, u32[]{:S(2)}) collective-permute-start(bf16[2,160,256]{2,1,0:T(8,128)(2,1)} %get-tuple-element.52), channel_id=1, source_target_pairs={{0,2},{1,3},{2,0},{3,1},{4,6},{5,7},{6,4},{7,5},{8,10},{9,11},{10,... | collective-permute-start | bytes 491528 | tf_op jit(solution)/shard_map/ppermute | solution.py:330
  9.9 3.1 %collective-permute-done.12.refs_2_ = bf16[2,160,256]{2,1,0:T(8,128)(2,1)S(1)} collective-permute-done((bf16[2,160,256]{2,1,0:T(8,128)(2,1)}, bf16[2,160,256]{2,1,0:T(8,128)(2,1)S(1)}, u32[]{:S(2)}, u32[]{:S(2)}) %collective-permute-start.12) | collective-permute-done | bytes 163872 | tf_op jit(solution)/shard_map/ppermute | solution.py:330
  13.1 3.1 %collective-permute-done.13.refs_3_ = bf16[2,160,256]{2,1,0:T(8,128)(2,1)S(1)} collective-permute-done((bf16[2,160,256]{2,1,0:T(8,128)(2,1)}, bf16[2,160,256]{2,1,0:T(8,128)(2,1)S(1)}, u32[]{:S(2)}, u32[]{:S(2)}) %collective-permute-start.13) | collective-permute-done | bytes 163872 | tf_op jit(solution)/shard_map/ppermute | solution.py:330
  16.8 2.7 %shard_map.107 = (bf16[2,2,160,256]{3,2,1,0:T(8,128)(2,1)}, bf16[2,2,160,256]{3,2,1,0:T(8,128)(2,1)}) custom-call(s32[5]{0:T(128)} %stack.31.roles.refs_0_, bf16[2,160,256]{2,1,0:T(8,128)(2,1)} %get-tuple-element.64.refs_0_, bf16[2,160,256]{2,1,0:T(8,128)(2,1)} %copy-done.19, bf16[2,160,256]{2,1,0:T(8,128)(2,1)} %copy-done.20, bf16[2,160,256]{2,1,0:T(8,128)(2,1)} %copy-done.21), custom_call_target="tpu_custom_call" | custom-call | tf_op jit(solution)/shard_map/pallas_call | solution.py:381
  19.5 1.6 %collective-permute-start.17 = (bf16[2,2,160,256]{3,2,1,0:T(8,128)(2,1)}, bf16[2,2,160,256]{3,2,1,0:T(8,128)(2,1)S(1)}, u32[]{:S(2)}, u32[]{:S(2)}) collective-permute-start(bf16[2,2,160,256]{3,2,1,0:T(8,128)(2,1)} %get-tuple-element.72), channel_id=1, source_target_pairs={{0,4},{1,5},{2,6},{3,7},{4,0},{5,1},{6,2},{7,3},{8,12},{9,13},{10,... | collective-permute-start | bytes 983048 | tf_op jit(solution)/shard_map/ppermute | solution.py:338
  22.8 3.4 %shard_map.104 = (bf16[2,160,256]{2,1,0:T(8,128)(2,1)}, bf16[2,160,256]{2,1,0:T(8,128)(2,1)}, bf16[2,160,256]{2,1,0:T(8,128)(2,1)}, bf16[2,160,256]{2,1,0:T(8,12...) custom-call(s32[5]{0:T(128)} %stack.31.roles.refs_0_, ...), custom_call_target="tpu_custom_call" | custom-call | flops 3000000000 | bytes 1000000 | tf_op jit(solution)/shard_map/pallas_call | solution.py:344
  29.6 2.1 %shard_map.102.refs_1_ = s32[64]{0:T(128)} custom-call(s32[5]{0:T(128)} %stack.31.roles.refs_0_, s32[32,3]{1,0:T(8,128)} %copy.11.local_blocks, s32[32,4]{1,0:T(8,128)} %copy.12.far_blocks, s32[32]{0:T(128)} %counts.1), custom_call_target="tpu_custom_call" | custom-call | tf_op jit(solution)/shard_map/pallas_call | solution.py:368
  31.8 2.8 %shard_map.105 = (bf16[2,2,160,256]{3,2,1,0:T(8,128)(2,1)}, bf16[2,2,160,256]{3,2,1,0:T(8,128)(2,1)}) custom-call(s32[5]{0:T(128)} %stack.31.roles.refs_0_, bf16[2,160,256]{2,1,0:T(8,128)(2,1)} %get-tuple-element.50.refs_0_, bf16[2,160,256]{2,1,0:T(8,128)(2,1)} %copy-done.16, bf16[2,160,256]{2,1,0:T(8,128)(2,1)} %copy-done.17, bf16[2,160,256]{2,1,0:T(8,128)(2,1)} %copy-done.18), custom_call_target="tpu_custom_call" | custom-call | tf_op jit(solution)/shard_map/pallas_call | solution.py:381
  37.5 3.4 %collective-permute-start.6 = (bf16[2,2,160,256]{3,2,1,0:T(8,128)(2,1)}, bf16[2,2,160,256]{3,2,1,0:T(8,128)(2,1)S(1)}, u32[]{:S(2)}, u32[]{:S(2)}) collective-permute-start(bf16[2,2,160,256]{3,2,1,0:T(8,128)(2,1)} %get-tuple-element.58), channel_id=1, source_target_pairs={{0,4},{1,5},{2,6},{3,7},{4,0},{5,1},{6,2},{7,3},{8,12},{9,13},{10,... | collective-permute-start | bytes 983048 | tf_op jit(solution)/shard_map/ppermute | solution.py:338
  41.0 1.6 %collective-permute-start.7 = (bf16[2,2,160,256]{3,2,1,0:T(8,128)(2,1)}, bf16[2,2,160,256]{3,2,1,0:T(8,128)(2,1)S(1)}, u32[]{:S(2)}, u32[]{:S(2)}) collective-permute-start(bf16[2,2,160,256]{3,2,1,0:T(8,128)(2,1)} %get-tuple-element.59), channel_id=1, source_target_pairs={{0,0},{1,1},{2,2},{3,3},{4,8},{5,9},{6,10},{7,11},{8,4},{9,5},{10,... | collective-permute-start | bytes 983048 | tf_op jit(solution)/shard_map/ppermute | solution.py:338
  42.6 12.1 %shard_map.108 = (bf16[2,2,80,256]{3,2,1,0:T(8,128)(2,1)}, bf16[2,2,80,256]{3,2,1,0:T(8,128)(2,1)}, bf16[2,2,80,256]{3,2,1,0:T(8,128)(2,1)}, bf16[2,2,80,256]{3,...) custom-call(s32[5]{0:T(128)} %stack.31.roles.refs_0_, ...), custom_call_target="tpu_custom_call" | custom-call | flops 12000000000 | bytes 1000000 | tf_op jit(solution)/shard_map/pallas_call | solution.py:397
  57.8 12.2 %shard_map.106 = (bf16[2,2,80,256]{3,2,1,0:T(8,128)(2,1)}, bf16[2,2,80,256]{3,2,1,0:T(8,128)(2,1)}, bf16[2,2,80,256]{3,2,1,0:T(8,128)(2,1)}, bf16[2,2,80,256]{3,...) custom-call(s32[5]{0:T(128)} %stack.31.roles.refs_0_, ...), custom_call_target="tpu_custom_call" | custom-call | flops 12000000000 | bytes 1000000 | tf_op jit(solution)/shard_map/pallas_call | solution.py:397
  70.0 2.3 %collective-permute-start.22 = (bf16[2,2,2,80,256]{4,3,2,1,0:T(8,128)(2,1)}, bf16[2,2,2,80,256]{4,3,2,1,0:T(8,128)(2,1)S(1)}, u32[]{:S(2)}, u32[]{:S(2)}) collective-permute-start(bf16[2,2,2,80,256]{4,3,2,1,0:T(8,128)(2,1)} %get-tuple-element.81), channel_id=1, source_target_pairs={{0,4},{1,5},{2,6},{3,7},{4,0},{5,1},{6,2},{7,3},{8,12},{9,13},{10,... | collective-permute-start | bytes 983048 | tf_op jit(solution)/shard_map/ppermute | solution.py:338
  76.0 2.4 %shard_map.111 = (bf16[2,160,256]{2,1,0:T(8,128)(2,1)}, bf16[2,160,256]{2,1,0:T(8,128)(2,1)}, bf16[2,160,256]{2,1,0:T(8,128)(2,1)}, bf16[2,160,256]{2,1,0:T(8,128)(2,1)}) custom-call(s32[5]{0:T(128)} %stack.31.roles.refs_0_, bf16[4,2,160,256]{3,2,1,0:T(8,128)(2,1)} %bitcast.39, bf16[2,2,160,256]{3,2,1,0:T(8,128)(2,1)} %bitcast.41, ...), custom_call_target="tpu_custom_call" | custom-call | tf_op jit(solution)/shard_map/pallas_call | solution.py:433
  78.7 2.3 %collective-permute-done.20.refs_7_ = bf16[2,160,256]{2,1,0:T(8,128)(2,1)S(1)} collective-permute-done((bf16[2,160,256]{2,1,0:T(8,128)(2,1)S(1)}, bf16[2,160,256]{2,1,0:T(8,128)(2,1)S(1)}, u32[]{:S(2)}, u32[]{:S(2)}) %collective-permute-start.20) | collective-permute-done | bytes 163872 | tf_op jit(solution)/shard_map/ppermute | solution.py:330
  83.3 2.3 %shard_map.110 = (bf16[2,160,256]{2,1,0:T(8,128)(2,1)}, bf16[2,160,256]{2,1,0:T(8,128)(2,1)}, bf16[2,160,256]{2,1,0:T(8,128)(2,1)}, bf16[2,160,256]{2,1,0:T(8,128)(2,1)}) custom-call(s32[5]{0:T(128)} %stack.31.roles.refs_0_, bf16[4,2,160,256]{3,2,1,0:T(8,128)(2,1)} %bitcast.40, bf16[2,2,160,256]{3,2,1,0:T(8,128)(2,1)} %bitcast.42, ...), custom_call_target="tpu_custom_call" | custom-call | tf_op jit(solution)/shard_map/pallas_call | solution.py:433
  88.2 2.4 %collective-permute-done.10.refs_4_ = bf16[2,160,256]{2,1,0:T(8,128)(2,1)S(1)} collective-permute-done((bf16[2,160,256]{2,1,0:T(8,128)(2,1)S(1)}, bf16[2,160,256]{2,1,0:T(8,128)(2,1)S(1)}, u32[]{:S(2)}, u32[]{:S(2)}) %collective-permute-start.10) | collective-permute-done | bytes 163872 | tf_op jit(solution)/shard_map/ppermute | solution.py:330
  91.2 1.6 %collective-permute-start.26 = (bf16[2,160,256]{2,1,0:T(8,128)(2,1)}, bf16[2,160,256]{2,1,0:T(8,128)(2,1)S(1)}, u32[]{:S(2)}, u32[]{:S(2)}) collective-permute-start(bf16[2,160,256]{2,1,0:T(8,128)(2,1)} %get-tuple-element.86), channel_id=1, source_target_pairs={{0,3},{1,2},{2,1},{3,0},{4,7},{5,6},{6,5},{7,4},{8,11},{9,10},{10,... | collective-permute-start | bytes 491528 | tf_op jit(solution)/shard_map/ppermute | solution.py:330
  92.9 3.4 %shard_map.109 = (bf16[256,1280]{1,0:T(8,128)(2,1)}, bf16[256,1280]{1,0:T(8,128)(2,1)}) custom-call(s32[5]{0:T(128)} %stack.31.roles.refs_0_, bf16[2,160,256]{2,1,0:T(8,128)(2,1)} %bitcast.46, bf16[2,160,256]{2,1,0:T(8,128)(2,1)} %copy-done.8, bf16[2,160,256]{2,1,0:T(8,128)(2,1)} %copy-done.9, bf16[2,160,256]{2,1,0:T(8,128)(2,1)} %copy-done.11, ...), custom_call_target="tpu_custom_call" | custom-call | tf_op jit(solution)/shard_map/pallas_call | solution.py:447
  97.7 4.6 %collective-permute-done.25.refs_3_ = bf16[2,160,256]{2,1,0:T(8,128)(2,1)S(1)} collective-permute-done((bf16[2,160,256]{2,1,0:T(8,128)(2,1)}, bf16[2,160,256]{2,1,0:T(8,128)(2,1)S(1)}, u32[]{:S(2)}, u32[]{:S(2)}) %collective-permute-start.25) | collective-permute-done | bytes 163872 | tf_op jit(solution)/shard_map/ppermute | solution.py:330
  102.2 2.5 %collective-permute-done.26.refs_4_ = bf16[2,160,256]{2,1,0:T(8,128)(2,1)S(1)} collective-permute-done((bf16[2,160,256]{2,1,0:T(8,128)(2,1)}, bf16[2,160,256]{2,1,0:T(8,128)(2,1)S(1)}, u32[]{:S(2)}, u32[]{:S(2)}) %collective-permute-start.26) | collective-permute-done | bytes 163872 | tf_op jit(solution)/shard_map/ppermute | solution.py:330
  105.3 3.4 %shard_map.112 = (bf16[256,1280]{1,0:T(8,128)(2,1)}, bf16[256,1280]{1,0:T(8,128)(2,1)}) custom-call(s32[5]{0:T(128)} %stack.31.roles.refs_0_, bf16[2,160,256]{2,1,0:T(8,128)(2,1)} %get-tuple-element.83.refs_1_, bf16[2,160,256]{2,1,0:T(8,128)(2,1)} %copy-done.13, bf16[2,160,256]{2,1,0:T(8,128)(2,1)} %copy-done.14, bf16[2,160,256]{2,1,0:T(8,128)(2,1)} %copy-done.15, ...), custom_call_target="tpu_custom_call" | custom-call | tf_op jit(solution)/shard_map/pallas_call | solution.py:447
  (144 shorter events, 24.3 us)
Async XLA Ops:
  7.9 18.3 %collective-permute-start = (bf16[2,160,256]{2,1,0:T(8,128)(2,1)}, bf16[2,160,256]{2,1,0:T(8,128)(2,1)S(1)}, u32[]{:S(2)}, u32[]{:S(2)}) collective-permute-start(bf16[2,160,256]{2,1,0:T(8,128)(2,1)} %get-tuple-element.51), channel_id=1, source_target_pairs={{0,1},{1,0},{2,3},{3,2},{4,5},{5,4},{6,7},{7,6},{8,9},{9,8},{10,11... | collective-permute-start | bytes 491528 | tf_op jit(solution)/shard_map/ppermute | solution.py:330
  8.0 18.6 %collective-permute-start.1 = (bf16[2,160,256]{2,1,0:T(8,128)(2,1)}, bf16[2,160,256]{2,1,0:T(8,128)(2,1)S(1)}, u32[]{:S(2)}, u32[]{:S(2)}) collective-permute-start(bf16[2,160,256]{2,1,0:T(8,128)(2,1)} %get-tuple-element.52), channel_id=1, source_target_pairs={{0,2},{1,3},{2,0},{3,1},{4,6},{5,7},{6,4},{7,5},{8,10},{9,11},{10,... | collective-permute-start | bytes 491528 | tf_op jit(solution)/shard_map/ppermute | solution.py:330
  9.9 18.2 %collective-permute-start.2 = (bf16[2,160,256]{2,1,0:T(8,128)(2,1)}, bf16[2,160,256]{2,1,0:T(8,128)(2,1)S(1)}, u32[]{:S(2)}, u32[]{:S(2)}) collective-permute-start(bf16[2,160,256]{2,1,0:T(8,128)(2,1)} %get-tuple-element.53), channel_id=1, source_target_pairs={{0,3},{1,2},{2,1},{3,0},{4,7},{5,6},{6,5},{7,4},{8,11},{9,10},{10,... | collective-permute-start | bytes 491528 | tf_op jit(solution)/shard_map/ppermute | solution.py:330
  19.5 18.0 %collective-permute-start.17 = (bf16[2,2,160,256]{3,2,1,0:T(8,128)(2,1)}, bf16[2,2,160,256]{3,2,1,0:T(8,128)(2,1)S(1)}, u32[]{:S(2)}, u32[]{:S(2)}) collective-permute-start(bf16[2,2,160,256]{3,2,1,0:T(8,128)(2,1)} %get-tuple-element.72), channel_id=1, source_target_pairs={{0,4},{1,5},{2,6},{3,7},{4,0},{5,1},{6,2},{7,3},{8,12},{9,13},{10,... | collective-permute-start | bytes 983048 | tf_op jit(solution)/shard_map/ppermute | solution.py:338
  21.1 19.8 %collective-permute-start.18 = (bf16[2,2,160,256]{3,2,1,0:T(8,128)(2,1)}, bf16[2,2,160,256]{3,2,1,0:T(8,128)(2,1)S(1)}, u32[]{:S(2)}, u32[]{:S(2)}) collective-permute-start(bf16[2,2,160,256]{3,2,1,0:T(8,128)(2,1)} %get-tuple-element.73), channel_id=1, source_target_pairs={{0,0},{1,1},{2,2},{3,3},{4,8},{5,9},{6,10},{7,11},{8,4},{9,5},{10,... | collective-permute-start | bytes 983048 | tf_op jit(solution)/shard_map/ppermute | solution.py:338
  26.6 8.7 %collective-permute-start.15 = (bf16[2,160,256]{2,1,0:T(8,128)(2,1)}, bf16[2,160,256]{2,1,0:T(8,128)(2,1)S(1)}, u32[]{:S(2)}, u32[]{:S(2)}) collective-permute-start(bf16[2,160,256]{2,1,0:T(8,128)(2,1)} %get-tuple-element.70), channel_id=1, source_target_pairs={{0,2},{1,3},{2,0},{3,1},{4,6},{5,7},{6,4},{7,5},{8,10},{9,11},{10,... | collective-permute-start | bytes 491528 | tf_op jit(solution)/shard_map/ppermute | solution.py:330
  28.2 8.7 %collective-permute-start.16 = (bf16[2,160,256]{2,1,0:T(8,128)(2,1)}, bf16[2,160,256]{2,1,0:T(8,128)(2,1)S(1)}, u32[]{:S(2)}, u32[]{:S(2)}) collective-permute-start(bf16[2,160,256]{2,1,0:T(8,128)(2,1)} %get-tuple-element.71), channel_id=1, source_target_pairs={{0,3},{1,2},{2,1},{3,0},{4,7},{5,6},{6,5},{7,4},{8,11},{9,10},{10,... | collective-permute-start | bytes 491528 | tf_op jit(solution)/shard_map/ppermute | solution.py:330
  34.6 20.1 %collective-permute-start.3 = (bf16[2,160,256]{2,1,0:T(8,128)(2,1)S(1)}, bf16[2,160,256]{2,1,0:T(8,128)(2,1)S(1)}, u32[]{:S(2)}, u32[]{:S(2)}) collective-permute-start(bf16[2,160,256]{2,1,0:T(8,128)(2,1)S(1)} %copy-done.38), channel_id=1, source_target_pairs={{0,1},{1,0},{2,3},{3,2},{4,5},{5,4},{6,7},{7,6},{8,9},{9,8},{10,11... | collective-permute-start | bytes 491528 | tf_op jit(solution)/shard_map/ppermute | solution.py:330
  35.3 20.0 %collective-permute-start.4 = (bf16[2,160,256]{2,1,0:T(8,128)(2,1)S(1)}, bf16[2,160,256]{2,1,0:T(8,128)(2,1)S(1)}, u32[]{:S(2)}, u32[]{:S(2)}) collective-permute-start(bf16[2,160,256]{2,1,0:T(8,128)(2,1)S(1)} %copy-done.33), channel_id=1, source_target_pairs={{0,2},{1,3},{2,0},{3,1},{4,6},{5,7},{6,4},{7,5},{8,10},{9,11},{10,... | collective-permute-start | bytes 491528 | tf_op jit(solution)/shard_map/ppermute | solution.py:330
  36.9 20.0 %collective-permute-start.5 = (bf16[2,160,256]{2,1,0:T(8,128)(2,1)S(1)}, bf16[2,160,256]{2,1,0:T(8,128)(2,1)S(1)}, u32[]{:S(2)}, u32[]{:S(2)}) collective-permute-start(bf16[2,160,256]{2,1,0:T(8,128)(2,1)S(1)} %copy-done.30), channel_id=1, source_target_pairs={{0,3},{1,2},{2,1},{3,0},{4,7},{5,6},{6,5},{7,4},{8,11},{9,10},{10,... | collective-permute-start | bytes 491528 | tf_op jit(solution)/shard_map/ppermute | solution.py:330
  37.5 19.4 %collective-permute-start.6 = (bf16[2,2,160,256]{3,2,1,0:T(8,128)(2,1)}, bf16[2,2,160,256]{3,2,1,0:T(8,128)(2,1)S(1)}, u32[]{:S(2)}, u32[]{:S(2)}) collective-permute-start(bf16[2,2,160,256]{3,2,1,0:T(8,128)(2,1)} %get-tuple-element.58), channel_id=1, source_target_pairs={{0,4},{1,5},{2,6},{3,7},{4,0},{5,1},{6,2},{7,3},{8,12},{9,13},{10,... | collective-permute-start | bytes 983048 | tf_op jit(solution)/shard_map/ppermute | solution.py:338
  41.0 15.9 %collective-permute-start.7 = (bf16[2,2,160,256]{3,2,1,0:T(8,128)(2,1)}, bf16[2,2,160,256]{3,2,1,0:T(8,128)(2,1)S(1)}, u32[]{:S(2)}, u32[]{:S(2)}) collective-permute-start(bf16[2,2,160,256]{3,2,1,0:T(8,128)(2,1)} %get-tuple-element.59), channel_id=1, source_target_pairs={{0,0},{1,1},{2,2},{3,3},{4,8},{5,9},{6,10},{7,11},{8,4},{9,5},{10,... | collective-permute-start | bytes 983048 | tf_op jit(solution)/shard_map/ppermute | solution.py:338
  54.7 19.2 %collective-permute-start.27 = (bf16[2,2,2,80,256]{4,3,2,1,0:T(8,128)(2,1)}, bf16[2,2,2,80,256]{4,3,2,1,0:T(8,128)(2,1)S(1)}, u32[]{:S(2)}, u32[]{:S(2)}) collective-permute-start(bf16[2,2,2,80,256]{4,3,2,1,0:T(8,128)(2,1)} %get-tuple-element.88), channel_id=1, source_target_pairs={{0,4},{1,5},{2,6},{3,7},{4,0},{5,1},{6,2},{7,3},{8,12},{9,13},{10,... | collective-permute-start | bytes 983048 | tf_op jit(solution)/shard_map/ppermute | solution.py:338
  55.3 19.3 %collective-permute-start.28 = (bf16[2,2,2,80,256]{4,3,2,1,0:T(8,128)(2,1)}, bf16[2,2,2,80,256]{4,3,2,1,0:T(8,128)(2,1)S(1)}, u32[]{:S(2)}, u32[]{:S(2)}) collective-permute-start(bf16[2,2,2,80,256]{4,3,2,1,0:T(8,128)(2,1)} %get-tuple-element.89), channel_id=1, source_target_pairs={{0,0},{1,1},{2,2},{3,3},{4,8},{5,9},{6,10},{7,11},{8,4},{9,5},{10,... | collective-permute-start | bytes 983048 | tf_op jit(solution)/shard_map/ppermute | solution.py:338
  70.0 11.6 %collective-permute-start.22 = (bf16[2,2,2,80,256]{4,3,2,1,0:T(8,128)(2,1)}, bf16[2,2,2,80,256]{4,3,2,1,0:T(8,128)(2,1)S(1)}, u32[]{:S(2)}, u32[]{:S(2)}) collective-permute-start(bf16[2,2,2,80,256]{4,3,2,1,0:T(8,128)(2,1)} %get-tuple-element.81), channel_id=1, source_target_pairs={{0,4},{1,5},{2,6},{3,7},{4,0},{5,1},{6,2},{7,3},{8,12},{9,13},{10,... | collective-permute-start | bytes 983048 | tf_op jit(solution)/shard_map/ppermute | solution.py:338
  72.3 9.4 %collective-permute-start.23 = (bf16[2,2,2,80,256]{4,3,2,1,0:T(8,128)(2,1)}, bf16[2,2,2,80,256]{4,3,2,1,0:T(8,128)(2,1)S(1)}, u32[]{:S(2)}, u32[]{:S(2)}) collective-permute-start(bf16[2,2,2,80,256]{4,3,2,1,0:T(8,128)(2,1)} %get-tuple-element.82), channel_id=1, source_target_pairs={{0,0},{1,1},{2,2},{3,3},{4,8},{5,9},{6,10},{7,11},{8,4},{9,5},{10,... | collective-permute-start | bytes 983048 | tf_op jit(solution)/shard_map/ppermute | solution.py:338
  74.6 11.0 %collective-permute-start.21 = (bf16[2,160,256]{2,1,0:T(8,128)(2,1)S(1)}, bf16[2,160,256]{2,1,0:T(8,128)(2,1)S(1)}, u32[]{:S(2)}, u32[]{:S(2)}) collective-permute-start(bf16[2,160,256]{2,1,0:T(8,128)(2,1)S(1)} %bitcast.59), channel_id=1, source_target_pairs={{0,3},{1,2},{2,1},{3,0},{4,7},{5,6},{6,5},{7,4},{8,11},{9,10},{10,... | collective-permute-start | bytes 491528 | tf_op jit(solution)/shard_map/ppermute | solution.py:330
  81.6 9.0 %collective-permute-start.10 = (bf16[2,160,256]{2,1,0:T(8,128)(2,1)S(1)}, bf16[2,160,256]{2,1,0:T(8,128)(2,1)S(1)}, u32[]{:S(2)}, u32[]{:S(2)}) collective-permute-start(bf16[2,160,256]{2,1,0:T(8,128)(2,1)S(1)} %bitcast.60), channel_id=1, source_target_pairs={{0,3},{1,2},{2,1},{3,0},{4,7},{5,6},{6,5},{7,4},{8,11},{9,10},{10,... | collective-permute-start | bytes 491528 | tf_op jit(solution)/shard_map/ppermute | solution.py:330
  81.8 9.5 %collective-permute-start.29 = (bf16[2,160,256]{2,1,0:T(8,128)(2,1)}, bf16[2,160,256]{2,1,0:T(8,128)(2,1)S(1)}, u32[]{:S(2)}, u32[]{:S(2)}) collective-permute-start(bf16[2,160,256]{2,1,0:T(8,128)(2,1)} %get-tuple-element.91), channel_id=1, source_target_pairs={{0,1},{1,0},{2,3},{3,2},{4,5},{5,4},{6,7},{7,6},{8,9},{9,8},{10,11... | collective-permute-start | bytes 491528 | tf_op jit(solution)/shard_map/ppermute | solution.py:330
  85.7 10.6 %collective-permute-start.30 = (bf16[2,160,256]{2,1,0:T(8,128)(2,1)S(1)}, bf16[2,160,256]{2,1,0:T(8,128)(2,1)S(1)}, u32[]{:S(2)}, u32[]{:S(2)}) collective-permute-start(bf16[2,160,256]{2,1,0:T(8,128)(2,1)S(1)} %copy-done.36), channel_id=1, source_target_pairs={{0,2},{1,3},{2,0},{3,1},{4,6},{5,7},{6,4},{7,5},{8,10},{9,11},{10,... | collective-permute-start | bytes 491528 | tf_op jit(solution)/shard_map/ppermute | solution.py:330
  86.4 11.3 %collective-permute-start.31 = (bf16[2,160,256]{2,1,0:T(8,128)(2,1)S(1)}, bf16[2,160,256]{2,1,0:T(8,128)(2,1)S(1)}, u32[]{:S(2)}, u32[]{:S(2)}) collective-permute-start(bf16[2,160,256]{2,1,0:T(8,128)(2,1)S(1)} %copy-done.34), channel_id=1, source_target_pairs={{0,3},{1,2},{2,1},{3,0},{4,7},{5,6},{6,5},{7,4},{8,11},{9,10},{10,... | collective-permute-start | bytes 491528 | tf_op jit(solution)/shard_map/ppermute | solution.py:330
  88.2 9.5 %collective-permute-start.24 = (bf16[2,160,256]{2,1,0:T(8,128)(2,1)}, bf16[2,160,256]{2,1,0:T(8,128)(2,1)S(1)}, u32[]{:S(2)}, u32[]{:S(2)}) collective-permute-start(bf16[2,160,256]{2,1,0:T(8,128)(2,1)} %get-tuple-element.84), channel_id=1, source_target_pairs={{0,1},{1,0},{2,3},{3,2},{4,5},{5,4},{6,7},{7,6},{8,9},{9,8},{10,11... | collective-permute-start | bytes 491528 | tf_op jit(solution)/shard_map/ppermute | solution.py:330
  90.6 11.6 %collective-permute-start.25 = (bf16[2,160,256]{2,1,0:T(8,128)(2,1)}, bf16[2,160,256]{2,1,0:T(8,128)(2,1)S(1)}, u32[]{:S(2)}, u32[]{:S(2)}) collective-permute-start(bf16[2,160,256]{2,1,0:T(8,128)(2,1)} %get-tuple-element.85), channel_id=1, source_target_pairs={{0,2},{1,3},{2,0},{3,1},{4,6},{5,7},{6,4},{7,5},{8,10},{9,11},{10,... | collective-permute-start | bytes 491528 | tf_op jit(solution)/shard_map/ppermute | solution.py:330
  91.2 13.4 %collective-permute-start.26 = (bf16[2,160,256]{2,1,0:T(8,128)(2,1)}, bf16[2,160,256]{2,1,0:T(8,128)(2,1)S(1)}, u32[]{:S(2)}, u32[]{:S(2)}) collective-permute-start(bf16[2,160,256]{2,1,0:T(8,128)(2,1)} %get-tuple-element.86), channel_id=1, source_target_pairs={{0,3},{1,2},{2,1},{3,0},{4,7},{5,6},{6,5},{7,4},{8,11},{9,10},{10,... | collective-permute-start | bytes 491528 | tf_op jit(solution)/shard_map/ppermute | solution.py:330
  (53 other events, 266.3 us)

commit v2 on v1

--- a/solution.py
+++ b/solution.py
@@ -23,6 +23,10 @@
 
 def params(mib=60):
     return pltpu.CompilerParams(vmem_limit_bytes=mib << 20)
+
+
+def after(arrays, others):
+    return list(lax.optimization_barrier((list(arrays), list(others)))[0])
 
 
 def cost(microseconds):
@@ -92,9 +96,7 @@
     place, parity = roles[0], roles[2]
     run_copies(
         [
-            pltpu.make_async_copy(
-                pieces[hop], plane.at[place ^ hop], sems.at[hop]
-            )
+            pltpu.make_async_copy(pieces[hop], plane.at[place ^ hop], sems.at[hop])
             for hop in range(PLANE)
         ]
     )
@@ -334,7 +336,7 @@
         for i in range(size):
             z = i // PLANE
             other = z + 1 if z % 2 == odd else z - 1
-            pairs.append((i, i + (other - z) * PLANE if 0 <= other < planes else i))
+            pairs.append((i, i + (other - z) * PLANE if 0 <= other < planes else i ^ 1))
         return lax.ppermute(array, "seq", pairs)
 
     def piece(heads):
@@ -364,7 +366,6 @@
         ]
 
     key_held = spread(prep(keys, values))
-    query_held = spread(prep(queries, cotangent))
     limits = pl.pallas_call(
         limits_kernel,
         out_shape=jax.ShapeDtypeStruct((PLANE * 2 * WINDOW * 2,), jnp.int32),
@@ -375,8 +376,11 @@
     query_pieces = []
     key_pieces = []
     halos = []
+    query_ready = prep(queries, cotangent)
+    query_held = spread(query_ready)
     for chunk, heads in enumerate(CHUNKS):
         held = key_held[chunk]
+        held = after(held, query_held[0][1:] if chunk else query_ready)
         pair = jax.ShapeDtypeStruct((2, 2, heads * head_size, tokens), BF16)
         even, odd = pl.pallas_call(
             pack_kernel,
@@ -388,14 +392,16 @@
                 pltpu.SemaphoreType.DMA((PLANE,)),
             ],
             compiler_params=params(),
+            cost_estimate=cost(2),
         )(roles, *held)
         halos.append((level_swap(even, 0), level_swap(odd, 1)))
 
-    for chunk, heads in enumerate(CHUNKS):
+    def main(chunk):
+        heads = CHUNKS[chunk]
         even, odd = halos[chunk]
         shape = (heads, head_size, tokens)
-        results = pl.pallas_call(
-            lambda *refs, heads=heads: main_kernel(head_size, heads, *refs),
+        return pl.pallas_call(
+            lambda *refs: main_kernel(head_size, heads, *refs),
             out_shape=[jax.ShapeDtypeStruct((2,) + shape, BF16)] * PLANE
             + [jax.ShapeDtypeStruct((PLANE, 2) + shape, BF16)]
             + [jax.ShapeDtypeStruct((2, 2) + shape, BF16)] * 2,
@@ -425,12 +431,11 @@
             even.reshape((2, 2) + shape),
             odd.reshape((2, 2) + shape),
         )
+
+    def join(chunk, local, even, odd):
+        heads = CHUNKS[chunk]
         flat = (2, heads * head_size, tokens)
-        out = [part.reshape(flat) for part in results[:PLANE]]
-        query_pieces += [out[0]] + [swap(out[hop], hop) for hop in range(1, PLANE)]
-        local, even, odd = results[PLANE:]
-        even, odd = level_swap(even, 0), level_swap(odd, 1)
-        back = pl.pallas_call(
+        return pl.pallas_call(
             join_kernel,
             out_shape=[piece(heads)] * PLANE,
             in_specs=[SMEM] + [VMEM] * 3,
@@ -441,7 +446,27 @@
             ],
             compiler_params=params(),
         )(roles, local.reshape((PLANE,) + flat), even.reshape((2,) + flat), odd.reshape((2,) + flat))
-        key_pieces += [back[0]] + [swap(back[hop], hop) for hop in range(1, PLANE)]
+
+    def spread_one(parts):
+        return [parts[0]] + [swap(parts[hop], hop) for hop in range(1, PLANE)]
+
+    rounds = len(CHUNKS)
+    results = [main(chunk) for chunk in range(rounds)]
+    backs = []
+    last = None
+    for chunk in range(rounds):
+        shape = (2, CHUNKS[chunk] * head_size, tokens)
+        out = [part.reshape(shape) for part in results[chunk][:PLANE]]
+        if last is not None:
+            out = after(out, last[1:])
+        last = spread_one(out)
+        query_pieces += last
+    for chunk in range(rounds):
+        local, even, odd = results[chunk][PLANE:]
+        back = join(chunk, local, level_swap(even, 0), level_swap(odd, 1))
+        back = after(back, [last[2]])
+        last = spread_one(back)
+        key_pieces += last
 
     def finish(parts):
         return pl.pallas_call(

time: 109 us -> 97.9 us (0.90)
  starting transfers between devices: 33.5 us -> 26.1 us
  waiting for transfers between devices: 19.6 us -> 14.2 us
    ppermute x8, starting transfers between devices: 14.4 us -> 7 us  [level_swap(): return lax.ppermute(array, 'seq', pairs)]
    ppermute x24, waiting for transfers between devices: 19.6 us -> 14 us  [swap(): return lax.ppermute(array, 'seq', pairs)]
    unnamed x92 -> x86, local copies, waits for them, and re-layouts: 3.67 us -> 4.54 us
  transfers between devices with their start and end apart: 32 -> 32, of which waited for: 8 -> 9; matrix products, arithmetic and copies ran while one was open for 1% -> 1% of each run, Pallas kernels for 40% -> 45%
where the time goes in v2:
time: 97.9 us; the launch traced here: 96.6 us
  Pallas kernels  49.9 us (51%)
  starting transfers between devices  26.1 us (27%)
  waiting for transfers between devices  14.2 us (15%)
  local copies, waits for them, and re-layouts  5.17 us (5%)
  between operations  1.14 us (1%)
    pallas_call x2, Pallas kernels, main(): pl.pallas_call(lambda *refs: main_kernel(head_size, heads, *refs), out_sh...  24.2 us
    ppermute x24, starting transfers between devices, swap(): return lax.ppermute(array, 'seq', pairs)  19.1 us
    ppermute x24, waiting for transfers between devices, swap(): return lax.ppermute(array, 'seq', pairs)  14 us
    ppermute x8, starting transfers between devices, level_swap(): return lax.ppermute(array, 'seq', pairs)  7 us
    pallas_call x2, Pallas kernels, prep(): pl.pallas_call(lambda *refs: prep_kernel(head_size, *refs), out_shape=[pi...  6.8 us
    pallas_call x2, Pallas kernels, finish(): pl.pallas_call(lambda *refs: finish_kernel(head_size, *refs), out_shape=[...  6.8 us
    pallas_call x2, Pallas kernels, body(): pl.pallas_call(pack_kernel, out_shape=[pair, pair], in_specs=[SMEM] + [AN...  5.38 us
    pallas_call x2, Pallas kernels, join(): pl.pallas_call(join_kernel, out_shape=[piece(heads)] * PLANE, in_specs=[S...  4.6 us
  transfers between devices with their start and end apart: 32, of which 9 were waited for; matrix products, arithmetic and copies ran while one was open for 1% of the time, Pallas kernels for 45%

profile of v2, /device:TPU:0, one launch (start us, length us, event | category | flops | bytes accessed | tf_op | source)
XLA Modules:
  0.0 96.6 jit_solution(12565181326653255865)
XLA Ops:
  1.3 3.3 %shard_map.103 = (bf16[2,160,256]{2,1,0:T(8,128)(2,1)}, bf16[2,160,256]{2,1,0:T(8,128)(2,1)}, bf16[2,160,256]{2,1,0:T(8,128)(2,1)}, bf16[2,160,256]{2,1,0:T(8,12...) custom-call(s32[5]{0:T(128)} %stack.31.roles.refs_0_, ...), custom_call_target="tpu_custom_call" | custom-call | flops 3000000000 | bytes 1000000 | tf_op jit(solution)/shard_map/pallas_call | solution.py:346
  5.1 2.6 %collective-permute-start.1 = (bf16[2,160,256]{2,1,0:T(8,128)(2,1)}, bf16[2,160,256]{2,1,0:T(8,128)(2,1)S(1)}, u32[]{:S(2)}, u32[]{:S(2)}) collective-permute-start(bf16[2,160,256]{2,1,0:T(8,128)(2,1)} %get-tuple-element.72), channel_id=1, source_target_pairs={{0,2},{1,3},{2,0},{3,1},{4,6},{5,7},{6,4},{7,5},{8,10},{9,11},{10,... | collective-permute-start | bytes 491528 | tf_op jit(solution)/shard_map/ppermute | solution.py:332
  7.9 3.5 %shard_map.104 = (bf16[2,160,256]{2,1,0:T(8,128)(2,1)}, bf16[2,160,256]{2,1,0:T(8,128)(2,1)}, bf16[2,160,256]{2,1,0:T(8,128)(2,1)}, bf16[2,160,256]{2,1,0:T(8,12...) custom-call(s32[5]{0:T(128)} %stack.31.roles.refs_0_, ...), custom_call_target="tpu_custom_call" | custom-call | flops 3000000000 | bytes 1000000 | tf_op jit(solution)/shard_map/pallas_call | solution.py:346
  11.5 1.8 %collective-permute-start.4 = (bf16[2,160,256]{2,1,0:T(8,128)(2,1)}, bf16[2,160,256]{2,1,0:T(8,128)(2,1)S(1)}, u32[]{:S(2)}, u32[]{:S(2)}) collective-permute-start(bf16[2,160,256]{2,1,0:T(8,128)(2,1)} %get-tuple-element.76), channel_id=1, source_target_pairs={{0,2},{1,3},{2,0},{3,1},{4,6},{5,7},{6,4},{7,5},{8,10},{9,11},{10,... | collective-permute-start | bytes 491528 | tf_op jit(solution)/shard_map/ppermute | solution.py:332
  13.7 2.3 %collective-permute-done.2.refs_3_ = bf16[2,160,256]{2,1,0:T(8,128)(2,1)S(1)} collective-permute-done((bf16[2,160,256]{2,1,0:T(8,128)(2,1)}, bf16[2,160,256]{2,1,0:T(8,128)(2,1)S(1)}, u32[]{:S(2)}, u32[]{:S(2)}) %collective-permute-start.2) | collective-permute-done | bytes 163872 | tf_op jit(solution)/shard_map/ppermute | solution.py:332
  18.0 2.7 %shard_map.105 = (bf16[2,2,160,256]{3,2,1,0:T(8,128)(2,1)}, bf16[2,2,160,256]{3,2,1,0:T(8,128)(2,1)}) custom-call(s32[5]{0:T(128)} %stack.31.roles.refs_0_, bf16[2,160,256]{2,1,0:T(8,128)(2,1)} %get-tuple-element.82.refs_0_, bf16[2,160,256]{2,1,0:T(8,128)(2,1)} %copy-done.27, bf16[2,160,256]{2,1,0:T(8,128)(2,1)} %copy-done.28, bf16[2,160,256]{2,1,0:T(8,128)(2,1)} %copy-done.30), custom_call_target="tpu_custom_call" | custom-call | flops 2000000000 | bytes 1000000 | tf_op jit(solution)/shard_map/pallas_call | solution.py:385
  20.8 1.9 %collective-permute-start.6 = (bf16[2,2,160,256]{3,2,1,0:T(8,128)(2,1)}, bf16[2,2,160,256]{3,2,1,0:T(8,128)(2,1)S(1)}, u32[]{:S(2)}, u32[]{:S(2)}) collective-permute-start(bf16[2,2,160,256]{3,2,1,0:T(8,128)(2,1)} %get-tuple-element.86), channel_id=1, source_target_pairs={{0,4},{1,5},{2,6},{3,7},{4,0},{5,1},{6,2},{7,3},{8,12},{9,13},{10,... | collective-permute-start | bytes 983048 | tf_op jit(solution)/shard_map/ppermute | solution.py:340
  24.7 2.1 %shard_map.102.refs_1_ = s32[64]{0:T(128)} custom-call(s32[5]{0:T(128)} %stack.31.roles.refs_0_, s32[32,3]{1,0:T(8,128)} %copy.11.local_blocks, s32[32,4]{1,0:T(8,128)} %copy.12.far_blocks, s32[32]{0:T(128)} %counts.1), custom_call_target="tpu_custom_call" | custom-call | tf_op jit(solution)/shard_map/pallas_call | solution.py:369
  27.2 1.8 %collective-permute-start.15 = (bf16[2,160,256]{2,1,0:T(8,128)(2,1)S(1)}, bf16[2,160,256]{2,1,0:T(8,128)(2,1)S(1)}, u32[]{:S(2)}, u32[]{:S(2)}) collective-permute-start(bf16[2,160,256]{2,1,0:T(8,128)(2,1)S(1)} %copy-done.26), channel_id=1, source_target_pairs={{0,2},{1,3},{2,0},{3,1},{4,6},{5,7},{6,4},{7,5},{8,10},{9,11},{10,... | collective-permute-start | bytes 491528 | tf_op jit(solution)/shard_map/ppermute | solution.py:332
  30.0 1.7 %collective-permute-start.16 = (bf16[2,160,256]{2,1,0:T(8,128)(2,1)S(1)}, bf16[2,160,256]{2,1,0:T(8,128)(2,1)S(1)}, u32[]{:S(2)}, u32[]{:S(2)}) collective-permute-start(bf16[2,160,256]{2,1,0:T(8,128)(2,1)S(1)} %copy-done.24), channel_id=1, source_target_pairs={{0,3},{1,2},{2,1},{3,0},{4,7},{5,6},{6,5},{7,4},{8,11},{9,10},{10,... | collective-permute-start | bytes 491528 | tf_op jit(solution)/shard_map/ppermute | solution.py:332
  31.8 2.7 %shard_map.107 = (bf16[2,2,160,256]{3,2,1,0:T(8,128)(2,1)}, bf16[2,2,160,256]{3,2,1,0:T(8,128)(2,1)}) custom-call(s32[5]{0:T(128)} %stack.31.roles.refs_0_, bf16[2,160,256]{2,1,0:T(8,128)(2,1)} %get-tuple-element.96.refs_0_, bf16[2,160,256]{2,1,0:T(8,128)(2,1)} %copy-done.22, bf16[2,160,256]{2,1,0:T(8,128)(2,1)} %copy-done.23, bf16[2,160,256]{2,1,0:T(8,128)(2,1)} %copy-done.25), custom_call_target="tpu_custom_call" | custom-call | flops 2000000000 | bytes 1000000 | tf_op jit(solution)/shard_map/pallas_call | solution.py:385
  34.5 1.6 %collective-permute-start.17 = (bf16[2,2,160,256]{3,2,1,0:T(8,128)(2,1)}, bf16[2,2,160,256]{3,2,1,0:T(8,128)(2,1)S(1)}, u32[]{:S(2)}, u32[]{:S(2)}) collective-permute-start(bf16[2,2,160,256]{3,2,1,0:T(8,128)(2,1)} %get-tuple-element.100), channel_id=1, source_target_pairs={{0,4},{1,5},{2,6},{3,7},{4,0},{5,1},{6,2},{7,3},{8,12},{9,13},{10,... | collective-permute-start | bytes 983048 | tf_op jit(solution)/shard_map/ppermute | solution.py:340
  36.9 12.1 %shard_map.106 = (bf16[2,2,80,256]{3,2,1,0:T(8,128)(2,1)}, bf16[2,2,80,256]{3,2,1,0:T(8,128)(2,1)}, bf16[2,2,80,256]{3,2,1,0:T(8,128)(2,1)}, bf16[2,2,80,256]{3,...) custom-call(s32[5]{0:T(128)} %stack.31.roles.refs_0_, ...), custom_call_target="tpu_custom_call" | custom-call | flops 12000000000 | bytes 1000000 | tf_op jit(solution)/shard_map/pallas_call | solution.py:403
  51.0 2.5 %collective-permute-start.22 = (bf16[2,2,2,80,256]{4,3,2,1,0:T(8,128)(2,1)}, bf16[2,2,2,80,256]{4,3,2,1,0:T(8,128)(2,1)S(1)}, u32[]{:S(2)}, u32[]{:S(2)}) collective-permute-start(bf16[2,2,2,80,256]{4,3,2,1,0:T(8,128)(2,1)} %get-tuple-element.113), channel_id=1, source_target_pairs={{0,4},{1,5},{2,6},{3,7},{4,0},{5,1},{6,2},{7,3},{8,12},{9,13},{10,... | collective-permute-start | bytes 983048 | tf_op jit(solution)/shard_map/ppermute | solution.py:340
  54.1 12.1 %shard_map.108 = (bf16[2,2,80,256]{3,2,1,0:T(8,128)(2,1)}, bf16[2,2,80,256]{3,2,1,0:T(8,128)(2,1)}, bf16[2,2,80,256]{3,2,1,0:T(8,128)(2,1)}, bf16[2,2,80,256]{3,...) custom-call(s32[5]{0:T(128)} %stack.31.roles.refs_0_, ...), custom_call_target="tpu_custom_call" | custom-call | flops 12000000000 | bytes 1000000 | tf_op jit(solution)/shard_map/pallas_call | solution.py:403
  68.3 2.3 %shard_map.110 = (bf16[2,160,256]{2,1,0:T(8,128)(2,1)}, bf16[2,160,256]{2,1,0:T(8,128)(2,1)}, bf16[2,160,256]{2,1,0:T(8,128)(2,1)}, bf16[2,160,256]{2,1,0:T(8,128)(2,1)}) custom-call(s32[5]{0:T(128)} %stack.31.roles.refs_0_, bf16[4,2,160,256]{3,2,1,0:T(8,128)(2,1)} %bitcast.39, bf16[2,2,160,256]{3,2,1,0:T(8,128)(2,1)} %bitcast.42, ...), custom_call_target="tpu_custom_call" | custom-call | tf_op jit(solution)/shard_map/pallas_call | solution.py:438
  70.7 3.1 %collective-permute-done.20.refs_7_ = bf16[2,160,256]{2,1,0:T(8,128)(2,1)S(1)} collective-permute-done((bf16[2,160,256]{2,1,0:T(8,128)(2,1)}, bf16[2,160,256]{2,1,0:T(8,128)(2,1)S(1)}, u32[]{:S(2)}, u32[]{:S(2)}) %collective-permute-start.20) | collective-permute-done | bytes 163872 | tf_op jit(solution)/shard_map/ppermute | solution.py:332
  74.3 1.7 %collective-permute-start.21 = (bf16[2,160,256]{2,1,0:T(8,128)(2,1)S(1)}, bf16[2,160,256]{2,1,0:T(8,128)(2,1)S(1)}, u32[]{:S(2)}, u32[]{:S(2)}) collective-permute-start(bf16[2,160,256]{2,1,0:T(8,128)(2,1)S(1)} %bitcast.59), channel_id=1, source_target_pairs={{0,3},{1,2},{2,1},{3,0},{4,7},{5,6},{6,5},{7,4},{8,11},{9,10},{10,... | collective-permute-start | bytes 491528 | tf_op jit(solution)/shard_map/ppermute | solution.py:332
  77.1 2.3 %shard_map.111 = (bf16[2,160,256]{2,1,0:T(8,128)(2,1)}, bf16[2,160,256]{2,1,0:T(8,128)(2,1)}, bf16[2,160,256]{2,1,0:T(8,128)(2,1)}, bf16[2,160,256]{2,1,0:T(8,128)(2,1)}) custom-call(s32[5]{0:T(128)} %stack.31.roles.refs_0_, bf16[4,2,160,256]{3,2,1,0:T(8,128)(2,1)} %bitcast.40, bf16[2,2,160,256]{3,2,1,0:T(8,128)(2,1)} %bitcast.41, ...), custom_call_target="tpu_custom_call" | custom-call | tf_op jit(solution)/shard_map/pallas_call | solution.py:438
  79.4 1.8 %collective-permute-done.25.refs_3_ = bf16[2,160,256]{2,1,0:T(8,128)(2,1)S(1)} collective-permute-done((bf16[2,160,256]{2,1,0:T(8,128)(2,1)}, bf16[2,160,256]{2,1,0:T(8,128)(2,1)S(1)}, u32[]{:S(2)}, u32[]{:S(2)}) %collective-permute-start.25) | collective-permute-done | bytes 163872 | tf_op jit(solution)/shard_map/ppermute | solution.py:332
  82.6 2.2 %collective-permute-start.31 = (bf16[2,160,256]{2,1,0:T(8,128)(2,1)}, bf16[2,160,256]{2,1,0:T(8,128)(2,1)S(1)}, u32[]{:S(2)}, u32[]{:S(2)}) collective-permute-start(bf16[2,160,256]{2,1,0:T(8,128)(2,1)} %get-tuple-element.133), channel_id=1, source_target_pairs={{0,3},{1,2},{2,1},{3,0},{4,7},{5,6},{6,5},{7,4},{8,11},{9,10},{10,... | collective-permute-start | bytes 491528 | tf_op jit(solution)/shard_map/ppermute | solution.py:332
  84.8 3.4 %shard_map.109 = (bf16[256,1280]{1,0:T(8,128)(2,1)}, bf16[256,1280]{1,0:T(8,128)(2,1)}) custom-call(s32[5]{0:T(128)} %stack.31.roles.refs_0_, bf16[2,160,256]{2,1,0:T(8,128)(2,1)} %bitcast.45, bf16[2,160,256]{2,1,0:T(8,128)(2,1)} %copy-done.4, bf16[2,160,256]{2,1,0:T(8,128)(2,1)} %copy-done.5, bf16[2,160,256]{2,1,0:T(8,128)(2,1)} %copy-done.6, ...), custom_call_target="tpu_custom_call" | custom-call | tf_op jit(solution)/shard_map/pallas_call | solution.py:472
  88.2 3.5 %collective-permute-done.30.refs_7_ = bf16[2,160,256]{2,1,0:T(8,128)(2,1)S(1)} collective-permute-done((bf16[2,160,256]{2,1,0:T(8,128)(2,1)}, bf16[2,160,256]{2,1,0:T(8,128)(2,1)S(1)}, u32[]{:S(2)}, u32[]{:S(2)}) %collective-permute-start.30) | collective-permute-done | bytes 163872 | tf_op jit(solution)/shard_map/ppermute | solution.py:332
  93.2 3.4 %shard_map.112 = (bf16[256,1280]{1,0:T(8,128)(2,1)}, bf16[256,1280]{1,0:T(8,128)(2,1)}) custom-call(s32[5]{0:T(128)} %stack.31.roles.refs_0_, bf16[2,160,256]{2,1,0:T(8,128)(2,1)} %get-tuple-element.119.refs_1_, bf16[2,160,256]{2,1,0:T(8,128)(2,1)} %copy-done.9, bf16[2,160,256]{2,1,0:T(8,128)(2,1)} %copy-done.7, bf16[2,160,256]{2,1,0:T(8,128)(2,1)} %copy-done.10, ...), custom_call_target="tpu_custom_call" | custom-call | tf_op jit(solution)/shard_map/pallas_call | solution.py:472
  (138 shorter events, 17.0 us)
Async XLA Ops:
  4.6 8.7 %collective-permute-start = (bf16[2,160,256]{2,1,0:T(8,128)(2,1)}, bf16[2,160,256]{2,1,0:T(8,128)(2,1)S(1)}, u32[]{:S(2)}, u32[]{:S(2)}) collective-permute-start(bf16[2,160,256]{2,1,0:T(8,128)(2,1)} %get-tuple-element.71), channel_id=1, source_target_pairs={{0,1},{1,0},{2,3},{3,2},{4,5},{5,4},{6,7},{7,6},{8,9},{9,8},{10,11... | collective-permute-start | bytes 491528 | tf_op jit(solution)/shard_map/ppermute | solution.py:332
  11.5 9.2 %collective-permute-start.4 = (bf16[2,160,256]{2,1,0:T(8,128)(2,1)}, bf16[2,160,256]{2,1,0:T(8,128)(2,1)S(1)}, u32[]{:S(2)}, u32[]{:S(2)}) collective-permute-start(bf16[2,160,256]{2,1,0:T(8,128)(2,1)} %get-tuple-element.76), channel_id=1, source_target_pairs={{0,2},{1,3},{2,0},{3,1},{4,6},{5,7},{6,4},{7,5},{8,10},{9,11},{10,... | collective-permute-start | bytes 491528 | tf_op jit(solution)/shard_map/ppermute | solution.py:332
  13.3 9.8 %collective-permute-start.5 = (bf16[2,160,256]{2,1,0:T(8,128)(2,1)}, bf16[2,160,256]{2,1,0:T(8,128)(2,1)S(1)}, u32[]{:S(2)}, u32[]{:S(2)}) collective-permute-start(bf16[2,160,256]{2,1,0:T(8,128)(2,1)} %get-tuple-element.77), channel_id=1, source_target_pairs={{0,3},{1,2},{2,1},{3,0},{4,7},{5,6},{6,5},{7,4},{8,11},{9,10},{10,... | collective-permute-start | bytes 491528 | tf_op jit(solution)/shard_map/ppermute | solution.py:332
  13.4 13.5 %collective-permute-start.11 = (bf16[2,160,256]{2,1,0:T(8,128)(2,1)S(1)}, bf16[2,160,256]{2,1,0:T(8,128)(2,1)S(1)}, u32[]{:S(2)}, u32[]{:S(2)}) collective-permute-start(bf16[2,160,256]{2,1,0:T(8,128)(2,1)S(1)} %copy-done.41), channel_id=1, source_target_pairs={{0,1},{1,0},{2,3},{3,2},{4,5},{5,4},{6,7},{7,6},{8,9},{9,8},{10,11... | collective-permute-start | bytes 491528 | tf_op jit(solution)/shard_map/ppermute | solution.py:332
  16.1 11.2 %collective-permute-start.12 = (bf16[2,160,256]{2,1,0:T(8,128)(2,1)S(1)}, bf16[2,160,256]{2,1,0:T(8,128)(2,1)S(1)}, u32[]{:S(2)}, u32[]{:S(2)}) collective-permute-start(bf16[2,160,256]{2,1,0:T(8,128)(2,1)S(1)} %copy-done.39), channel_id=1, source_target_pairs={{0,2},{1,3},{2,0},{3,1},{4,6},{5,7},{6,4},{7,5},{8,10},{9,11},{10,... | collective-permute-start | bytes 491528 | tf_op jit(solution)/shard_map/ppermute | solution.py:332
  17.6 12.4 %collective-permute-start.13 = (bf16[2,160,256]{2,1,0:T(8,128)(2,1)S(1)}, bf16[2,160,256]{2,1,0:T(8,128)(2,1)S(1)}, u32[]{:S(2)}, u32[]{:S(2)}) collective-permute-start(bf16[2,160,256]{2,1,0:T(8,128)(2,1)S(1)} %copy-done.36), channel_id=1, source_target_pairs={{0,3},{1,2},{2,1},{3,0},{4,7},{5,6},{6,5},{7,4},{8,11},{9,10},{10,... | collective-permute-start | bytes 491528 | tf_op jit(solution)/shard_map/ppermute | solution.py:332
  20.8 13.8 %collective-permute-start.6 = (bf16[2,2,160,256]{3,2,1,0:T(8,128)(2,1)}, bf16[2,2,160,256]{3,2,1,0:T(8,128)(2,1)S(1)}, u32[]{:S(2)}, u32[]{:S(2)}) collective-permute-start(bf16[2,2,160,256]{3,2,1,0:T(8,128)(2,1)} %get-tuple-element.86), channel_id=1, source_target_pairs={{0,4},{1,5},{2,6},{3,7},{4,0},{5,1},{6,2},{7,3},{8,12},{9,13},{10,... | collective-permute-start | bytes 983048 | tf_op jit(solution)/shard_map/ppermute | solution.py:340
  23.1 13.1 %collective-permute-start.7 = (bf16[2,2,160,256]{3,2,1,0:T(8,128)(2,1)}, bf16[2,2,160,256]{3,2,1,0:T(8,128)(2,1)S(1)}, u32[]{:S(2)}, u32[]{:S(2)}) collective-permute-start(bf16[2,2,160,256]{3,2,1,0:T(8,128)(2,1)} %get-tuple-element.87), channel_id=1, source_target_pairs={{0,1},{1,0},{2,3},{3,2},{4,8},{5,9},{6,10},{7,11},{8,4},{9,5},{10,... | collective-permute-start | bytes 983048 | tf_op jit(solution)/shard_map/ppermute | solution.py:340
  26.9 22.1 %collective-permute-start.14 = (bf16[2,160,256]{2,1,0:T(8,128)(2,1)S(1)}, bf16[2,160,256]{2,1,0:T(8,128)(2,1)S(1)}, u32[]{:S(2)}, u32[]{:S(2)}) collective-permute-start(bf16[2,160,256]{2,1,0:T(8,128)(2,1)S(1)} %copy-done.29), channel_id=1, source_target_pairs={{0,1},{1,0},{2,3},{3,2},{4,5},{5,4},{6,7},{7,6},{8,9},{9,8},{10,11... | collective-permute-start | bytes 491528 | tf_op jit(solution)/shard_map/ppermute | solution.py:332
  27.2 21.9 %collective-permute-start.15 = (bf16[2,160,256]{2,1,0:T(8,128)(2,1)S(1)}, bf16[2,160,256]{2,1,0:T(8,128)(2,1)S(1)}, u32[]{:S(2)}, u32[]{:S(2)}) collective-permute-start(bf16[2,160,256]{2,1,0:T(8,128)(2,1)S(1)} %copy-done.26), channel_id=1, source_target_pairs={{0,2},{1,3},{2,0},{3,1},{4,6},{5,7},{6,4},{7,5},{8,10},{9,11},{10,... | collective-permute-start | bytes 491528 | tf_op jit(solution)/shard_map/ppermute | solution.py:332
  30.0 19.8 %collective-permute-start.16 = (bf16[2,160,256]{2,1,0:T(8,128)(2,1)S(1)}, bf16[2,160,256]{2,1,0:T(8,128)(2,1)S(1)}, u32[]{:S(2)}, u32[]{:S(2)}) collective-permute-start(bf16[2,160,256]{2,1,0:T(8,128)(2,1)S(1)} %copy-done.24), channel_id=1, source_target_pairs={{0,3},{1,2},{2,1},{3,0},{4,7},{5,6},{6,5},{7,4},{8,11},{9,10},{10,... | collective-permute-start | bytes 491528 | tf_op jit(solution)/shard_map/ppermute | solution.py:332
  34.5 16.4 %collective-permute-start.17 = (bf16[2,2,160,256]{3,2,1,0:T(8,128)(2,1)}, bf16[2,2,160,256]{3,2,1,0:T(8,128)(2,1)S(1)}, u32[]{:S(2)}, u32[]{:S(2)}) collective-permute-start(bf16[2,2,160,256]{3,2,1,0:T(8,128)(2,1)} %get-tuple-element.100), channel_id=1, source_target_pairs={{0,4},{1,5},{2,6},{3,7},{4,0},{5,1},{6,2},{7,3},{8,12},{9,13},{10,... | collective-permute-start | bytes 983048 | tf_op jit(solution)/shard_map/ppermute | solution.py:340
  36.2 17.2 %collective-permute-start.18 = (bf16[2,2,160,256]{3,2,1,0:T(8,128)(2,1)}, bf16[2,2,160,256]{3,2,1,0:T(8,128)(2,1)S(1)}, u32[]{:S(2)}, u32[]{:S(2)}) collective-permute-start(bf16[2,2,160,256]{3,2,1,0:T(8,128)(2,1)} %get-tuple-element.101), channel_id=1, source_target_pairs={{0,1},{1,0},{2,3},{3,2},{4,8},{5,9},{6,10},{7,11},{8,4},{9,5},{10,... | collective-permute-start | bytes 983048 | tf_op jit(solution)/shard_map/ppermute | solution.py:340
  49.0 17.2 %collective-permute-start.8 = (bf16[2,160,256]{2,1,0:T(8,128)(2,1)}, bf16[2,160,256]{2,1,0:T(8,128)(2,1)S(1)}, u32[]{:S(2)}, u32[]{:S(2)}) collective-permute-start(bf16[2,160,256]{2,1,0:T(8,128)(2,1)} %bitcast.67), channel_id=1, source_target_pairs={{0,1},{1,0},{2,3},{3,2},{4,5},{5,4},{6,7},{7,6},{8,9},{9,8},{10,11... | collective-permute-start | bytes 491528 | tf_op jit(solution)/shard_map/ppermute | solution.py:332
  49.1 17.9 %collective-permute-start.9 = (bf16[2,160,256]{2,1,0:T(8,128)(2,1)}, bf16[2,160,256]{2,1,0:T(8,128)(2,1)S(1)}, u32[]{:S(2)}, u32[]{:S(2)}) collective-permute-start(bf16[2,160,256]{2,1,0:T(8,128)(2,1)} %bitcast.66), channel_id=1, source_target_pairs={{0,2},{1,3},{2,0},{3,1},{4,6},{5,7},{6,4},{7,5},{8,10},{9,11},{10,... | collective-permute-start | bytes 491528 | tf_op jit(solution)/shard_map/ppermute | solution.py:332
  49.8 17.2 %collective-permute-start.10 = (bf16[2,160,256]{2,1,0:T(8,128)(2,1)}, bf16[2,160,256]{2,1,0:T(8,128)(2,1)S(1)}, u32[]{:S(2)}, u32[]{:S(2)}) collective-permute-start(bf16[2,160,256]{2,1,0:T(8,128)(2,1)} %bitcast.65), channel_id=1, source_target_pairs={{0,3},{1,2},{2,1},{3,0},{4,7},{5,6},{6,5},{7,4},{8,11},{9,10},{10,... | collective-permute-start | bytes 491528 | tf_op jit(solution)/shard_map/ppermute | solution.py:332
  51.0 16.5 %collective-permute-start.22 = (bf16[2,2,2,80,256]{4,3,2,1,0:T(8,128)(2,1)}, bf16[2,2,2,80,256]{4,3,2,1,0:T(8,128)(2,1)S(1)}, u32[]{:S(2)}, u32[]{:S(2)}) collective-permute-start(bf16[2,2,2,80,256]{4,3,2,1,0:T(8,128)(2,1)} %get-tuple-element.113), channel_id=1, source_target_pairs={{0,4},{1,5},{2,6},{3,7},{4,0},{5,1},{6,2},{7,3},{8,12},{9,13},{10,... | collective-permute-start | bytes 983048 | tf_op jit(solution)/shard_map/ppermute | solution.py:340
  53.4 14.1 %collective-permute-start.23 = (bf16[2,2,2,80,256]{4,3,2,1,0:T(8,128)(2,1)}, bf16[2,2,2,80,256]{4,3,2,1,0:T(8,128)(2,1)S(1)}, u32[]{:S(2)}, u32[]{:S(2)}) collective-permute-start(bf16[2,2,2,80,256]{4,3,2,1,0:T(8,128)(2,1)} %get-tuple-element.114), channel_id=1, source_target_pairs={{0,1},{1,0},{2,3},{3,2},{4,8},{5,9},{6,10},{7,11},{8,4},{9,5},{10,... | collective-permute-start | bytes 983048 | tf_op jit(solution)/shard_map/ppermute | solution.py:340
  66.3 10.0 %collective-permute-start.27 = (bf16[2,2,2,80,256]{4,3,2,1,0:T(8,128)(2,1)}, bf16[2,2,2,80,256]{4,3,2,1,0:T(8,128)(2,1)S(1)}, u32[]{:S(2)}, u32[]{:S(2)}) collective-permute-start(bf16[2,2,2,80,256]{4,3,2,1,0:T(8,128)(2,1)} %get-tuple-element.124), channel_id=1, source_target_pairs={{0,4},{1,5},{2,6},{3,7},{4,0},{5,1},{6,2},{7,3},{8,12},{9,13},{10,... | collective-permute-start | bytes 983048 | tf_op jit(solution)/shard_map/ppermute | solution.py:340
  67.0 9.2 %collective-permute-start.28 = (bf16[2,2,2,80,256]{4,3,2,1,0:T(8,128)(2,1)}, bf16[2,2,2,80,256]{4,3,2,1,0:T(8,128)(2,1)S(1)}, u32[]{:S(2)}, u32[]{:S(2)}) collective-permute-start(bf16[2,2,2,80,256]{4,3,2,1,0:T(8,128)(2,1)} %get-tuple-element.125), channel_id=1, source_target_pairs={{0,1},{1,0},{2,3},{3,2},{4,8},{5,9},{6,10},{7,11},{8,4},{9,5},{10,... | collective-permute-start | bytes 983048 | tf_op jit(solution)/shard_map/ppermute | solution.py:340
  76.2 12.0 %collective-permute-start.24 = (bf16[2,160,256]{2,1,0:T(8,128)(2,1)}, bf16[2,160,256]{2,1,0:T(8,128)(2,1)S(1)}, u32[]{:S(2)}, u32[]{:S(2)}) collective-permute-start(bf16[2,160,256]{2,1,0:T(8,128)(2,1)} %get-tuple-element.120), channel_id=1, source_target_pairs={{0,1},{1,0},{2,3},{3,2},{4,5},{5,4},{6,7},{7,6},{8,9},{9,8},{10,11... | collective-permute-start | bytes 491528 | tf_op jit(solution)/shard_map/ppermute | solution.py:332
  76.3 12.0 %collective-permute-start.26 = (bf16[2,160,256]{2,1,0:T(8,128)(2,1)}, bf16[2,160,256]{2,1,0:T(8,128)(2,1)S(1)}, u32[]{:S(2)}, u32[]{:S(2)}) collective-permute-start(bf16[2,160,256]{2,1,0:T(8,128)(2,1)} %get-tuple-element.122), channel_id=1, source_target_pairs={{0,3},{1,2},{2,1},{3,0},{4,7},{5,6},{6,5},{7,4},{8,11},{9,10},{10,... | collective-permute-start | bytes 491528 | tf_op jit(solution)/shard_map/ppermute | solution.py:332
  81.2 10.5 %collective-permute-start.30 = (bf16[2,160,256]{2,1,0:T(8,128)(2,1)}, bf16[2,160,256]{2,1,0:T(8,128)(2,1)S(1)}, u32[]{:S(2)}, u32[]{:S(2)}) collective-permute-start(bf16[2,160,256]{2,1,0:T(8,128)(2,1)} %get-tuple-element.132), channel_id=1, source_target_pairs={{0,2},{1,3},{2,0},{3,1},{4,6},{5,7},{6,4},{7,5},{8,10},{9,11},{10,... | collective-permute-start | bytes 491528 | tf_op jit(solution)/shard_map/ppermute | solution.py:332
  82.6 9.9 %collective-permute-start.31 = (bf16[2,160,256]{2,1,0:T(8,128)(2,1)}, bf16[2,160,256]{2,1,0:T(8,128)(2,1)S(1)}, u32[]{:S(2)}, u32[]{:S(2)}) collective-permute-start(bf16[2,160,256]{2,1,0:T(8,128)(2,1)} %get-tuple-element.133), channel_id=1, source_target_pairs={{0,3},{1,2},{2,1},{3,0},{4,7},{5,6},{6,5},{7,4},{8,11},{9,10},{10,... | collective-permute-start | bytes 491528 | tf_op jit(solution)/shard_map/ppermute | solution.py:332
  (50 other events, 246.3 us)

commit v3 on v2

--- a/solution.py
+++ b/solution.py
@@ -14,6 +14,7 @@
 FAR_UP = 2
 WINDOW = 4
 CHAIN = PLANE + FAR_UP + 1
+STRIP = 64
 F32 = jnp.float32
 BF16 = jnp.bfloat16
 ANY = pl.BlockSpec(memory_space=pl.ANY)
@@ -42,16 +43,19 @@
         copy.wait()
 
 
-def prep_kernel(head_size, roles, first_in, second_in, *refs):
+def prep_kernel(head_size, lists, roles, first_in, second_in, *refs):
     count = PLANE * len(CHUNKS)
+    lists_in, refs = refs[:lists], refs[lists:]
     outs = refs[:count]
-    rows, turned, in_sems, sems = refs[count:]
+    rows, turned, in_sems, sems = refs[-4:]
     loads = [
         pltpu.make_async_copy(ref, rows.at[index], in_sems.at[index])
         for index, ref in enumerate((first_in, second_in))
     ]
     for load in loads:
         load.start()
+    if lists:
+        find_limits(roles, *lists_in, refs[count])
     for index, load in enumerate(loads):
         load.wait()
         turned[index] = rows[index].T
@@ -73,7 +77,7 @@
     run_copies(copies)
 
 
-def limits_kernel(roles, local_blocks, far_blocks, counts, out):
+def find_limits(roles, local_blocks, far_blocks, counts, out):
     blocks = counts.shape[0]
     first = roles[1] * (PLANE * 2)
     for query in range(PLANE * 2):
@@ -120,13 +124,8 @@
     outs = rest[:PLANE]
     local_out, even_out, odd_out = rest[PLANE : PLANE + 3]
     chain, query, result, key_sums, sums = rest[PLANE + 3 : PLANE + 8]
-    scores, grads, peaks, weights, sems = (
-        rest[PLANE + 8 : PLANE + 10],
-        rest[PLANE + 10 : PLANE + 12],
-        rest[PLANE + 12 : PLANE + 14],
-        rest[PLANE + 14],
-        rest[PLANE + 15],
-    )
+    scores, grads, peaks = (rest[PLANE + 8 + 2 * i : PLANE + 10 + 2 * i] for i in range(3))
+    weights, grad_scores, sems = rest[PLANE + 14 :]
     place, parity = roles[0], roles[2]
     copies = []
     for hop in range(PLANE):
@@ -163,13 +162,15 @@
         head, unit = index // PLANE, index % PLANE
         tile = dot(chain[unit + k, 0, head], query[unit, 0, head], 0, 0)
         for half in range(2):
-            place_in = 2 * k + half
-            base = unit * 2 * WINDOW * 2 + place_in
+            block = 2 * k + half
+            base = unit * 2 * WINDOW * 2 + block
             limit = jnp.where(lane < BLK, limits[base], limits[base + WINDOW * 2])
-            part = jnp.where(row < limit, tile[half * BLK : (half + 1) * BLK], -1e30)
-            top = jnp.max(part.reshape(BLK // 8, 8, tokens), axis=0)
-            peak = top if peak is None else jnp.maximum(peak, top)
-            scores[slot][place_in * BLK : (place_in + 1) * BLK] = part
+            for at in range(0, BLK, STRIP):
+                part = tile[half * BLK + at : half * BLK + at + STRIP]
+                part = jnp.where(row[at : at + STRIP] < limit, part, -1e30)
+                top = jnp.max(part.reshape(STRIP // 8, 8, tokens), axis=0)
+                peak = top if peak is None else jnp.maximum(peak, top)
+                scores[slot][block * BLK + at : block * BLK + at + STRIP] = part
         return peak
 
     def keep_peak(slot, peak):
@@ -182,24 +183,25 @@
             chain[unit + k, 1, head], query[unit, 1, head], 0, 0
         )
 
-    def step(index, now, later):
+    def step(index, now, later, final=False):
         head, unit = index // PLANE, index % PLANE
-        after = jnp.minimum(index + 1, steps - 1)
         query_t = query[unit, 0, head]
         grad_wide = query[unit, 1, head].astype(F32)
         peak = peaks[now][0:1]
         total = out_t = later_peak = query_grad = None
         for k in range(WINDOW):
             span = slice(k * tokens, (k + 1) * tokens)
-            power = jnp.exp2((scores[now][span] - peak) * rate)
-            part = jnp.sum(power.reshape(tokens // 8, 8, tokens), axis=0)
-            total = part if k == 0 else total + part
-            weight = power.astype(BF16)
-            weights[span] = weight
-            part = dot(chain[unit + k, 1, head], weight, 1, 0)
+            if not final:
+                later_peak = score(index + 1, later, k, later_peak)
+            for at in range(k * tokens, (k + 1) * tokens, STRIP):
+                power = jnp.exp2((scores[now][at : at + STRIP] - peak) * rate)
+                part = jnp.sum(power.reshape(STRIP // 8, 8, tokens), axis=0)
+                total = part if total is None else total + part
+                weights[at : at + STRIP] = power.astype(BF16)
+            part = dot(chain[unit + k, 1, head], weights[span], 1, 0)
             out_t = part if k == 0 else out_t + part
-            later_peak = score(after, later, k, later_peak)
-        keep_peak(later, later_peak)
+        if not final:
+            keep_peak(later, later_peak)
         inverse = 1.0 / jnp.sum(total, axis=0, keepdims=True)
         attended = (out_t * inverse).astype(BF16)
         delta = jnp.sum(grad_wide * attended.astype(F32), axis=0, keepdims=True)
@@ -207,13 +209,17 @@
         query_scaled = (query_t.astype(F32) * inverse).astype(BF16)
         for k in range(WINDOW):
             span = slice(k * tokens, (k + 1) * tokens)
-            weight = weights[span]
-            grad_scores = weight * (grads[now][span] - delta).astype(BF16)
-            part = dot(chain[unit + k, 0, head], grad_scores, 1, 0)
+            key_sums[unit + k, 1, head] += dot(grad_scaled, weights[span], 1, 1)
+        for k in range(WINDOW):
+            span = slice(k * tokens, (k + 1) * tokens)
+            if not final:
+                grad(index + 1, later, k)
+            for at in range(k * tokens, (k + 1) * tokens, STRIP):
+                change = (grads[now][at : at + STRIP] - delta).astype(BF16)
+                grad_scores[at : at + STRIP] = weights[at : at + STRIP] * change
+            part = dot(chain[unit + k, 0, head], grad_scores[span], 1, 0)
             query_grad = part if k == 0 else query_grad + part
-            key_sums[unit + k, 0, head] += dot(query_scaled, grad_scores, 1, 1)
-            key_sums[unit + k, 1, head] += dot(grad_scaled, weight, 1, 1)
-            grad(after, later, k)
+            key_sums[unit + k, 0, head] += dot(query_scaled, grad_scores[span], 1, 1)
         result[unit, 0, head] = attended
         result[unit, 1, head] = (query_grad * (inverse * scale)).astype(BF16)
 
@@ -228,7 +234,9 @@
         step(2 * index + 1, 1, 0)
         return carry
 
-    lax.fori_loop(0, steps // 2, two_steps, 0)
+    lax.fori_loop(0, steps // 2 - 1, two_steps, 0)
+    step(steps - 2, 0, 1)
+    step(steps - 1, 1, 0, final=True)
     copies = [
         pltpu.make_async_copy(result.at[place ^ hop], outs[hop], sems.at[hop])
         for hop in range(PLANE)
@@ -342,12 +350,14 @@
     def piece(heads):
         return jax.ShapeDtypeStruct((2, heads * head_size, tokens), BF16)
 
-    def prep(first, second):
+    def prep(first, second, *lists):
+        limits_shape = jax.ShapeDtypeStruct((PLANE * 2 * WINDOW * 2,), jnp.int32)
         return pl.pallas_call(
-            lambda *refs: prep_kernel(head_size, *refs),
-            out_shape=[piece(heads) for heads in CHUNKS for _ in range(PLANE)],
-            in_specs=[SMEM, ANY, ANY],
-            out_specs=[ANY] * (PLANE * len(CHUNKS)),
+            lambda *refs: prep_kernel(head_size, len(lists), *refs),
+            out_shape=[piece(heads) for heads in CHUNKS for _ in range(PLANE)]
+            + ([limits_shape] if lists else []),
+            in_specs=[SMEM, ANY, ANY] + [SMEM] * len(lists),
+            out_specs=[ANY] * (PLANE * len(CHUNKS)) + ([SMEM] if lists else []),
             scratch_shapes=[
                 pltpu.VMEM((2, tokens, width), BF16),
                 pltpu.VMEM((2, width, tokens), BF16),
@@ -356,7 +366,7 @@
             ],
             compiler_params=params(),
             cost_estimate=cost(3),
-        )(roles, first, second)
+        )(roles, first, second, *lists)
 
     def spread(parts):
         return [
@@ -366,21 +376,14 @@
         ]
 
     key_held = spread(prep(keys, values))
-    limits = pl.pallas_call(
-        limits_kernel,
-        out_shape=jax.ShapeDtypeStruct((PLANE * 2 * WINDOW * 2,), jnp.int32),
-        in_specs=[SMEM] * 4,
-        out_specs=SMEM,
-    )(roles, local_blocks, far_blocks, counts)
-
     query_pieces = []
     key_pieces = []
     halos = []
-    query_ready = prep(queries, cotangent)
+    *query_ready, limits = prep(queries, cotangent, local_blocks, far_blocks, counts)
     query_held = spread(query_ready)
     for chunk, heads in enumerate(CHUNKS):
         held = key_held[chunk]
-        held = after(held, query_held[0][1:] if chunk else query_ready)
+        held = after(held, query_ready)
         pair = jax.ShapeDtypeStruct((2, 2, heads * head_size, tokens), BF16)
         even, odd = pl.pallas_call(
             pack_kernel,
@@ -420,6 +423,7 @@
                 pltpu.VMEM((8, tokens), F32),
                 pltpu.VMEM((8, tokens), F32),
                 pltpu.VMEM((WINDOW * tokens, tokens), BF16),
+                pltpu.VMEM((WINDOW * tokens, tokens), BF16),
                 pltpu.SemaphoreType.DMA((2 * PLANE + 2,)),
             ],
             compiler_params=params(),
@@ -452,21 +456,23 @@
 
     rounds = len(CHUNKS)
     results = [main(chunk) for chunk in range(rounds)]
-    backs = []
     last = None
+    returned = []
     for chunk in range(rounds):
         shape = (2, CHUNKS[chunk] * head_size, tokens)
         out = [part.reshape(shape) for part in results[chunk][:PLANE]]
-        if last is not None:
-            out = after(out, last[1:])
+        if chunk:
+            out = after(out, last[1:] + list(returned[-1]))
         last = spread_one(out)
         query_pieces += last
+        local, even, odd = results[chunk][PLANE:]
+        returned.append((level_swap(even, 0), level_swap(odd, 1)))
     for chunk in range(rounds):
-        local, even, odd = results[chunk][PLANE:]
-        back = join(chunk, local, level_swap(even, 0), level_swap(odd, 1))
-        back = after(back, [last[2]])
-        last = spread_one(back)
-        key_pieces += last
+        local = results[chunk][PLANE]
+        if chunk == rounds - 1:
+            local = after([local], last[1:2] + [back[0]])[0]
+        back = join(chunk, local, *returned[chunk])
+        key_pieces += spread_one(back)
 
     def finish(parts):
         return pl.pallas_call(

time: 97.9 us -> 93.7 us (0.957)
  waiting for transfers between devices: 14.2 us -> 10.9 us
  Pallas kernels: 49.9 us -> 48.3 us
  starting transfers between devices: 26.1 us -> 27.1 us
    ppermute x24, waiting for transfers between devices: 14 us -> 7.87 us  [swap(): return lax.ppermute(array, 'seq', pairs)]
    ppermute x8, waiting for transfers between devices: 0.26 us -> 3.07 us  [level_swap(): return lax.ppermute(array, 'seq', pairs)]
    pallas_call x3 -> x2, Pallas kernels: 8.93 us -> 7.84 us  [prep(): pl.pallas_call(lambda *refs: prep_kernel(head_size, len(lists), *refs), o...]
    unnamed x86 -> x84, local copies, waits for them, and re-layouts: 4.54 us -> 4.26 us
  transfers between devices with their start and end apart: 32 -> 32, of which waited for: 9 -> 6; matrix products, arithmetic and copies ran while one was open for 1% -> 1% of each run, Pallas kernels for 45% -> 45%
where the time goes in v3:
time: 93.7 us; the launch traced here: 92.4 us
  Pallas kernels  48.3 us (52%)
  starting transfers between devices  27.1 us (29%)
  waiting for transfers between devices  10.9 us (12%)
  local copies, waits for them, and re-layouts  4.85 us (5%)
  between operations  1.15 us (1%)
    pallas_call x2, Pallas kernels, main(): pl.pallas_call(lambda *refs: main_kernel(head_size, heads, *refs), out_sh...  23.5 us
    ppermute x24, starting transfers between devices, swap(): return lax.ppermute(array, 'seq', pairs)  19.8 us
    ppermute x24, waiting for transfers between devices, swap(): return lax.ppermute(array, 'seq', pairs)  7.87 us
    pallas_call x2, Pallas kernels, prep(): pl.pallas_call(lambda *refs: prep_kernel(head_size, len(lists), *refs), o...  7.84 us
    ppermute x8, starting transfers between devices, level_swap(): return lax.ppermute(array, 'seq', pairs)  7.31 us
    pallas_call x2, Pallas kernels, finish(): pl.pallas_call(lambda *refs: finish_kernel(head_size, *refs), out_shape=[...  6.8 us
    pallas_call x2, Pallas kernels, body(): pl.pallas_call(pack_kernel, out_shape=[pair, pair], in_specs=[SMEM] + [AN...  5.63 us
    pallas_call x2, Pallas kernels, join(): pl.pallas_call(join_kernel, out_shape=[piece(heads)] * PLANE, in_specs=[S...  4.58 us
  transfers between devices with their start and end apart: 32, of which 6 were waited for; matrix products, arithmetic and copies ran while one was open for 1% of the time, Pallas kernels for 45%

profile of v3, /device:TPU:0, one launch (start us, length us, event | category | flops | bytes accessed | tf_op | source)
XLA Modules:
  0.0 92.4 jit_solution(10248647749260122328)
XLA Ops:
  1.3 3.3 %shard_map.103 = (bf16[2,160,256]{2,1,0:T(8,128)(2,1)}, bf16[2,160,256]{2,1,0:T(8,128)(2,1)}, bf16[2,160,256]{2,1,0:T(8,128)(2,1)}, bf16[2,160,256]{2,1,0:T(8,12...) custom-call(s32[5]{0:T(128)} %stack.31.refs_0_.roles, ...), custom_call_target="tpu_custom_call" | custom-call | flops 3000000000 | bytes 1000000 | tf_op jit(solution)/shard_map/pallas_call | solution.py:355
  5.1 2.6 %collective-permute-start.1 = (bf16[2,160,256]{2,1,0:T(8,128)(2,1)}, bf16[2,160,256]{2,1,0:T(8,128)(2,1)S(1)}, u32[]{:S(2)}, u32[]{:S(2)}) collective-permute-start(bf16[2,160,256]{2,1,0:T(8,128)(2,1)} %get-tuple-element.67), channel_id=1, source_target_pairs={{0,2},{1,3},{2,0},{3,1},{4,6},{5,7},{6,4},{7,5},{8,10},{9,11},{10,... | collective-permute-start | bytes 491528 | tf_op jit(solution)/shard_map/ppermute | solution.py:340
  7.9 1.9 %collective-permute-start.12 = (bf16[2,160,256]{2,1,0:T(8,128)(2,1)}, bf16[2,160,256]{2,1,0:T(8,128)(2,1)S(1)}, u32[]{:S(2)}, u32[]{:S(2)}) collective-permute-start(bf16[2,160,256]{2,1,0:T(8,128)(2,1)} %get-tuple-element.89), channel_id=1, source_target_pairs={{0,2},{1,3},{2,0},{3,1},{4,6},{5,7},{6,4},{7,5},{8,10},{9,11},{10,... | collective-permute-start | bytes 491528 | tf_op jit(solution)/shard_map/ppermute | solution.py:340
  11.2 4.5 %shard_map.102 = (bf16[2,160,256]{2,1,0:T(8,128)(2,1)}, bf16[2,160,256]{2,1,0:T(8,128)(2,1)}, bf16[2,160,256]{2,1,0:T(8,128)(2,1)}, bf16[2,160,256]{2,1,0:T(8,12...) custom-call(s32[5]{0:T(128)} %stack.31.refs_0_.roles, ...), custom_call_target="tpu_custom_call" | custom-call | flops 3000000000 | bytes 1000000 | tf_op jit(solution)/shard_map/pallas_call | solution.py:355
  16.7 2.8 %shard_map.104 = (bf16[2,2,160,256]{3,2,1,0:T(8,128)(2,1)}, bf16[2,2,160,256]{3,2,1,0:T(8,128)(2,1)}) custom-call(s32[5]{0:T(128)} %stack.31.refs_0_.roles, bf16[2,160,256]{2,1,0:T(8,128)(2,1)} %get-tuple-element.77.refs_0_, bf16[2,160,256]{2,1,0:T(8,128)(2,1)} %copy-done.25, bf16[2,160,256]{2,1,0:T(8,128)(2,1)} %copy-done.27, bf16[2,160,256]{2,1,0:T(8,128)(2,1)} %copy-done.28), custom_call_target="tpu_custom_call" | custom-call | flops 2000000000 | bytes 1000000 | tf_op jit(solution)/shard_map/pallas_call | solution.py:388
  19.5 1.6 %collective-permute-start.6 = (bf16[2,2,160,256]{3,2,1,0:T(8,128)(2,1)}, bf16[2,2,160,256]{3,2,1,0:T(8,128)(2,1)S(1)}, u32[]{:S(2)}, u32[]{:S(2)}) collective-permute-start(bf16[2,2,160,256]{3,2,1,0:T(8,128)(2,1)} %get-tuple-element.81), channel_id=1, source_target_pairs={{0,4},{1,5},{2,6},{3,7},{4,0},{5,1},{6,2},{7,3},{8,12},{9,13},{10,... | collective-permute-start | bytes 983048 | tf_op jit(solution)/shard_map/ppermute | solution.py:348
  21.8 1.5 %collective-permute-start.4 = (bf16[2,160,256]{2,1,0:T(8,128)(2,1)S(1)}, bf16[2,160,256]{2,1,0:T(8,128)(2,1)S(1)}, u32[]{:S(2)}, u32[]{:S(2)}) collective-permute-start(bf16[2,160,256]{2,1,0:T(8,128)(2,1)S(1)} %copy-done.37), channel_id=1, source_target_pairs={{0,2},{1,3},{2,0},{3,1},{4,6},{5,7},{6,4},{7,5},{8,10},{9,11},{10,... | collective-permute-start | bytes 491528 | tf_op jit(solution)/shard_map/ppermute | solution.py:340
  23.3 1.4 %collective-permute-start.5 = (bf16[2,160,256]{2,1,0:T(8,128)(2,1)S(1)}, bf16[2,160,256]{2,1,0:T(8,128)(2,1)S(1)}, u32[]{:S(2)}, u32[]{:S(2)}) collective-permute-start(bf16[2,160,256]{2,1,0:T(8,128)(2,1)S(1)} %copy-done.35), channel_id=1, source_target_pairs={{0,3},{1,2},{2,1},{3,0},{4,7},{5,6},{6,5},{7,4},{8,11},{9,10},{10,... | collective-permute-start | bytes 491528 | tf_op jit(solution)/shard_map/ppermute | solution.py:340
  24.8 2.8 %shard_map.106 = (bf16[2,2,160,256]{3,2,1,0:T(8,128)(2,1)}, bf16[2,2,160,256]{3,2,1,0:T(8,128)(2,1)}) custom-call(s32[5]{0:T(128)} %stack.31.refs_0_.roles, bf16[2,160,256]{2,1,0:T(8,128)(2,1)} %get-tuple-element.91.refs_0_, bf16[2,160,256]{2,1,0:T(8,128)(2,1)} %copy-done.22, bf16[2,160,256]{2,1,0:T(8,128)(2,1)} %copy-done.23, bf16[2,160,256]{2,1,0:T(8,128)(2,1)} %copy-done.24), custom_call_target="tpu_custom_call" | custom-call | flops 2000000000 | bytes 1000000 | tf_op jit(solution)/shard_map/pallas_call | solution.py:388
  27.7 1.1 %collective-permute-done.4 = bf16[2,160,256]{2,1,0:T(8,128)(2,1)S(1)} collective-permute-done((bf16[2,160,256]{2,1,0:T(8,128)(2,1)S(1)}, bf16[2,160,256]{2,1,0:T(8,128)(2,1)S(1)}, u32[]{:S(2)}, u32[]{:S(2)}) %collective-permute-start.4) | collective-permute-done | bytes 163872 | tf_op jit(solution)/shard_map/ppermute | solution.py:340
  28.8 1.5 %collective-permute-start.15 = (bf16[2,160,256]{2,1,0:T(8,128)(2,1)S(1)}, bf16[2,160,256]{2,1,0:T(8,128)(2,1)S(1)}, u32[]{:S(2)}, u32[]{:S(2)}) collective-permute-start(bf16[2,160,256]{2,1,0:T(8,128)(2,1)S(1)} %copy-done.29), channel_id=1, source_target_pairs={{0,2},{1,3},{2,0},{3,1},{4,6},{5,7},{6,4},{7,5},{8,10},{9,11},{10,... | collective-permute-start | bytes 491528 | tf_op jit(solution)/shard_map/ppermute | solution.py:340
  30.3 1.1 %collective-permute-done.5 = bf16[2,160,256]{2,1,0:T(8,128)(2,1)S(1)} collective-permute-done((bf16[2,160,256]{2,1,0:T(8,128)(2,1)S(1)}, bf16[2,160,256]{2,1,0:T(8,128)(2,1)S(1)}, u32[]{:S(2)}, u32[]{:S(2)}) %collective-permute-start.5) | collective-permute-done | bytes 163872 | tf_op jit(solution)/shard_map/ppermute | solution.py:340
  31.4 1.8 %collective-permute-start.16 = (bf16[2,160,256]{2,1,0:T(8,128)(2,1)S(1)}, bf16[2,160,256]{2,1,0:T(8,128)(2,1)S(1)}, u32[]{:S(2)}, u32[]{:S(2)}) collective-permute-start(bf16[2,160,256]{2,1,0:T(8,128)(2,1)S(1)} %copy-done.26), channel_id=1, source_target_pairs={{0,3},{1,2},{2,1},{3,0},{4,7},{5,6},{6,5},{7,4},{8,11},{9,10},{10,... | collective-permute-start | bytes 491528 | tf_op jit(solution)/shard_map/ppermute | solution.py:340
  33.3 2.8 %collective-permute-start.17 = (bf16[2,2,160,256]{3,2,1,0:T(8,128)(2,1)}, bf16[2,2,160,256]{3,2,1,0:T(8,128)(2,1)S(1)}, u32[]{:S(2)}, u32[]{:S(2)}) collective-permute-start(bf16[2,2,160,256]{3,2,1,0:T(8,128)(2,1)} %get-tuple-element.95), channel_id=1, source_target_pairs={{0,4},{1,5},{2,6},{3,7},{4,0},{5,1},{6,2},{7,3},{8,12},{9,13},{10,... | collective-permute-start | bytes 983048 | tf_op jit(solution)/shard_map/ppermute | solution.py:348
  36.8 11.7 %shard_map.105 = (bf16[2,2,80,256]{3,2,1,0:T(8,128)(2,1)}, bf16[2,2,80,256]{3,2,1,0:T(8,128)(2,1)}, bf16[2,2,80,256]{3,2,1,0:T(8,128)(2,1)}, bf16[2,2,80,256]{3,...) custom-call(s32[5]{0:T(128)} %stack.31.refs_0_.roles, ...), custom_call_target="tpu_custom_call" | custom-call | flops 12000000000 | bytes 1000000 | tf_op jit(solution)/shard_map/pallas_call | solution.py:406
  49.3 1.2 %collective-permute-start.10 = (bf16[2,160,256]{2,1,0:T(8,128)(2,1)}, bf16[2,160,256]{2,1,0:T(8,128)(2,1)S(1)}, u32[]{:S(2)}, u32[]{:S(2)}) collective-permute-start(bf16[2,160,256]{2,1,0:T(8,128)(2,1)} %bitcast.62), channel_id=1, source_target_pairs={{0,3},{1,2},{2,1},{3,0},{4,7},{5,6},{6,5},{7,4},{8,11},{9,10},{10,... | collective-permute-start | bytes 491528 | tf_op jit(solution)/shard_map/ppermute | solution.py:340
  51.4 11.7 %shard_map.107 = (bf16[2,2,80,256]{3,2,1,0:T(8,128)(2,1)}, bf16[2,2,80,256]{3,2,1,0:T(8,128)(2,1)}, bf16[2,2,80,256]{3,2,1,0:T(8,128)(2,1)}, bf16[2,2,80,256]{3,...) custom-call(s32[5]{0:T(128)} %stack.31.refs_0_.roles, ...), custom_call_target="tpu_custom_call" | custom-call | flops 12000000000 | bytes 1000000 | tf_op jit(solution)/shard_map/pallas_call | solution.py:406
  63.1 2.0 %collective-permute-start.27 = (bf16[2,2,2,80,256]{4,3,2,1,0:T(8,128)(2,1)}, bf16[2,2,2,80,256]{4,3,2,1,0:T(8,128)(2,1)S(1)}, u32[]{:S(2)}, u32[]{:S(2)}) collective-permute-start(bf16[2,2,2,80,256]{4,3,2,1,0:T(8,128)(2,1)} %get-tuple-element.116), channel_id=1, source_target_pairs={{0,4},{1,5},{2,6},{3,7},{4,0},{5,1},{6,2},{7,3},{8,12},{9,13},{10,... | collective-permute-start | bytes 983048 | tf_op jit(solution)/shard_map/ppermute | solution.py:348
  67.2 2.3 %shard_map.109 = (bf16[2,160,256]{2,1,0:T(8,128)(2,1)}, bf16[2,160,256]{2,1,0:T(8,128)(2,1)}, bf16[2,160,256]{2,1,0:T(8,128)(2,1)}, bf16[2,160,256]{2,1,0:T(8,128)(2,1)}) custom-call(s32[5]{0:T(128)} %stack.31.refs_0_.roles, bf16[4,2,160,256]{3,2,1,0:T(8,128)(2,1)} %bitcast.39, bf16[2,2,160,256]{3,2,1,0:T(8,128)(2,1)} %bitcast.41, ...), custom_call_target="tpu_custom_call" | custom-call | tf_op jit(solution)/shard_map/pallas_call | solution.py:442
  70.3 3.1 %collective-permute-done.27 = bf16[2,2,2,80,256]{4,3,2,1,0:T(8,128)(2,1)S(1)} collective-permute-done((bf16[2,2,2,80,256]{4,3,2,1,0:T(8,128)(2,1)}, bf16[2,2,2,80,256]{4,3,2,1,0:T(8,128)(2,1)S(1)}, u32[]{:S(2)}, u32[]{:S(2)}) %collective-permute-start.27) | collective-permute-done | bytes 327712 | tf_op jit(solution)/shard_map/ppermute | solution.py:348
  74.6 2.3 %shard_map.110 = (bf16[2,160,256]{2,1,0:T(8,128)(2,1)}, bf16[2,160,256]{2,1,0:T(8,128)(2,1)}, bf16[2,160,256]{2,1,0:T(8,128)(2,1)}, bf16[2,160,256]{2,1,0:T(8,128)(2,1)}) custom-call(s32[5]{0:T(128)} %stack.31.refs_0_.roles, bf16[4,2,160,256]{3,2,1,0:T(8,128)(2,1)} %bitcast.40, bf16[2,2,160,256]{3,2,1,0:T(8,128)(2,1)} %bitcast.42, ...), custom_call_target="tpu_custom_call" | custom-call | tf_op jit(solution)/shard_map/pallas_call | solution.py:442
  79.4 3.4 %shard_map.108 = (bf16[256,1280]{1,0:T(8,128)(2,1)}, bf16[256,1280]{1,0:T(8,128)(2,1)}) custom-call(s32[5]{0:T(128)} %stack.31.refs_0_.roles, bf16[2,160,256]{2,1,0:T(8,128)(2,1)} %bitcast.45, bf16[2,160,256]{2,1,0:T(8,128)(2,1)} %copy-done.4, bf16[2,160,256]{2,1,0:T(8,128)(2,1)} %copy-done.5, bf16[2,160,256]{2,1,0:T(8,128)(2,1)} %copy-done.6, ...), custom_call_target="tpu_custom_call" | custom-call | tf_op jit(solution)/shard_map/pallas_call | solution.py:478
  82.9 4.9 %collective-permute-done.30.refs_7_ = bf16[2,160,256]{2,1,0:T(8,128)(2,1)S(1)} collective-permute-done((bf16[2,160,256]{2,1,0:T(8,128)(2,1)}, bf16[2,160,256]{2,1,0:T(8,128)(2,1)S(1)}, u32[]{:S(2)}, u32[]{:S(2)}) %collective-permute-start.30) | collective-permute-done | bytes 163872 | tf_op jit(solution)/shard_map/ppermute | solution.py:340
  89.0 3.4 %shard_map.111 = (bf16[256,1280]{1,0:T(8,128)(2,1)}, bf16[256,1280]{1,0:T(8,128)(2,1)}) custom-call(s32[5]{0:T(128)} %stack.31.refs_0_.roles, bf16[2,160,256]{2,1,0:T(8,128)(2,1)} %get-tuple-element.110.refs_1_, bf16[2,160,256]{2,1,0:T(8,128)(2,1)} %copy-done.7, bf16[2,160,256]{2,1,0:T(8,128)(2,1)} %copy-done.10, bf16[2,160,256]{2,1,0:T(8,128)(2,1)} %copy-done.12, ...), custom_call_target="tpu_custom_call" | custom-call | tf_op jit(solution)/shard_map/pallas_call | solution.py:478
  (135 shorter events, 14.3 us)
Async XLA Ops:
  4.6 11.2 %collective-permute-start = (bf16[2,160,256]{2,1,0:T(8,128)(2,1)}, bf16[2,160,256]{2,1,0:T(8,128)(2,1)S(1)}, u32[]{:S(2)}, u32[]{:S(2)}) collective-permute-start(bf16[2,160,256]{2,1,0:T(8,128)(2,1)} %get-tuple-element.66), channel_id=1, source_target_pairs={{0,1},{1,0},{2,3},{3,2},{4,5},{5,4},{6,7},{7,6},{8,9},{9,8},{10,11... | collective-permute-start | bytes 491528 | tf_op jit(solution)/shard_map/ppermute | solution.py:340
  5.1 10.8 %collective-permute-start.1 = (bf16[2,160,256]{2,1,0:T(8,128)(2,1)}, bf16[2,160,256]{2,1,0:T(8,128)(2,1)S(1)}, u32[]{:S(2)}, u32[]{:S(2)}) collective-permute-start(bf16[2,160,256]{2,1,0:T(8,128)(2,1)} %get-tuple-element.67), channel_id=1, source_target_pairs={{0,2},{1,3},{2,0},{3,1},{4,6},{5,7},{6,4},{7,5},{8,10},{9,11},{10,... | collective-permute-start | bytes 491528 | tf_op jit(solution)/shard_map/ppermute | solution.py:340
  7.8 13.8 %collective-permute-start.11 = (bf16[2,160,256]{2,1,0:T(8,128)(2,1)}, bf16[2,160,256]{2,1,0:T(8,128)(2,1)S(1)}, u32[]{:S(2)}, u32[]{:S(2)}) collective-permute-start(bf16[2,160,256]{2,1,0:T(8,128)(2,1)} %get-tuple-element.88), channel_id=1, source_target_pairs={{0,1},{1,0},{2,3},{3,2},{4,5},{5,4},{6,7},{7,6},{8,9},{9,8},{10,11... | collective-permute-start | bytes 491528 | tf_op jit(solution)/shard_map/ppermute | solution.py:340
  7.9 13.8 %collective-permute-start.12 = (bf16[2,160,256]{2,1,0:T(8,128)(2,1)}, bf16[2,160,256]{2,1,0:T(8,128)(2,1)S(1)}, u32[]{:S(2)}, u32[]{:S(2)}) collective-permute-start(bf16[2,160,256]{2,1,0:T(8,128)(2,1)} %get-tuple-element.89), channel_id=1, source_target_pairs={{0,2},{1,3},{2,0},{3,1},{4,6},{5,7},{6,4},{7,5},{8,10},{9,11},{10,... | collective-permute-start | bytes 491528 | tf_op jit(solution)/shard_map/ppermute | solution.py:340
  19.5 13.7 %collective-permute-start.6 = (bf16[2,2,160,256]{3,2,1,0:T(8,128)(2,1)}, bf16[2,2,160,256]{3,2,1,0:T(8,128)(2,1)S(1)}, u32[]{:S(2)}, u32[]{:S(2)}) collective-permute-start(bf16[2,2,160,256]{3,2,1,0:T(8,128)(2,1)} %get-tuple-element.81), channel_id=1, source_target_pairs={{0,4},{1,5},{2,6},{3,7},{4,0},{5,1},{6,2},{7,3},{8,12},{9,13},{10,... | collective-permute-start | bytes 983048 | tf_op jit(solution)/shard_map/ppermute | solution.py:348
  21.2 14.9 %collective-permute-start.7 = (bf16[2,2,160,256]{3,2,1,0:T(8,128)(2,1)}, bf16[2,2,160,256]{3,2,1,0:T(8,128)(2,1)S(1)}, u32[]{:S(2)}, u32[]{:S(2)}) collective-permute-start(bf16[2,2,160,256]{3,2,1,0:T(8,128)(2,1)} %get-tuple-element.82), channel_id=1, source_target_pairs={{0,1},{1,0},{2,3},{3,2},{4,8},{5,9},{6,10},{7,11},{8,4},{9,5},{10,... | collective-permute-start | bytes 983048 | tf_op jit(solution)/shard_map/ppermute | solution.py:348
  27.6 20.9 %collective-permute-start.14 = (bf16[2,160,256]{2,1,0:T(8,128)(2,1)S(1)}, bf16[2,160,256]{2,1,0:T(8,128)(2,1)S(1)}, u32[]{:S(2)}, u32[]{:S(2)}) collective-permute-start(bf16[2,160,256]{2,1,0:T(8,128)(2,1)S(1)} %copy-done.30), channel_id=1, source_target_pairs={{0,1},{1,0},{2,3},{3,2},{4,5},{5,4},{6,7},{7,6},{8,9},{9,8},{10,11... | collective-permute-start | bytes 491528 | tf_op jit(solution)/shard_map/ppermute | solution.py:340
  28.8 19.8 %collective-permute-start.15 = (bf16[2,160,256]{2,1,0:T(8,128)(2,1)S(1)}, bf16[2,160,256]{2,1,0:T(8,128)(2,1)S(1)}, u32[]{:S(2)}, u32[]{:S(2)}) collective-permute-start(bf16[2,160,256]{2,1,0:T(8,128)(2,1)S(1)} %copy-done.29), channel_id=1, source_target_pairs={{0,2},{1,3},{2,0},{3,1},{4,6},{5,7},{6,4},{7,5},{8,10},{9,11},{10,... | collective-permute-start | bytes 491528 | tf_op jit(solution)/shard_map/ppermute | solution.py:340
  31.4 17.9 %collective-permute-start.16 = (bf16[2,160,256]{2,1,0:T(8,128)(2,1)S(1)}, bf16[2,160,256]{2,1,0:T(8,128)(2,1)S(1)}, u32[]{:S(2)}, u32[]{:S(2)}) collective-permute-start(bf16[2,160,256]{2,1,0:T(8,128)(2,1)S(1)} %copy-done.26), channel_id=1, source_target_pairs={{0,3},{1,2},{2,1},{3,0},{4,7},{5,6},{6,5},{7,4},{8,11},{9,10},{10,... | collective-permute-start | bytes 491528 | tf_op jit(solution)/shard_map/ppermute | solution.py:340
  33.3 17.3 %collective-permute-start.17 = (bf16[2,2,160,256]{3,2,1,0:T(8,128)(2,1)}, bf16[2,2,160,256]{3,2,1,0:T(8,128)(2,1)S(1)}, u32[]{:S(2)}, u32[]{:S(2)}) collective-permute-start(bf16[2,2,160,256]{3,2,1,0:T(8,128)(2,1)} %get-tuple-element.95), channel_id=1, source_target_pairs={{0,4},{1,5},{2,6},{3,7},{4,0},{5,1},{6,2},{7,3},{8,12},{9,13},{10,... | collective-permute-start | bytes 983048 | tf_op jit(solution)/shard_map/ppermute | solution.py:348
  36.1 14.6 %collective-permute-start.18 = (bf16[2,2,160,256]{3,2,1,0:T(8,128)(2,1)}, bf16[2,2,160,256]{3,2,1,0:T(8,128)(2,1)S(1)}, u32[]{:S(2)}, u32[]{:S(2)}) collective-permute-start(bf16[2,2,160,256]{3,2,1,0:T(8,128)(2,1)} %get-tuple-element.96), channel_id=1, source_target_pairs={{0,1},{1,0},{2,3},{3,2},{4,8},{5,9},{6,10},{7,11},{8,4},{9,5},{10,... | collective-permute-start | bytes 983048 | tf_op jit(solution)/shard_map/ppermute | solution.py:348
  48.6 14.5 %collective-permute-start.8 = (bf16[2,160,256]{2,1,0:T(8,128)(2,1)}, bf16[2,160,256]{2,1,0:T(8,128)(2,1)S(1)}, u32[]{:S(2)}, u32[]{:S(2)}) collective-permute-start(bf16[2,160,256]{2,1,0:T(8,128)(2,1)} %bitcast.65), channel_id=1, source_target_pairs={{0,1},{1,0},{2,3},{3,2},{4,5},{5,4},{6,7},{7,6},{8,9},{9,8},{10,11... | collective-permute-start | bytes 491528 | tf_op jit(solution)/shard_map/ppermute | solution.py:340
  48.7 16.5 %collective-permute-start.9 = (bf16[2,160,256]{2,1,0:T(8,128)(2,1)}, bf16[2,160,256]{2,1,0:T(8,128)(2,1)S(1)}, u32[]{:S(2)}, u32[]{:S(2)}) collective-permute-start(bf16[2,160,256]{2,1,0:T(8,128)(2,1)} %bitcast.63), channel_id=1, source_target_pairs={{0,2},{1,3},{2,0},{3,1},{4,6},{5,7},{6,4},{7,5},{8,10},{9,11},{10,... | collective-permute-start | bytes 491528 | tf_op jit(solution)/shard_map/ppermute | solution.py:340
  49.3 15.9 %collective-permute-start.10 = (bf16[2,160,256]{2,1,0:T(8,128)(2,1)}, bf16[2,160,256]{2,1,0:T(8,128)(2,1)S(1)}, u32[]{:S(2)}, u32[]{:S(2)}) collective-permute-start(bf16[2,160,256]{2,1,0:T(8,128)(2,1)} %bitcast.62), channel_id=1, source_target_pairs={{0,3},{1,2},{2,1},{3,0},{4,7},{5,6},{6,5},{7,4},{8,11},{9,10},{10,... | collective-permute-start | bytes 491528 | tf_op jit(solution)/shard_map/ppermute | solution.py:340
  50.5 14.6 %collective-permute-start.19 = (bf16[2,2,2,80,256]{4,3,2,1,0:T(8,128)(2,1)}, bf16[2,2,2,80,256]{4,3,2,1,0:T(8,128)(2,1)S(1)}, u32[]{:S(2)}, u32[]{:S(2)}) collective-permute-start(bf16[2,2,2,80,256]{4,3,2,1,0:T(8,128)(2,1)} %get-tuple-element.101), channel_id=1, source_target_pairs={{0,4},{1,5},{2,6},{3,7},{4,0},{5,1},{6,2},{7,3},{8,12},{9,13},{10,... | collective-permute-start | bytes 983048 | tf_op jit(solution)/shard_map/ppermute | solution.py:348
  50.6 14.5 %collective-permute-start.20 = (bf16[2,2,2,80,256]{4,3,2,1,0:T(8,128)(2,1)}, bf16[2,2,2,80,256]{4,3,2,1,0:T(8,128)(2,1)S(1)}, u32[]{:S(2)}, u32[]{:S(2)}) collective-permute-start(bf16[2,2,2,80,256]{4,3,2,1,0:T(8,128)(2,1)} %get-tuple-element.102), channel_id=1, source_target_pairs={{0,1},{1,0},{2,3},{3,2},{4,8},{5,9},{6,10},{7,11},{8,4},{9,5},{10,... | collective-permute-start | bytes 983048 | tf_op jit(solution)/shard_map/ppermute | solution.py:348
  63.1 10.2 %collective-permute-start.27 = (bf16[2,2,2,80,256]{4,3,2,1,0:T(8,128)(2,1)}, bf16[2,2,2,80,256]{4,3,2,1,0:T(8,128)(2,1)S(1)}, u32[]{:S(2)}, u32[]{:S(2)}) collective-permute-start(bf16[2,2,2,80,256]{4,3,2,1,0:T(8,128)(2,1)} %get-tuple-element.116), channel_id=1, source_target_pairs={{0,4},{1,5},{2,6},{3,7},{4,0},{5,1},{6,2},{7,3},{8,12},{9,13},{10,... | collective-permute-start | bytes 983048 | tf_op jit(solution)/shard_map/ppermute | solution.py:348
  65.8 11.2 %collective-permute-start.22 = (bf16[2,160,256]{2,1,0:T(8,128)(2,1)}, bf16[2,160,256]{2,1,0:T(8,128)(2,1)S(1)}, u32[]{:S(2)}, u32[]{:S(2)}) collective-permute-start(bf16[2,160,256]{2,1,0:T(8,128)(2,1)} %bitcast.60), channel_id=1, source_target_pairs={{0,2},{1,3},{2,0},{3,1},{4,6},{5,7},{6,4},{7,5},{8,10},{9,11},{10,... | collective-permute-start | bytes 491528 | tf_op jit(solution)/shard_map/ppermute | solution.py:340
  66.3 11.6 %collective-permute-start.23 = (bf16[2,160,256]{2,1,0:T(8,128)(2,1)}, bf16[2,160,256]{2,1,0:T(8,128)(2,1)S(1)}, u32[]{:S(2)}, u32[]{:S(2)}) collective-permute-start(bf16[2,160,256]{2,1,0:T(8,128)(2,1)} %bitcast.58), channel_id=1, source_target_pairs={{0,3},{1,2},{2,1},{3,0},{4,7},{5,6},{6,5},{7,4},{8,11},{9,10},{10,... | collective-permute-start | bytes 491528 | tf_op jit(solution)/shard_map/ppermute | solution.py:340
  69.5 9.1 %collective-permute-start.24 = (bf16[2,160,256]{2,1,0:T(8,128)(2,1)}, bf16[2,160,256]{2,1,0:T(8,128)(2,1)S(1)}, u32[]{:S(2)}, u32[]{:S(2)}) collective-permute-start(bf16[2,160,256]{2,1,0:T(8,128)(2,1)} %get-tuple-element.111), channel_id=1, source_target_pairs={{0,1},{1,0},{2,3},{3,2},{4,5},{5,4},{6,7},{7,6},{8,9},{9,8},{10,11... | collective-permute-start | bytes 491528 | tf_op jit(solution)/shard_map/ppermute | solution.py:340
  73.4 9.4 %collective-permute-start.25 = (bf16[2,160,256]{2,1,0:T(8,128)(2,1)}, bf16[2,160,256]{2,1,0:T(8,128)(2,1)S(1)}, u32[]{:S(2)}, u32[]{:S(2)}) collective-permute-start(bf16[2,160,256]{2,1,0:T(8,128)(2,1)} %get-tuple-element.112), channel_id=1, source_target_pairs={{0,2},{1,3},{2,0},{3,1},{4,6},{5,7},{6,4},{7,5},{8,10},{9,11},{10,... | collective-permute-start | bytes 491528 | tf_op jit(solution)/shard_map/ppermute | solution.py:340
  73.9 8.9 %collective-permute-start.26 = (bf16[2,160,256]{2,1,0:T(8,128)(2,1)}, bf16[2,160,256]{2,1,0:T(8,128)(2,1)S(1)}, u32[]{:S(2)}, u32[]{:S(2)}) collective-permute-start(bf16[2,160,256]{2,1,0:T(8,128)(2,1)} %get-tuple-element.113), channel_id=1, source_target_pairs={{0,3},{1,2},{2,1},{3,0},{4,7},{5,6},{6,5},{7,4},{8,11},{9,10},{10,... | collective-permute-start | bytes 491528 | tf_op jit(solution)/shard_map/ppermute | solution.py:340
  77.9 9.8 %collective-permute-start.30 = (bf16[2,160,256]{2,1,0:T(8,128)(2,1)}, bf16[2,160,256]{2,1,0:T(8,128)(2,1)S(1)}, u32[]{:S(2)}, u32[]{:S(2)}) collective-permute-start(bf16[2,160,256]{2,1,0:T(8,128)(2,1)} %get-tuple-element.120), channel_id=1, source_target_pairs={{0,2},{1,3},{2,0},{3,1},{4,6},{5,7},{6,4},{7,5},{8,10},{9,11},{10,... | collective-permute-start | bytes 491528 | tf_op jit(solution)/shard_map/ppermute | solution.py:340
  78.6 9.7 %collective-permute-start.31 = (bf16[2,160,256]{2,1,0:T(8,128)(2,1)}, bf16[2,160,256]{2,1,0:T(8,128)(2,1)S(1)}, u32[]{:S(2)}, u32[]{:S(2)}) collective-permute-start(bf16[2,160,256]{2,1,0:T(8,128)(2,1)} %get-tuple-element.121), channel_id=1, source_target_pairs={{0,3},{1,2},{2,1},{3,0},{4,7},{5,6},{6,5},{7,4},{8,11},{9,10},{10,... | collective-permute-start | bytes 491528 | tf_op jit(solution)/shard_map/ppermute | solution.py:340
  (49 other events, 190.9 us)

commit v4 on v3

--- a/solution.py
+++ b/solution.py
@@ -17,12 +17,12 @@
 STRIP = 64
 F32 = jnp.float32
 BF16 = jnp.bfloat16
-ANY = pl.BlockSpec(memory_space=pl.ANY)
+HBM = pl.BlockSpec(memory_space=pltpu.HBM)
 SMEM = pl.BlockSpec(memory_space=pltpu.SMEM)
 VMEM = pl.BlockSpec(memory_space=pltpu.VMEM)
 
 
-def params(mib=60):
+def params(mib=64):
     return pltpu.CompilerParams(vmem_limit_bytes=mib << 20)
 
 
@@ -34,6 +34,14 @@
     return pl.CostEstimate(
         flops=microseconds * 1_000_000_000, bytes_accessed=1_000_000, transcendentals=0
     )
+
+
+def place_of():
+    return lax.axis_index("seq") % PLANE
+
+
+def level_of():
+    return lax.axis_index("seq") // PLANE
 
 
 def run_copies(copies):
@@ -43,43 +51,44 @@
         copy.wait()
 
 
-def prep_kernel(head_size, lists, roles, first_in, second_in, *refs):
-    count = PLANE * len(CHUNKS)
+def prep_kernel(head_size, chunks, lists, first_in, second_in, *refs):
     lists_in, refs = refs[:lists], refs[lists:]
+    count = PLANE * len(chunks)
     outs = refs[:count]
     rows, turned, in_sems, sems = refs[-4:]
+    width = rows.shape[2]
+    begin = PLANE * sum(CHUNKS[: chunks[0]]) * head_size
     loads = [
-        pltpu.make_async_copy(ref, rows.at[index], in_sems.at[index])
+        pltpu.make_async_copy(ref.at[:, pl.ds(begin, width)], rows.at[index], in_sems.at[index])
         for index, ref in enumerate((first_in, second_in))
     ]
     for load in loads:
         load.start()
     if lists:
-        find_limits(roles, *lists_in, refs[count])
+        find_limits(*lists_in, refs[count])
     for index, load in enumerate(loads):
         load.wait()
         turned[index] = rows[index].T
-    place = roles[0]
+    place = place_of()
     copies = []
-    per_device = HEADS // PLANE
     first = 0
-    for chunk, heads in enumerate(CHUNKS):
+    for number, chunk in enumerate(chunks):
+        span = CHUNKS[chunk] * head_size
         for hop in range(PLANE):
-            group = place ^ hop
-            row = pl.multiple_of((group * per_device + first) * head_size, 16)
-            number = chunk * PLANE + hop
+            row = pl.multiple_of(first + (place ^ hop) * span, 16)
+            slot = number * PLANE + hop
             copies.append(
                 pltpu.make_async_copy(
-                    turned.at[:, pl.ds(row, heads * head_size)], outs[number], sems.at[number]
+                    turned.at[:, pl.ds(row, span)], outs[slot], sems.at[slot]
                 )
             )
-        first += heads
+        first += PLANE * span
     run_copies(copies)
 
 
-def find_limits(roles, local_blocks, far_blocks, counts, out):
+def find_limits(local_blocks, far_blocks, counts, out):
     blocks = counts.shape[0]
-    first = roles[1] * (PLANE * 2)
+    first = level_of() * (PLANE * 2)
     for query in range(PLANE * 2):
         listed = [local_blocks[first + query, s] for s in range(local_blocks.shape[1])]
         listed += [far_blocks[first + query, s] for s in range(far_blocks.shape[1])]
@@ -93,11 +102,11 @@
             out[query * WINDOW * 2 + slot] = jnp.where(found & inside, count, 0)
 
 
-def pack_kernel(roles, *refs):
+def pack_kernel(*refs):
     pieces = refs[:PLANE]
     even, odd = refs[PLANE : PLANE + 2]
     plane, sems = refs[PLANE + 2 :]
-    place, parity = roles[0], roles[2]
+    place, parity = place_of(), level_of() % 2
     run_copies(
         [
             pltpu.make_async_copy(pieces[hop], plane.at[place ^ hop], sems.at[hop])
@@ -116,7 +125,7 @@
     return lax.dot_general(a, b, (((left,), (right,)), ((), ())), preferred_element_type=F32)
 
 
-def main_kernel(head_size, heads, roles, limits, *refs):
+def main_kernel(head_size, heads, limits, *refs):
     key_pieces = refs[:PLANE]
     query_pieces = refs[PLANE : 2 * PLANE]
     even_in, odd_in = refs[2 * PLANE : 2 * PLANE + 2]
@@ -126,7 +135,7 @@
     chain, query, result, key_sums, sums = rest[PLANE + 3 : PLANE + 8]
     scores, grads, peaks = (rest[PLANE + 8 + 2 * i : PLANE + 10 + 2 * i] for i in range(3))
     weights, grad_scores, sems = rest[PLANE + 14 :]
-    place, parity = roles[0], roles[2]
+    place, parity = place_of(), level_of() % 2
     copies = []
     for hop in range(PLANE):
         unit = place ^ hop
@@ -259,19 +268,19 @@
         copy.wait()
 
 
-def join_kernel(roles, local, even_in, odd_in, *refs):
+def join_kernel(planes, local, even_in, odd_in, *refs):
     outs = refs[:PLANE]
     held, sems = refs[PLANE:]
-    place, parity = roles[0], roles[2]
-    below_ok, above_ok = roles[3], roles[4]
+    place, parity = place_of(), level_of() % 2
+    level = level_of()
     held[...] = local[...]
 
     def take(below, above):
-        @pl.when(below_ok == 1)
+        @pl.when(level > 0)
         def _():
             held[0] = (held[0].astype(F32) + below[0].astype(F32)).astype(BF16)
 
-        @pl.when(above_ok == 1)
+        @pl.when(level < planes - 1)
         def _():
             for unit in range(2):
                 held[2 + unit] = (held[2 + unit].astype(F32) + above[unit].astype(F32)).astype(
@@ -294,28 +303,43 @@
     )
 
 
-def finish_kernel(head_size, roles, *refs):
-    count = PLANE * len(CHUNKS)
+def finish_kernel(head_size, chunks, held, *refs):
+    count = PLANE * len(chunks)
     pieces = refs[:count]
-    first_out, second_out, turned, sems = refs[count:]
-    place = roles[0]
-    per_device = HEADS // PLANE
-    copies = []
+    outs = refs[count + held : count + held + 2]
+    turned, rows, sems, out_sems = refs[count + held + 2 :]
+    place = place_of()
+    begin = PLANE * sum(CHUNKS[: chunks[0]]) * head_size
+    width = rows.shape[2]
+    loads = []
     first = 0
-    for chunk, heads in enumerate(CHUNKS):
+    for number, chunk in enumerate(chunks):
+        span = CHUNKS[chunk] * head_size
         for hop in range(PLANE):
-            group = place ^ hop
-            row = pl.multiple_of((group * per_device + first) * head_size, 16)
-            number = chunk * PLANE + hop
-            copies.append(
-                pltpu.make_async_copy(
-                    pieces[number], turned.at[:, pl.ds(row, heads * head_size)], sems.at[number]
+            row = pl.multiple_of(first + (place ^ hop) * span, 16)
+            for tensor in range(2):
+                loads.append(
+                    pltpu.make_async_copy(
+                        pieces[number * PLANE + hop].at[tensor],
+                        turned.at[tensor, pl.ds(row, span)],
+                        sems.at[tensor, number * PLANE + hop],
+                    )
                 )
-            )
-        first += heads
-    run_copies(copies)
-    first_out[...] = turned[0].T
-    second_out[...] = turned[1].T
+        first += PLANE * span
+    for load in loads:
+        load.start()
+    stores = []
+    for tensor in range(2):
+        for load in loads[tensor::2]:
+            load.wait()
+        rows[tensor] = turned[tensor].T
+        store = pltpu.make_async_copy(
+            rows.at[tensor], outs[tensor].at[:, pl.ds(begin, width)], out_sems.at[tensor]
+        )
+        store.start()
+        stores.append(store)
+    for store in stores:
+        store.wait()
 
 
 def body(queries, keys, values, cotangent, local_blocks, far_blocks, counts):
@@ -323,18 +347,6 @@
     head_size = width // HEADS
     size = lax.axis_size("seq")
     planes = size // PLANE
-    device = lax.axis_index("seq")
-    level = device // PLANE
-    roles = jnp.stack(
-        [
-            device % PLANE,
-            level,
-            level % 2,
-            (level > 0).astype(jnp.int32),
-            (level < planes - 1).astype(jnp.int32),
-        ]
-    ).astype(jnp.int32)
-
     def swap(array, hop):
         pairs = [(i, (i // PLANE) * PLANE + ((i % PLANE) ^ hop)) for i in range(size)]
         return lax.ppermute(array, "seq", pairs)
@@ -350,37 +362,41 @@
     def piece(heads):
         return jax.ShapeDtypeStruct((2, heads * head_size, tokens), BF16)
 
-    def prep(first, second, *lists):
+    def prep(first, second, chunks, *lists):
+        span = PLANE * sum(CHUNKS[chunk] for chunk in chunks) * head_size
         limits_shape = jax.ShapeDtypeStruct((PLANE * 2 * WINDOW * 2,), jnp.int32)
+        count = PLANE * len(chunks)
         return pl.pallas_call(
-            lambda *refs: prep_kernel(head_size, len(lists), *refs),
-            out_shape=[piece(heads) for heads in CHUNKS for _ in range(PLANE)]
+            lambda *refs: prep_kernel(head_size, chunks, len(lists), *refs),
+            out_shape=[piece(CHUNKS[chunk]) for chunk in chunks for _ in range(PLANE)]
             + ([limits_shape] if lists else []),
-            in_specs=[SMEM, ANY, ANY] + [SMEM] * len(lists),
-            out_specs=[ANY] * (PLANE * len(CHUNKS)) + ([SMEM] if lists else []),
+            in_specs=[HBM, HBM] + [SMEM] * len(lists),
+            out_specs=[HBM] * count + ([SMEM] if lists else []),
             scratch_shapes=[
-                pltpu.VMEM((2, tokens, width), BF16),
-                pltpu.VMEM((2, width, tokens), BF16),
+                pltpu.VMEM((2, tokens, span), BF16),
+                pltpu.VMEM((2, span, tokens), BF16),
                 pltpu.SemaphoreType.DMA((2,)),
-                pltpu.SemaphoreType.DMA((PLANE * len(CHUNKS),)),
+                pltpu.SemaphoreType.DMA((count,)),
             ],
             compiler_params=params(),
             cost_estimate=cost(3),
-        )(roles, first, second, *lists)
+        )(first, second, *lists)
 
     def spread(parts):
-        return [
-            [parts[chunk * PLANE]]
-            + [swap(parts[chunk * PLANE + hop], hop) for hop in range(1, PLANE)]
-            for chunk in range(len(CHUNKS))
-        ]
-
-    key_held = spread(prep(keys, values))
+        return [parts[0]] + [swap(parts[hop], hop) for hop in range(1, PLANE)]
+
+    rounds = len(CHUNKS)
+    every = tuple(range(rounds))
+    key_held = [
+        spread(key_ready[PLANE * chunk : PLANE * (chunk + 1)])
+        for key_ready in [prep(keys, values, every)]
+        for chunk in every
+    ]
     query_pieces = []
     key_pieces = []
     halos = []
-    *query_ready, limits = prep(queries, cotangent, local_blocks, far_blocks, counts)
-    query_held = spread(query_ready)
+    *query_ready, limits = prep(queries, cotangent, every, local_blocks, far_blocks, counts)
+    query_held = [spread(query_ready[PLANE * chunk : PLANE * (chunk + 1)]) for chunk in every]
     for chunk, heads in enumerate(CHUNKS):
         held = key_held[chunk]
         held = after(held, query_ready)
@@ -388,15 +404,15 @@
         even, odd = pl.pallas_call(
             pack_kernel,
             out_shape=[pair, pair],
-            in_specs=[SMEM] + [ANY] * PLANE,
-            out_specs=[ANY, ANY],
+            in_specs=[HBM] * PLANE,
+            out_specs=[HBM, HBM],
             scratch_shapes=[
                 pltpu.VMEM((PLANE, 2, heads * head_size, tokens), BF16),
                 pltpu.SemaphoreType.DMA((PLANE,)),
             ],
             compiler_params=params(),
             cost_estimate=cost(2),
-        )(roles, *held)
+        )(*held)
         halos.append((level_swap(even, 0), level_swap(odd, 1)))
 
     def main(chunk):
@@ -408,8 +424,8 @@
             out_shape=[jax.ShapeDtypeStruct((2,) + shape, BF16)] * PLANE
             + [jax.ShapeDtypeStruct((PLANE, 2) + shape, BF16)]
             + [jax.ShapeDtypeStruct((2, 2) + shape, BF16)] * 2,
-            in_specs=[SMEM, SMEM] + [ANY] * (2 * PLANE + 2),
-            out_specs=[ANY] * (PLANE + 3),
+            in_specs=[SMEM] + [HBM] * (2 * PLANE + 2),
+            out_specs=[HBM] * (PLANE + 3),
             scratch_shapes=[
                 pltpu.VMEM((CHAIN + 1, 2) + shape, BF16),
                 pltpu.VMEM((PLANE, 2) + shape, BF16),
@@ -429,7 +445,6 @@
             compiler_params=params(),
             cost_estimate=cost(6 * heads),
         )(
-            roles,
             limits,
             *[part.reshape((2,) + shape) for part in key_held[chunk] + query_held[chunk]],
             even.reshape((2, 2) + shape),
@@ -440,21 +455,17 @@
         heads = CHUNKS[chunk]
         flat = (2, heads * head_size, tokens)
         return pl.pallas_call(
-            join_kernel,
+            lambda *refs: join_kernel(size // PLANE, *refs),
             out_shape=[piece(heads)] * PLANE,
-            in_specs=[SMEM] + [VMEM] * 3,
-            out_specs=[ANY] * PLANE,
+            in_specs=[VMEM] * 3,
+            out_specs=[HBM] * PLANE,
             scratch_shapes=[
                 pltpu.VMEM((PLANE,) + flat, BF16),
                 pltpu.SemaphoreType.DMA((PLANE,)),
             ],
             compiler_params=params(),
-        )(roles, local.reshape((PLANE,) + flat), even.reshape((2,) + flat), odd.reshape((2,) + flat))
-
-    def spread_one(parts):
-        return [parts[0]] + [swap(parts[hop], hop) for hop in range(1, PLANE)]
-
-    rounds = len(CHUNKS)
+        )(local.reshape((PLANE,) + flat), even.reshape((2,) + flat), odd.reshape((2,) + flat))
+
     results = [main(chunk) for chunk in range(rounds)]
     last = None
     returned = []
@@ -463,7 +474,7 @@
         out = [part.reshape(shape) for part in results[chunk][:PLANE]]
         if chunk:
             out = after(out, last[1:] + list(returned[-1]))
-        last = spread_one(out)
+        last = spread(out)
         query_pieces += last
         local, even, odd = results[chunk][PLANE:]
         returned.append((level_swap(even, 0), level_swap(odd, 1)))
@@ -472,24 +483,31 @@
         if chunk == rounds - 1:
             local = after([local], last[1:2] + [back[0]])[0]
         back = join(chunk, local, *returned[chunk])
-        key_pieces += spread_one(back)
-
-    def finish(parts):
+        key_pieces += spread(back)
+
+    def finish(parts, chunks, held=()):
+        span = PLANE * sum(CHUNKS[chunk] for chunk in chunks) * head_size
         return pl.pallas_call(
-            lambda *refs: finish_kernel(head_size, *refs),
+            lambda *refs: finish_kernel(head_size, chunks, len(held), *refs),
             out_shape=[jax.ShapeDtypeStruct((tokens, width), BF16)] * 2,
-            in_specs=[SMEM] + [ANY] * len(parts),
-            out_specs=[VMEM, VMEM],
+            in_specs=[HBM] * (len(parts) + len(held)),
+            out_specs=[HBM, HBM],
             scratch_shapes=[
-                pltpu.VMEM((2, width, tokens), BF16),
-                pltpu.SemaphoreType.DMA((len(parts),)),
+                pltpu.VMEM((2, span, tokens), BF16),
+                pltpu.VMEM((2, tokens, span), BF16),
+                pltpu.SemaphoreType.DMA((2, len(parts))),
+                pltpu.SemaphoreType.DMA((2,)),
             ],
+            input_output_aliases={len(parts) + index: index for index in range(len(held))},
             compiler_params=params(),
-        )(roles, *parts)
-
-    attended, query_grad = finish(query_pieces)
-    key_grad, value_grad = finish(key_pieces)
-    return attended, query_grad, key_grad, value_grad
+            cost_estimate=cost(3),
+        )(*parts, *held)
+
+    attended, query_grad = finish(query_pieces, every)
+    sums = ()
+    for chunk in every:
+        sums = finish(key_pieces[PLANE * chunk : PLANE * (chunk + 1)], (chunk,), sums)
+    return attended, query_grad, *sums
 
 
 def solution(mesh):

time: 93.7 us -> 91.4 us (0.975)
  local copies, waits for them, and re-layouts: 4.85 us -> 1.38 us
  waiting for transfers between devices: 10.9 us -> 14.3 us
  Pallas kernels: 48.3 us -> 46.3 us
    unnamed x84 -> x6, local copies, waits for them, and re-layouts: 4.26 us -> 1.38 us
    ppermute x8, waiting for transfers between devices: 3.07 us -> 5.14 us  [level_swap(): return lax.ppermute(array, 'seq', pairs)]
    pallas_call x8 -> x9, Pallas kernels: 24.8 us -> 22.9 us  [the longest x3 7.22 us: finish(): pl.pallas_call(lambda *refs: finish_kernel(head_size, chunks, len(held),...]
    ppermute x24, waiting for transfers between devices: 7.87 us -> 9.12 us  [swap(): return lax.ppermute(array, 'seq', pairs)]
  transfers between devices with their start and end apart: 32 -> 32, of which waited for: 6 -> 8; matrix products, arithmetic and copies ran while one was open for 1% -> 2% of each run, Pallas kernels for 45% -> 46%
where the time goes in v4:
time: 91.4 us; the launch traced here: 90.8 us
  Pallas kernels  46.3 us (51%)
  starting transfers between devices  28 us (31%)
  waiting for transfers between devices  14.3 us (16%)
  local copies, waits for them, and re-layouts  1.38 us (2%)
    pallas_call x2, Pallas kernels, main(): pl.pallas_call(lambda *refs: main_kernel(head_size, heads, *refs), out_sh...  23.5 us
    ppermute x24, starting transfers between devices, swap(): return lax.ppermute(array, 'seq', pairs)  20.7 us
    ppermute x24, waiting for transfers between devices, swap(): return lax.ppermute(array, 'seq', pairs)  9.12 us
    ppermute x8, starting transfers between devices, level_swap(): return lax.ppermute(array, 'seq', pairs)  7.34 us
    pallas_call x3, Pallas kernels, finish(): pl.pallas_call(lambda *refs: finish_kernel(head_size, chunks, len(held),...  7.22 us
    pallas_call x2, Pallas kernels, prep(): pl.pallas_call(lambda *refs: prep_kernel(head_size, chunks, len(lists), *...  7.06 us
    ppermute x8, waiting for transfers between devices, level_swap(): return lax.ppermute(array, 'seq', pairs)  5.14 us
    pallas_call x2, Pallas kernels, join(): pl.pallas_call(lambda *refs: join_kernel(size // PLANE, *refs), out_shape...  4.56 us
  transfers between devices with their start and end apart: 32, of which 8 were waited for; matrix products, arithmetic and copies ran while one was open for 2% of the time, Pallas kernels for 46%

profile of v4, /device:TPU:0, one launch (start us, length us, event | category | flops | bytes accessed | tf_op | source)
XLA Modules:
  0.0 90.8 jit_solution(2675964851544988227)
XLA Ops:
  0.6 2.7 %shard_map.103 = (bf16[2,160,256]{2,1,0:T(8,128)(2,1)}, bf16[2,160,256]{2,1,0:T(8,128)(2,1)}, bf16[2,160,256]{2,1,0:T(8,128)(2,1)}, bf16[2,160,256]{2,1,0:T(8,12...) custom-call(bf16[256,1280]{1,0:T(8,128)(2,1)} %refs_0_.3, ...), custom_call_target="tpu_custom_call" | custom-call | flops 3000000000 | bytes 1000000 | tf_op jit(solution)/shard_map/pallas_call | solution.py:369
  3.8 2.6 %collective-permute-start.1 = (bf16[2,160,256]{2,1,0:T(8,128)(2,1)}, bf16[2,160,256]{2,1,0:T(8,128)(2,1)}, u32[]{:S(2)}, u32[]{:S(2)}) collective-permute-start(bf16[2,160,256]{2,1,0:T(8,128)(2,1)} %get-tuple-element.69), channel_id=1, source_target_pairs={{0,2},{1,3},{2,0},{3,1},{4,6},{5,7},{6,4},{7,5},{8,10},{9,11},{10,... | collective-permute-start | bytes 491528 | tf_op jit(solution)/shard_map/ppermute | solution.py:352
  6.7 1.9 %collective-permute-start.12 = (bf16[2,160,256]{2,1,0:T(8,128)(2,1)}, bf16[2,160,256]{2,1,0:T(8,128)(2,1)}, u32[]{:S(2)}, u32[]{:S(2)}) collective-permute-start(bf16[2,160,256]{2,1,0:T(8,128)(2,1)} %get-tuple-element.91), channel_id=1, source_target_pairs={{0,2},{1,3},{2,0},{3,1},{4,6},{5,7},{6,4},{7,5},{8,10},{9,11},{10,... | collective-permute-start | bytes 491528 | tf_op jit(solution)/shard_map/ppermute | solution.py:352
  10.0 4.4 %shard_map.102 = (bf16[2,160,256]{2,1,0:T(8,128)(2,1)}, bf16[2,160,256]{2,1,0:T(8,128)(2,1)}, bf16[2,160,256]{2,1,0:T(8,128)(2,1)}, bf16[2,160,256]{2,1,0:T(8,12...) custom-call(bf16[256,1280]{1,0:T(8,128)(2,1)} %refs_0_.2, ...), custom_call_target="tpu_custom_call" | custom-call | flops 3000000000 | bytes 1000000 | tf_op jit(solution)/shard_map/pallas_call | solution.py:369
  14.8 2.0 %shard_map.104 = (bf16[2,2,160,256]{3,2,1,0:T(8,128)(2,1)}, bf16[2,2,160,256]{3,2,1,0:T(8,128)(2,1)}) custom-call(bf16[2,160,256]{2,1,0:T(8,128)(2,1)} %get-tuple-element.79.refs_0_, bf16[2,160,256]{2,1,0:T(8,128)(2,1)} %collective-permute-done.refs_1_, bf16[2,160,256]{2,1,0:T(8,128)(2,1)} %collective-permute-done.1.refs_2_, ...), custom_call_target="tpu_custom_call" | custom-call | flops 2000000000 | bytes 1000000 | tf_op jit(solution)/shard_map/pallas_call | solution.py:404
  16.8 1.7 %collective-permute-start.6 = (bf16[2,2,160,256]{3,2,1,0:T(8,128)(2,1)}, bf16[2,2,160,256]{3,2,1,0:T(8,128)(2,1)}, u32[]{:S(2)}, u32[]{:S(2)}) collective-permute-start(bf16[2,2,160,256]{3,2,1,0:T(8,128)(2,1)} %get-tuple-element.83), channel_id=1, source_target_pairs={{0,4},{1,5},{2,6},{3,7},{4,0},{5,1},{6,2},{7,3},{8,12},{9,13},{10,... | collective-permute-start | bytes 983048 | tf_op jit(solution)/shard_map/ppermute | solution.py:360
  19.0 1.8 %collective-permute-start.4 = (bf16[2,160,256]{2,1,0:T(8,128)(2,1)}, bf16[2,160,256]{2,1,0:T(8,128)(2,1)}, u32[]{:S(2)}, u32[]{:S(2)}) collective-permute-start(bf16[2,160,256]{2,1,0:T(8,128)(2,1)} %get-tuple-element.73), channel_id=1, source_target_pairs={{0,2},{1,3},{2,0},{3,1},{4,6},{5,7},{6,4},{7,5},{8,10},{9,11},{10,... | collective-permute-start | bytes 491528 | tf_op jit(solution)/shard_map/ppermute | solution.py:352
  21.8 1.7 %collective-permute-start.5 = (bf16[2,160,256]{2,1,0:T(8,128)(2,1)}, bf16[2,160,256]{2,1,0:T(8,128)(2,1)}, u32[]{:S(2)}, u32[]{:S(2)}) collective-permute-start(bf16[2,160,256]{2,1,0:T(8,128)(2,1)} %get-tuple-element.74), channel_id=1, source_target_pairs={{0,3},{1,2},{2,1},{3,0},{4,7},{5,6},{6,5},{7,4},{8,11},{9,10},{10,... | collective-permute-start | bytes 491528 | tf_op jit(solution)/shard_map/ppermute | solution.py:352
  23.5 2.0 %shard_map.106 = (bf16[2,2,160,256]{3,2,1,0:T(8,128)(2,1)}, bf16[2,2,160,256]{3,2,1,0:T(8,128)(2,1)}) custom-call(bf16[2,160,256]{2,1,0:T(8,128)(2,1)} %get-tuple-element.93.refs_0_, bf16[2,160,256]{2,1,0:T(8,128)(2,1)} %collective-permute-done.11.refs_1_, bf16[2,160,256]{2,1,0:T(8,128)(2,1)} %collective-permute-done.12.refs_2_, ...), custom_call_target="tpu_custom_call" | custom-call | flops 2000000000 | bytes 1000000 | tf_op jit(solution)/shard_map/pallas_call | solution.py:404
  26.3 1.7 %collective-permute-start.15 = (bf16[2,160,256]{2,1,0:T(8,128)(2,1)}, bf16[2,160,256]{2,1,0:T(8,128)(2,1)}, u32[]{:S(2)}, u32[]{:S(2)}) collective-permute-start(bf16[2,160,256]{2,1,0:T(8,128)(2,1)} %get-tuple-element.77), channel_id=1, source_target_pairs={{0,2},{1,3},{2,0},{3,1},{4,6},{5,7},{6,4},{7,5},{8,10},{9,11},{10,... | collective-permute-start | bytes 491528 | tf_op jit(solution)/shard_map/ppermute | solution.py:352
  29.1 1.9 %collective-permute-start.16 = (bf16[2,160,256]{2,1,0:T(8,128)(2,1)}, bf16[2,160,256]{2,1,0:T(8,128)(2,1)}, u32[]{:S(2)}, u32[]{:S(2)}) collective-permute-start(bf16[2,160,256]{2,1,0:T(8,128)(2,1)} %get-tuple-element.78), channel_id=1, source_target_pairs={{0,3},{1,2},{2,1},{3,0},{4,7},{5,6},{6,5},{7,4},{8,11},{9,10},{10,... | collective-permute-start | bytes 491528 | tf_op jit(solution)/shard_map/ppermute | solution.py:352
  31.0 2.6 %collective-permute-start.17 = (bf16[2,2,160,256]{3,2,1,0:T(8,128)(2,1)}, bf16[2,2,160,256]{3,2,1,0:T(8,128)(2,1)}, u32[]{:S(2)}, u32[]{:S(2)}) collective-permute-start(bf16[2,2,160,256]{3,2,1,0:T(8,128)(2,1)} %get-tuple-element.97), channel_id=1, source_target_pairs={{0,4},{1,5},{2,6},{3,7},{4,0},{5,1},{6,2},{7,3},{8,12},{9,13},{10,... | collective-permute-start | bytes 983048 | tf_op jit(solution)/shard_map/ppermute | solution.py:360
  33.6 11.7 %shard_map.105 = (bf16[2,2,80,256]{3,2,1,0:T(8,128)(2,1)}, bf16[2,2,80,256]{3,2,1,0:T(8,128)(2,1)}, bf16[2,2,80,256]{3,2,1,0:T(8,128)(2,1)}, bf16[2,2,80,256]{3,...) custom-call(s32[64]{0:T(128)} %get-tuple-element.66.refs_0_, ...), custom_call_target="tpu_custom_call" | custom-call | flops 12000000000 | bytes 1000000 | tf_op jit(solution)/shard_map/pallas_call | solution.py:422
  47.4 1.9 %collective-permute-start.19 = (bf16[2,2,2,80,256]{4,3,2,1,0:T(8,128)(2,1)}, bf16[2,2,2,80,256]{4,3,2,1,0:T(8,128)(2,1)}, u32[]{:S(2)}, u32[]{:S(2)}) collective-permute-start(bf16[2,2,2,80,256]{4,3,2,1,0:T(8,128)(2,1)} %get-tuple-element.103), channel_id=1, source_target_pairs={{0,4},{1,5},{2,6},{3,7},{4,0},{5,1},{6,2},{7,3},{8,12},{9,13},{10,... | collective-permute-start | bytes 983048 | tf_op jit(solution)/shard_map/ppermute | solution.py:360
  49.4 11.7 %shard_map.107 = (bf16[2,2,80,256]{3,2,1,0:T(8,128)(2,1)}, bf16[2,2,80,256]{3,2,1,0:T(8,128)(2,1)}, bf16[2,2,80,256]{3,2,1,0:T(8,128)(2,1)}, bf16[2,2,80,256]{3,...) custom-call(s32[64]{0:T(128)} %get-tuple-element.66.refs_0_, ...), custom_call_target="tpu_custom_call" | custom-call | flops 12000000000 | bytes 1000000 | tf_op jit(solution)/shard_map/pallas_call | solution.py:422
  62.2 2.3 %shard_map.109 = (bf16[2,160,256]{2,1,0:T(8,128)(2,1)}, bf16[2,160,256]{2,1,0:T(8,128)(2,1)}, bf16[2,160,256]{2,1,0:T(8,128)(2,1)}, bf16[2,160,256]{2,1,0:T(8,128)(2,1)}) custom-call(bf16[4,2,160,256]{3,2,1,0:T(8,128)(2,1)} %bitcast.34, bf16[2,2,160,256]{3,2,1,0:T(8,128)(2,1)} %bitcast.29.refs_1_, bf16[2,2,160,256]{3,2,1,0:T(8,128)(2,1)} %bitcast.30.refs_2_), custom_call_target="tpu_custom_call" | custom-call | tf_op jit(solution)/shard_map/pallas_call | solution.py:457
  66.4 5.1 %collective-permute-done.24 = bf16[2,2,2,80,256]{4,3,2,1,0:T(8,128)(2,1)} collective-permute-done((bf16[2,2,2,80,256]{4,3,2,1,0:T(8,128)(2,1)}, bf16[2,2,2,80,256]{4,3,2,1,0:T(8,128)(2,1)}, u32[]{:S(2)}, u32[]{:S(2)}) %collective-permute-start.24) | collective-permute-done | bytes 327712 | tf_op jit(solution)/shard_map/ppermute | solution.py:360
  72.6 2.3 %shard_map.110 = (bf16[2,160,256]{2,1,0:T(8,128)(2,1)}, bf16[2,160,256]{2,1,0:T(8,128)(2,1)}, bf16[2,160,256]{2,1,0:T(8,128)(2,1)}, bf16[2,160,256]{2,1,0:T(8,128)(2,1)}) custom-call(bf16[4,2,160,256]{3,2,1,0:T(8,128)(2,1)} %bitcast.35, bf16[2,2,160,256]{3,2,1,0:T(8,128)(2,1)} %bitcast.32.refs_1_, bf16[2,2,160,256]{3,2,1,0:T(8,128)(2,1)} %bitcast.33.refs_2_), custom_call_target="tpu_custom_call" | custom-call | tf_op jit(solution)/shard_map/pallas_call | solution.py:457
  77.5 2.2 %shard_map.111 = (bf16[256,1280]{1,0:T(8,128)(2,1)}, bf16[256,1280]{1,0:T(8,128)(2,1)}) custom-call(bf16[2,160,256]{2,1,0:T(8,128)(2,1)} %get-tuple-element.113.refs_0_, bf16[2,160,256]{2,1,0:T(8,128)(2,1)} %collective-permute-done.29.refs_1_, bf16[2,160,256]{2,1,0:T(8,128)(2,1)} %collective-permute-done.30.refs_2_, ...), custom_call_target="tpu_custom_call" | custom-call | flops 3000000000 | bytes 1000000 | tf_op jit(solution)/shard_map/pallas_call | solution.py:490
  79.8 1.8 %collective-permute-done.23.refs_7_ = bf16[2,160,256]{2,1,0:T(8,128)(2,1)} collective-permute-done((bf16[2,160,256]{2,1,0:T(8,128)(2,1)}, bf16[2,160,256]{2,1,0:T(8,128)(2,1)}, u32[]{:S(2)}, u32[]{:S(2)}) %collective-permute-start.23) | collective-permute-done | bytes 163872 | tf_op jit(solution)/shard_map/ppermute | solution.py:352
  81.6 2.8 %shard_map.108 = (bf16[256,1280]{1,0:T(8,128)(2,1)}, bf16[256,1280]{1,0:T(8,128)(2,1)}) custom-call(bf16[2,160,256]{2,1,0:T(8,128)(2,1)} %bitcast.43, bf16[2,160,256]{2,1,0:T(8,128)(2,1)} %collective-permute-done.8.refs_1_, bf16[2,160,256]{2,1,0:T(8,128)(2,1)} %collective-permute-done.9.refs_2_, bf16[2,160,256]{2,1,0:T(8,128)(2,1)} %collective-permute-done.10.refs_3_, ...), custom_call_target="tpu_custom_call" | custom-call | flops 3000000000 | bytes 1000000 | tf_op jit(solution)/shard_map/pallas_call | solution.py:490
  84.4 1.6 %collective-permute-done.27.refs_2_ = bf16[2,160,256]{2,1,0:T(8,128)(2,1)} collective-permute-done((bf16[2,160,256]{2,1,0:T(8,128)(2,1)}, bf16[2,160,256]{2,1,0:T(8,128)(2,1)}, u32[]{:S(2)}, u32[]{:S(2)}) %collective-permute-start.27) | collective-permute-done | bytes 163872 | tf_op jit(solution)/shard_map/ppermute | solution.py:352
  86.0 2.6 %collective-permute-done.28.refs_3_ = bf16[2,160,256]{2,1,0:T(8,128)(2,1)} collective-permute-done((bf16[2,160,256]{2,1,0:T(8,128)(2,1)}, bf16[2,160,256]{2,1,0:T(8,128)(2,1)}, u32[]{:S(2)}, u32[]{:S(2)}) %collective-permute-start.28) | collective-permute-done | bytes 163872 | tf_op jit(solution)/shard_map/ppermute | solution.py:352
  88.6 2.2 %shard_map.112 = (bf16[256,1280]{1,0:T(8,128)(2,1)}, bf16[256,1280]{1,0:T(8,128)(2,1)}) custom-call(bf16[2,160,256]{2,1,0:T(8,128)(2,1)} %get-tuple-element.117.refs_0_, bf16[2,160,256]{2,1,0:T(8,128)(2,1)} %collective-permute-done.26.refs_1_, bf16[2,160,256]{2,1,0:T(8,128)(2,1)} %collective-permute-done.27.refs_2_, ...), custom_call_target="tpu_custom_call", output_to_operand_aliasing={{0}: (4, {}), {1}: (5, {})} | custom-call | flops 3000000000 | bytes 1000000 | tf_op jit(solution)/shard_map/pallas_call | solution.py:490
  (57 shorter events, 14.6 us)
Async XLA Ops:
  3.3 11.0 %collective-permute-start = (bf16[2,160,256]{2,1,0:T(8,128)(2,1)}, bf16[2,160,256]{2,1,0:T(8,128)(2,1)}, u32[]{:S(2)}, u32[]{:S(2)}) collective-permute-start(bf16[2,160,256]{2,1,0:T(8,128)(2,1)} %get-tuple-element.68), channel_id=1, source_target_pairs={{0,1},{1,0},{2,3},{3,2},{4,5},{5,4},{6,7},{7,6},{8,9},{9,8},{10,11... | collective-permute-start | bytes 491528 | tf_op jit(solution)/shard_map/ppermute | solution.py:352
  3.8 10.6 %collective-permute-start.1 = (bf16[2,160,256]{2,1,0:T(8,128)(2,1)}, bf16[2,160,256]{2,1,0:T(8,128)(2,1)}, u32[]{:S(2)}, u32[]{:S(2)}) collective-permute-start(bf16[2,160,256]{2,1,0:T(8,128)(2,1)} %get-tuple-element.69), channel_id=1, source_target_pairs={{0,2},{1,3},{2,0},{3,1},{4,6},{5,7},{6,4},{7,5},{8,10},{9,11},{10,... | collective-permute-start | bytes 491528 | tf_op jit(solution)/shard_map/ppermute | solution.py:352
  6.5 12.4 %collective-permute-start.11 = (bf16[2,160,256]{2,1,0:T(8,128)(2,1)}, bf16[2,160,256]{2,1,0:T(8,128)(2,1)}, u32[]{:S(2)}, u32[]{:S(2)}) collective-permute-start(bf16[2,160,256]{2,1,0:T(8,128)(2,1)} %get-tuple-element.90), channel_id=1, source_target_pairs={{0,1},{1,0},{2,3},{3,2},{4,5},{5,4},{6,7},{7,6},{8,9},{9,8},{10,11... | collective-permute-start | bytes 491528 | tf_op jit(solution)/shard_map/ppermute | solution.py:352
  6.7 12.4 %collective-permute-start.12 = (bf16[2,160,256]{2,1,0:T(8,128)(2,1)}, bf16[2,160,256]{2,1,0:T(8,128)(2,1)}, u32[]{:S(2)}, u32[]{:S(2)}) collective-permute-start(bf16[2,160,256]{2,1,0:T(8,128)(2,1)} %get-tuple-element.91), channel_id=1, source_target_pairs={{0,2},{1,3},{2,0},{3,1},{4,6},{5,7},{6,4},{7,5},{8,10},{9,11},{10,... | collective-permute-start | bytes 491528 | tf_op jit(solution)/shard_map/ppermute | solution.py:352
  16.8 14.2 %collective-permute-start.6 = (bf16[2,2,160,256]{3,2,1,0:T(8,128)(2,1)}, bf16[2,2,160,256]{3,2,1,0:T(8,128)(2,1)}, u32[]{:S(2)}, u32[]{:S(2)}) collective-permute-start(bf16[2,2,160,256]{3,2,1,0:T(8,128)(2,1)} %get-tuple-element.83), channel_id=1, source_target_pairs={{0,4},{1,5},{2,6},{3,7},{4,0},{5,1},{6,2},{7,3},{8,12},{9,13},{10,... | collective-permute-start | bytes 983048 | tf_op jit(solution)/shard_map/ppermute | solution.py:360
  18.5 15.1 %collective-permute-start.7 = (bf16[2,2,160,256]{3,2,1,0:T(8,128)(2,1)}, bf16[2,2,160,256]{3,2,1,0:T(8,128)(2,1)}, u32[]{:S(2)}, u32[]{:S(2)}) collective-permute-start(bf16[2,2,160,256]{3,2,1,0:T(8,128)(2,1)} %get-tuple-element.84), channel_id=1, source_target_pairs={{0,1},{1,0},{2,3},{3,2},{4,8},{5,9},{6,10},{7,11},{8,4},{9,5},{10,... | collective-permute-start | bytes 983048 | tf_op jit(solution)/shard_map/ppermute | solution.py:360
  25.6 19.7 %collective-permute-start.14 = (bf16[2,160,256]{2,1,0:T(8,128)(2,1)}, bf16[2,160,256]{2,1,0:T(8,128)(2,1)}, u32[]{:S(2)}, u32[]{:S(2)}) collective-permute-start(bf16[2,160,256]{2,1,0:T(8,128)(2,1)} %get-tuple-element.76), channel_id=1, source_target_pairs={{0,1},{1,0},{2,3},{3,2},{4,5},{5,4},{6,7},{7,6},{8,9},{9,8},{10,11... | collective-permute-start | bytes 491528 | tf_op jit(solution)/shard_map/ppermute | solution.py:352
  26.3 19.6 %collective-permute-start.15 = (bf16[2,160,256]{2,1,0:T(8,128)(2,1)}, bf16[2,160,256]{2,1,0:T(8,128)(2,1)}, u32[]{:S(2)}, u32[]{:S(2)}) collective-permute-start(bf16[2,160,256]{2,1,0:T(8,128)(2,1)} %get-tuple-element.77), channel_id=1, source_target_pairs={{0,2},{1,3},{2,0},{3,1},{4,6},{5,7},{6,4},{7,5},{8,10},{9,11},{10,... | collective-permute-start | bytes 491528 | tf_op jit(solution)/shard_map/ppermute | solution.py:352
  29.1 17.4 %collective-permute-start.16 = (bf16[2,160,256]{2,1,0:T(8,128)(2,1)}, bf16[2,160,256]{2,1,0:T(8,128)(2,1)}, u32[]{:S(2)}, u32[]{:S(2)}) collective-permute-start(bf16[2,160,256]{2,1,0:T(8,128)(2,1)} %get-tuple-element.78), channel_id=1, source_target_pairs={{0,3},{1,2},{2,1},{3,0},{4,7},{5,6},{6,5},{7,4},{8,11},{9,10},{10,... | collective-permute-start | bytes 491528 | tf_op jit(solution)/shard_map/ppermute | solution.py:352
  31.0 16.4 %collective-permute-start.17 = (bf16[2,2,160,256]{3,2,1,0:T(8,128)(2,1)}, bf16[2,2,160,256]{3,2,1,0:T(8,128)(2,1)}, u32[]{:S(2)}, u32[]{:S(2)}) collective-permute-start(bf16[2,2,160,256]{3,2,1,0:T(8,128)(2,1)} %get-tuple-element.97), channel_id=1, source_target_pairs={{0,4},{1,5},{2,6},{3,7},{4,0},{5,1},{6,2},{7,3},{8,12},{9,13},{10,... | collective-permute-start | bytes 983048 | tf_op jit(solution)/shard_map/ppermute | solution.py:360
  33.6 15.7 %collective-permute-start.18 = (bf16[2,2,160,256]{3,2,1,0:T(8,128)(2,1)}, bf16[2,2,160,256]{3,2,1,0:T(8,128)(2,1)}, u32[]{:S(2)}, u32[]{:S(2)}) collective-permute-start(bf16[2,2,160,256]{3,2,1,0:T(8,128)(2,1)} %get-tuple-element.98), channel_id=1, source_target_pairs={{0,1},{1,0},{2,3},{3,2},{4,8},{5,9},{6,10},{7,11},{8,4},{9,5},{10,... | collective-permute-start | bytes 983048 | tf_op jit(solution)/shard_map/ppermute | solution.py:360
  45.4 15.8 %collective-permute-start.8 = (bf16[2,160,256]{2,1,0:T(8,128)(2,1)}, bf16[2,160,256]{2,1,0:T(8,128)(2,1)}, u32[]{:S(2)}, u32[]{:S(2)}) collective-permute-start(bf16[2,160,256]{2,1,0:T(8,128)(2,1)} %bitcast.40), channel_id=1, source_target_pairs={{0,1},{1,0},{2,3},{3,2},{4,5},{5,4},{6,7},{7,6},{8,9},{9,8},{10,11... | collective-permute-start | bytes 491528 | tf_op jit(solution)/shard_map/ppermute | solution.py:352
  45.9 15.7 %collective-permute-start.9 = (bf16[2,160,256]{2,1,0:T(8,128)(2,1)}, bf16[2,160,256]{2,1,0:T(8,128)(2,1)}, u32[]{:S(2)}, u32[]{:S(2)}) collective-permute-start(bf16[2,160,256]{2,1,0:T(8,128)(2,1)} %bitcast.39), channel_id=1, source_target_pairs={{0,2},{1,3},{2,0},{3,1},{4,6},{5,7},{6,4},{7,5},{8,10},{9,11},{10,... | collective-permute-start | bytes 491528 | tf_op jit(solution)/shard_map/ppermute | solution.py:352
  46.5 15.3 %collective-permute-start.10 = (bf16[2,160,256]{2,1,0:T(8,128)(2,1)}, bf16[2,160,256]{2,1,0:T(8,128)(2,1)}, u32[]{:S(2)}, u32[]{:S(2)}) collective-permute-start(bf16[2,160,256]{2,1,0:T(8,128)(2,1)} %bitcast.38), channel_id=1, source_target_pairs={{0,3},{1,2},{2,1},{3,0},{4,7},{5,6},{6,5},{7,4},{8,11},{9,10},{10,... | collective-permute-start | bytes 491528 | tf_op jit(solution)/shard_map/ppermute | solution.py:352
  47.4 14.3 %collective-permute-start.19 = (bf16[2,2,2,80,256]{4,3,2,1,0:T(8,128)(2,1)}, bf16[2,2,2,80,256]{4,3,2,1,0:T(8,128)(2,1)}, u32[]{:S(2)}, u32[]{:S(2)}) collective-permute-start(bf16[2,2,2,80,256]{4,3,2,1,0:T(8,128)(2,1)} %get-tuple-element.103), channel_id=1, source_target_pairs={{0,4},{1,5},{2,6},{3,7},{4,0},{5,1},{6,2},{7,3},{8,12},{9,13},{10,... | collective-permute-start | bytes 983048 | tf_op jit(solution)/shard_map/ppermute | solution.py:360
  49.3 12.4 %collective-permute-start.20 = (bf16[2,2,2,80,256]{4,3,2,1,0:T(8,128)(2,1)}, bf16[2,2,2,80,256]{4,3,2,1,0:T(8,128)(2,1)}, u32[]{:S(2)}, u32[]{:S(2)}) collective-permute-start(bf16[2,2,2,80,256]{4,3,2,1,0:T(8,128)(2,1)} %get-tuple-element.104), channel_id=1, source_target_pairs={{0,1},{1,0},{2,3},{3,2},{4,8},{5,9},{6,10},{7,11},{8,4},{9,5},{10,... | collective-permute-start | bytes 983048 | tf_op jit(solution)/shard_map/ppermute | solution.py:360
  61.1 10.4 %collective-permute-start.24 = (bf16[2,2,2,80,256]{4,3,2,1,0:T(8,128)(2,1)}, bf16[2,2,2,80,256]{4,3,2,1,0:T(8,128)(2,1)}, u32[]{:S(2)}, u32[]{:S(2)}) collective-permute-start(bf16[2,2,2,80,256]{4,3,2,1,0:T(8,128)(2,1)} %get-tuple-element.115), channel_id=1, source_target_pairs={{0,4},{1,5},{2,6},{3,7},{4,0},{5,1},{6,2},{7,3},{8,12},{9,13},{10,... | collective-permute-start | bytes 983048 | tf_op jit(solution)/shard_map/ppermute | solution.py:360
  61.6 10.3 %collective-permute-start.25 = (bf16[2,2,2,80,256]{4,3,2,1,0:T(8,128)(2,1)}, bf16[2,2,2,80,256]{4,3,2,1,0:T(8,128)(2,1)}, u32[]{:S(2)}, u32[]{:S(2)}) collective-permute-start(bf16[2,2,2,80,256]{4,3,2,1,0:T(8,128)(2,1)} %get-tuple-element.116), channel_id=1, source_target_pairs={{0,1},{1,0},{2,3},{3,2},{4,8},{5,9},{6,10},{7,11},{8,4},{9,5},{10,... | collective-permute-start | bytes 983048 | tf_op jit(solution)/shard_map/ppermute | solution.py:360
  64.5 10.4 %collective-permute-start.29 = (bf16[2,160,256]{2,1,0:T(8,128)(2,1)}, bf16[2,160,256]{2,1,0:T(8,128)(2,1)}, u32[]{:S(2)}, u32[]{:S(2)}) collective-permute-start(bf16[2,160,256]{2,1,0:T(8,128)(2,1)} %get-tuple-element.121), channel_id=1, source_target_pairs={{0,1},{1,0},{2,3},{3,2},{4,5},{5,4},{6,7},{7,6},{8,9},{9,8},{10,11... | collective-permute-start | bytes 491528 | tf_op jit(solution)/shard_map/ppermute | solution.py:352
  64.6 11.5 %collective-permute-start.30 = (bf16[2,160,256]{2,1,0:T(8,128)(2,1)}, bf16[2,160,256]{2,1,0:T(8,128)(2,1)}, u32[]{:S(2)}, u32[]{:S(2)}) collective-permute-start(bf16[2,160,256]{2,1,0:T(8,128)(2,1)} %get-tuple-element.122), channel_id=1, source_target_pairs={{0,2},{1,3},{2,0},{3,1},{4,6},{5,7},{6,4},{7,5},{8,10},{9,11},{10,... | collective-permute-start | bytes 491528 | tf_op jit(solution)/shard_map/ppermute | solution.py:352
  65.3 11.1 %collective-permute-start.31 = (bf16[2,160,256]{2,1,0:T(8,128)(2,1)}, bf16[2,160,256]{2,1,0:T(8,128)(2,1)}, u32[]{:S(2)}, u32[]{:S(2)}) collective-permute-start(bf16[2,160,256]{2,1,0:T(8,128)(2,1)} %get-tuple-element.123), channel_id=1, source_target_pairs={{0,3},{1,2},{2,1},{3,0},{4,7},{5,6},{6,5},{7,4},{8,11},{9,10},{10,... | collective-permute-start | bytes 491528 | tf_op jit(solution)/shard_map/ppermute | solution.py:352
  71.9 9.7 %collective-permute-start.23 = (bf16[2,160,256]{2,1,0:T(8,128)(2,1)}, bf16[2,160,256]{2,1,0:T(8,128)(2,1)}, u32[]{:S(2)}, u32[]{:S(2)}) collective-permute-start(bf16[2,160,256]{2,1,0:T(8,128)(2,1)} %bitcast.36), channel_id=1, source_target_pairs={{0,3},{1,2},{2,1},{3,0},{4,7},{5,6},{6,5},{7,4},{8,11},{9,10},{10,... | collective-permute-start | bytes 491528 | tf_op jit(solution)/shard_map/ppermute | solution.py:352
  76.1 9.9 %collective-permute-start.27 = (bf16[2,160,256]{2,1,0:T(8,128)(2,1)}, bf16[2,160,256]{2,1,0:T(8,128)(2,1)}, u32[]{:S(2)}, u32[]{:S(2)}) collective-permute-start(bf16[2,160,256]{2,1,0:T(8,128)(2,1)} %get-tuple-element.119), channel_id=1, source_target_pairs={{0,2},{1,3},{2,0},{3,1},{4,6},{5,7},{6,4},{7,5},{8,10},{9,11},{10,... | collective-permute-start | bytes 491528 | tf_op jit(solution)/shard_map/ppermute | solution.py:352
  76.5 12.2 %collective-permute-start.28 = (bf16[2,160,256]{2,1,0:T(8,128)(2,1)}, bf16[2,160,256]{2,1,0:T(8,128)(2,1)}, u32[]{:S(2)}, u32[]{:S(2)}) collective-permute-start(bf16[2,160,256]{2,1,0:T(8,128)(2,1)} %get-tuple-element.120), channel_id=1, source_target_pairs={{0,3},{1,2},{2,1},{3,0},{4,7},{5,6},{6,5},{7,4},{8,11},{9,10},{10,... | collective-permute-start | bytes 491528 | tf_op jit(solution)/shard_map/ppermute | solution.py:352
  (10 other events, 63.1 us)

commit v5 on v4

--- a/solution.py
+++ b/solution.py
@@ -27,12 +27,14 @@
 
 
 def after(arrays, others):
+    if not others:
+        return list(arrays)
     return list(lax.optimization_barrier((list(arrays), list(others)))[0])
 
 
 def cost(microseconds):
     return pl.CostEstimate(
-        flops=microseconds * 1_000_000_000, bytes_accessed=1_000_000, transcendentals=0
+        flops=int(microseconds * 1_000_000_000), bytes_accessed=1_000_000, transcendentals=0
     )
 
 
@@ -383,7 +385,8 @@
         )(first, second, *lists)
 
     def spread(parts):
-        return [parts[0]] + [swap(parts[hop], hop) for hop in range(1, PLANE)]
+        moved = {hop: swap(parts[hop], hop) for hop in (1, 2, 3)}
+        return [parts[0]] + [moved[hop] for hop in range(1, PLANE)]
 
     rounds = len(CHUNKS)
     every = tuple(range(rounds))
@@ -399,7 +402,7 @@
     query_held = [spread(query_ready[PLANE * chunk : PLANE * (chunk + 1)]) for chunk in every]
     for chunk, heads in enumerate(CHUNKS):
         held = key_held[chunk]
-        held = after(held, query_ready)
+        held = after(held, query_ready if chunk else query_ready)
         pair = jax.ShapeDtypeStruct((2, 2, heads * head_size, tokens), BF16)
         even, odd = pl.pallas_call(
             pack_kernel,
@@ -443,7 +446,7 @@
                 pltpu.SemaphoreType.DMA((2 * PLANE + 2,)),
             ],
             compiler_params=params(),
-            cost_estimate=cost(6 * heads),
+            cost_estimate=cost(1 * heads),
         )(
             limits,
             *[part.reshape((2,) + shape) for part in key_held[chunk] + query_held[chunk]],
@@ -481,8 +484,9 @@
     for chunk in range(rounds):
         local = results[chunk][PLANE]
         if chunk == rounds - 1:
-            local = after([local], last[1:2] + [back[0]])[0]
+            local = after([local], last[2:3] + [back[0]])[0]
         back = join(chunk, local, *returned[chunk])
+        back = after(back, [] if chunk else [])
         key_pieces += spread(back)
 
     def finish(parts, chunks, held=()):

time: 91.4 us -> 88.6 us (0.969)
  waiting for transfers between devices: 14.3 us -> 12 us
    ppermute x8, waiting for transfers between devices: 5.14 us -> 1.35 us  [level_swap(): return lax.ppermute(array, 'seq', pairs)]
    ppermute x24, starting transfers between devices: 20.7 us -> 18.8 us  [swap(): return lax.ppermute(array, 'seq', pairs)]
    ppermute x24, waiting for transfers between devices: 9.12 us -> 10.6 us  [swap(): return lax.ppermute(array, 'seq', pairs)]
    ppermute x8, starting transfers between devices: 7.34 us -> 8.66 us  [level_swap(): return lax.ppermute(array, 'seq', pairs)]
  transfers between devices with their start and end apart: 32 -> 32, of which waited for: 8 -> 9; matrix products, arithmetic and copies ran while one was open for 2% -> 2% of each run, Pallas kernels for 46% -> 47%
where the time goes in v5:
time: 88.6 us; the launch traced here: 88 us
  Pallas kernels  46.4 us (52%)
  starting transfers between devices  27.4 us (31%)
  waiting for transfers between devices  12 us (14%)
  local copies, waits for them, and re-layouts  1.38 us (2%)
    pallas_call x2, Pallas kernels, main(): pl.pallas_call(lambda *refs: main_kernel(head_size, heads, *refs), out_sh...  23.5 us
    ppermute x24, starting transfers between devices, swap(): return lax.ppermute(array, 'seq', pairs)  18.8 us
    ppermute x24, waiting for transfers between devices, swap(): return lax.ppermute(array, 'seq', pairs)  10.6 us
    ppermute x8, starting transfers between devices, level_swap(): return lax.ppermute(array, 'seq', pairs)  8.66 us
    pallas_call x3, Pallas kernels, finish(): pl.pallas_call(lambda *refs: finish_kernel(head_size, chunks, len(held),...  7.22 us
    pallas_call x2, Pallas kernels, prep(): pl.pallas_call(lambda *refs: prep_kernel(head_size, chunks, len(lists), *...  7.04 us
    pallas_call x2, Pallas kernels, join(): pl.pallas_call(lambda *refs: join_kernel(size // PLANE, *refs), out_shape...  4.56 us
    pallas_call x2, Pallas kernels, body(): pl.pallas_call(pack_kernel, out_shape=[pair, pair], in_specs=[HBM] * PLAN...  4.06 us
  transfers between devices with their start and end apart: 32, of which 9 were waited for; matrix products, arithmetic and copies ran while one was open for 2% of the time, Pallas kernels for 47%

profile of v5, /device:TPU:0, one launch (start us, length us, event | category | flops | bytes accessed | tf_op | source)
XLA Modules:
  0.0 88.0 jit_solution(18086831931092659095)
XLA Ops:
  0.6 2.7 %shard_map.103 = (bf16[2,160,256]{2,1,0:T(8,128)(2,1)}, bf16[2,160,256]{2,1,0:T(8,128)(2,1)}, bf16[2,160,256]{2,1,0:T(8,128)(2,1)}, bf16[2,160,256]{2,1,0:T(8,12...) custom-call(bf16[256,1280]{1,0:T(8,128)(2,1)} %refs_0_.3, ...), custom_call_target="tpu_custom_call" | custom-call | flops 3000000000 | bytes 1000000 | tf_op jit(solution)/shard_map/pallas_call | solution.py:371
  3.8 2.6 %collective-permute-start.1 = (bf16[2,160,256]{2,1,0:T(8,128)(2,1)}, bf16[2,160,256]{2,1,0:T(8,128)(2,1)}, u32[]{:S(2)}, u32[]{:S(2)}) collective-permute-start(bf16[2,160,256]{2,1,0:T(8,128)(2,1)} %get-tuple-element.69), channel_id=1, source_target_pairs={{0,2},{1,3},{2,0},{3,1},{4,6},{5,7},{6,4},{7,5},{8,10},{9,11},{10,... | collective-permute-start | bytes 491528 | tf_op jit(solution)/shard_map/ppermute | solution.py:354
  6.6 1.9 %collective-permute-start.12 = (bf16[2,160,256]{2,1,0:T(8,128)(2,1)}, bf16[2,160,256]{2,1,0:T(8,128)(2,1)}, u32[]{:S(2)}, u32[]{:S(2)}) collective-permute-start(bf16[2,160,256]{2,1,0:T(8,128)(2,1)} %get-tuple-element.91), channel_id=1, source_target_pairs={{0,2},{1,3},{2,0},{3,1},{4,6},{5,7},{6,4},{7,5},{8,10},{9,11},{10,... | collective-permute-start | bytes 491528 | tf_op jit(solution)/shard_map/ppermute | solution.py:354
  9.9 4.4 %shard_map.102 = (bf16[2,160,256]{2,1,0:T(8,128)(2,1)}, bf16[2,160,256]{2,1,0:T(8,128)(2,1)}, bf16[2,160,256]{2,1,0:T(8,128)(2,1)}, bf16[2,160,256]{2,1,0:T(8,12...) custom-call(bf16[256,1280]{1,0:T(8,128)(2,1)} %refs_0_.2, ...), custom_call_target="tpu_custom_call" | custom-call | flops 3000000000 | bytes 1000000 | tf_op jit(solution)/shard_map/pallas_call | solution.py:371
  14.8 2.0 %shard_map.104 = (bf16[2,2,160,256]{3,2,1,0:T(8,128)(2,1)}, bf16[2,2,160,256]{3,2,1,0:T(8,128)(2,1)}) custom-call(bf16[2,160,256]{2,1,0:T(8,128)(2,1)} %get-tuple-element.79.refs_0_, bf16[2,160,256]{2,1,0:T(8,128)(2,1)} %collective-permute-done.refs_1_, bf16[2,160,256]{2,1,0:T(8,128)(2,1)} %collective-permute-done.1.refs_2_, ...), custom_call_target="tpu_custom_call" | custom-call | flops 2000000000 | bytes 1000000 | tf_op jit(solution)/shard_map/pallas_call | solution.py:407
  16.8 1.7 %collective-permute-start.6 = (bf16[2,2,160,256]{3,2,1,0:T(8,128)(2,1)}, bf16[2,2,160,256]{3,2,1,0:T(8,128)(2,1)}, u32[]{:S(2)}, u32[]{:S(2)}) collective-permute-start(bf16[2,2,160,256]{3,2,1,0:T(8,128)(2,1)} %get-tuple-element.83), channel_id=1, source_target_pairs={{0,4},{1,5},{2,6},{3,7},{4,0},{5,1},{6,2},{7,3},{8,12},{9,13},{10,... | collective-permute-start | bytes 983048 | tf_op jit(solution)/shard_map/ppermute | solution.py:362
  19.0 1.8 %collective-permute-start.4 = (bf16[2,160,256]{2,1,0:T(8,128)(2,1)}, bf16[2,160,256]{2,1,0:T(8,128)(2,1)}, u32[]{:S(2)}, u32[]{:S(2)}) collective-permute-start(bf16[2,160,256]{2,1,0:T(8,128)(2,1)} %get-tuple-element.73), channel_id=1, source_target_pairs={{0,2},{1,3},{2,0},{3,1},{4,6},{5,7},{6,4},{7,5},{8,10},{9,11},{10,... | collective-permute-start | bytes 491528 | tf_op jit(solution)/shard_map/ppermute | solution.py:354
  21.8 1.7 %collective-permute-start.5 = (bf16[2,160,256]{2,1,0:T(8,128)(2,1)}, bf16[2,160,256]{2,1,0:T(8,128)(2,1)}, u32[]{:S(2)}, u32[]{:S(2)}) collective-permute-start(bf16[2,160,256]{2,1,0:T(8,128)(2,1)} %get-tuple-element.74), channel_id=1, source_target_pairs={{0,3},{1,2},{2,1},{3,0},{4,7},{5,6},{6,5},{7,4},{8,11},{9,10},{10,... | collective-permute-start | bytes 491528 | tf_op jit(solution)/shard_map/ppermute | solution.py:354
  23.5 2.0 %shard_map.106 = (bf16[2,2,160,256]{3,2,1,0:T(8,128)(2,1)}, bf16[2,2,160,256]{3,2,1,0:T(8,128)(2,1)}) custom-call(bf16[2,160,256]{2,1,0:T(8,128)(2,1)} %get-tuple-element.93.refs_0_, bf16[2,160,256]{2,1,0:T(8,128)(2,1)} %collective-permute-done.11.refs_1_, bf16[2,160,256]{2,1,0:T(8,128)(2,1)} %collective-permute-done.12.refs_2_, ...), custom_call_target="tpu_custom_call" | custom-call | flops 2000000000 | bytes 1000000 | tf_op jit(solution)/shard_map/pallas_call | solution.py:407
  25.6 1.6 %collective-permute-start.17 = (bf16[2,2,160,256]{3,2,1,0:T(8,128)(2,1)}, bf16[2,2,160,256]{3,2,1,0:T(8,128)(2,1)}, u32[]{:S(2)}, u32[]{:S(2)}) collective-permute-start(bf16[2,2,160,256]{3,2,1,0:T(8,128)(2,1)} %get-tuple-element.97), channel_id=1, source_target_pairs={{0,4},{1,5},{2,6},{3,7},{4,0},{5,1},{6,2},{7,3},{8,12},{9,13},{10,... | collective-permute-start | bytes 983048 | tf_op jit(solution)/shard_map/ppermute | solution.py:362
  27.3 1.7 %collective-permute-done.5 = bf16[2,160,256]{2,1,0:T(8,128)(2,1)} collective-permute-done((bf16[2,160,256]{2,1,0:T(8,128)(2,1)}, bf16[2,160,256]{2,1,0:T(8,128)(2,1)}, u32[]{:S(2)}, u32[]{:S(2)}) %collective-permute-start.5) | collective-permute-done | bytes 163872 | tf_op jit(solution)/shard_map/ppermute | solution.py:354
  29.2 1.8 %collective-permute-start.15 = (bf16[2,160,256]{2,1,0:T(8,128)(2,1)}, bf16[2,160,256]{2,1,0:T(8,128)(2,1)}, u32[]{:S(2)}, u32[]{:S(2)}) collective-permute-start(bf16[2,160,256]{2,1,0:T(8,128)(2,1)} %get-tuple-element.77), channel_id=1, source_target_pairs={{0,2},{1,3},{2,0},{3,1},{4,6},{5,7},{6,4},{7,5},{8,10},{9,11},{10,... | collective-permute-start | bytes 491528 | tf_op jit(solution)/shard_map/ppermute | solution.py:354
  31.0 11.7 %shard_map.105 = (bf16[2,2,80,256]{3,2,1,0:T(8,128)(2,1)}, bf16[2,2,80,256]{3,2,1,0:T(8,128)(2,1)}, bf16[2,2,80,256]{3,2,1,0:T(8,128)(2,1)}, bf16[2,2,80,256]{3,...) custom-call(s32[64]{0:T(128)} %get-tuple-element.66.refs_0_, ...), custom_call_target="tpu_custom_call" | custom-call | flops 2000000000 | bytes 1000000 | tf_op jit(solution)/shard_map/pallas_call | solution.py:425
  42.8 2.8 %collective-permute-start.19 = (bf16[2,2,2,80,256]{4,3,2,1,0:T(8,128)(2,1)}, bf16[2,2,2,80,256]{4,3,2,1,0:T(8,128)(2,1)}, u32[]{:S(2)}, u32[]{:S(2)}) collective-permute-start(bf16[2,2,2,80,256]{4,3,2,1,0:T(8,128)(2,1)} %get-tuple-element.103), channel_id=1, source_target_pairs={{0,4},{1,5},{2,6},{3,7},{4,0},{5,1},{6,2},{7,3},{8,12},{9,13},{10,... | collective-permute-start | bytes 983048 | tf_op jit(solution)/shard_map/ppermute | solution.py:362
  47.8 11.8 %shard_map.107 = (bf16[2,2,80,256]{3,2,1,0:T(8,128)(2,1)}, bf16[2,2,80,256]{3,2,1,0:T(8,128)(2,1)}, bf16[2,2,80,256]{3,2,1,0:T(8,128)(2,1)}, bf16[2,2,80,256]{3,...) custom-call(s32[64]{0:T(128)} %get-tuple-element.66.refs_0_, ...), custom_call_target="tpu_custom_call" | custom-call | flops 2000000000 | bytes 1000000 | tf_op jit(solution)/shard_map/pallas_call | solution.py:425
  59.5 1.7 %collective-permute-start.24 = (bf16[2,2,2,80,256]{4,3,2,1,0:T(8,128)(2,1)}, bf16[2,2,2,80,256]{4,3,2,1,0:T(8,128)(2,1)}, u32[]{:S(2)}, u32[]{:S(2)}) collective-permute-start(bf16[2,2,2,80,256]{4,3,2,1,0:T(8,128)(2,1)} %get-tuple-element.115), channel_id=1, source_target_pairs={{0,4},{1,5},{2,6},{3,7},{4,0},{5,1},{6,2},{7,3},{8,12},{9,13},{10,... | collective-permute-start | bytes 983048 | tf_op jit(solution)/shard_map/ppermute | solution.py:362
  62.9 2.3 %shard_map.109 = (bf16[2,160,256]{2,1,0:T(8,128)(2,1)}, bf16[2,160,256]{2,1,0:T(8,128)(2,1)}, bf16[2,160,256]{2,1,0:T(8,128)(2,1)}, bf16[2,160,256]{2,1,0:T(8,128)(2,1)}) custom-call(bf16[4,2,160,256]{3,2,1,0:T(8,128)(2,1)} %bitcast.34, bf16[2,2,160,256]{3,2,1,0:T(8,128)(2,1)} %bitcast.29.refs_1_, bf16[2,2,160,256]{3,2,1,0:T(8,128)(2,1)} %bitcast.30.refs_2_), custom_call_target="tpu_custom_call" | custom-call | tf_op jit(solution)/shard_map/pallas_call | solution.py:460
  65.9 2.3 %collective-permute-done.22.refs_6_ = bf16[2,160,256]{2,1,0:T(8,128)(2,1)} collective-permute-done((bf16[2,160,256]{2,1,0:T(8,128)(2,1)}, bf16[2,160,256]{2,1,0:T(8,128)(2,1)}, u32[]{:S(2)}, u32[]{:S(2)}) %collective-permute-start.22) | collective-permute-done | bytes 163872 | tf_op jit(solution)/shard_map/ppermute | solution.py:354
  71.5 2.3 %shard_map.110 = (bf16[2,160,256]{2,1,0:T(8,128)(2,1)}, bf16[2,160,256]{2,1,0:T(8,128)(2,1)}, bf16[2,160,256]{2,1,0:T(8,128)(2,1)}, bf16[2,160,256]{2,1,0:T(8,128)(2,1)}) custom-call(bf16[4,2,160,256]{3,2,1,0:T(8,128)(2,1)} %bitcast.35, bf16[2,2,160,256]{3,2,1,0:T(8,128)(2,1)} %bitcast.32.refs_1_, bf16[2,2,160,256]{3,2,1,0:T(8,128)(2,1)} %bitcast.33.refs_2_), custom_call_target="tpu_custom_call" | custom-call | tf_op jit(solution)/shard_map/pallas_call | solution.py:460
  76.1 2.2 %shard_map.111 = (bf16[256,1280]{1,0:T(8,128)(2,1)}, bf16[256,1280]{1,0:T(8,128)(2,1)}) custom-call(bf16[2,160,256]{2,1,0:T(8,128)(2,1)} %get-tuple-element.113.refs_0_, bf16[2,160,256]{2,1,0:T(8,128)(2,1)} %collective-permute-done.29.refs_1_, bf16[2,160,256]{2,1,0:T(8,128)(2,1)} %collective-permute-done.30.refs_2_, ...), custom_call_target="tpu_custom_call" | custom-call | flops 3000000000 | bytes 1000000 | tf_op jit(solution)/shard_map/pallas_call | solution.py:494
  78.7 2.8 %shard_map.108 = (bf16[256,1280]{1,0:T(8,128)(2,1)}, bf16[256,1280]{1,0:T(8,128)(2,1)}) custom-call(bf16[2,160,256]{2,1,0:T(8,128)(2,1)} %bitcast.43, bf16[2,160,256]{2,1,0:T(8,128)(2,1)} %collective-permute-done.8.refs_1_, bf16[2,160,256]{2,1,0:T(8,128)(2,1)} %collective-permute-done.9.refs_2_, bf16[2,160,256]{2,1,0:T(8,128)(2,1)} %collective-permute-done.10.refs_3_, ...), custom_call_target="tpu_custom_call" | custom-call | flops 3000000000 | bytes 1000000 | tf_op jit(solution)/shard_map/pallas_call | solution.py:494
  81.6 1.6 %collective-permute-done.27.refs_2_ = bf16[2,160,256]{2,1,0:T(8,128)(2,1)} collective-permute-done((bf16[2,160,256]{2,1,0:T(8,128)(2,1)}, bf16[2,160,256]{2,1,0:T(8,128)(2,1)}, u32[]{:S(2)}, u32[]{:S(2)}) %collective-permute-start.27) | collective-permute-done | bytes 163872 | tf_op jit(solution)/shard_map/ppermute | solution.py:354
  83.2 2.6 %collective-permute-done.28.refs_3_ = bf16[2,160,256]{2,1,0:T(8,128)(2,1)} collective-permute-done((bf16[2,160,256]{2,1,0:T(8,128)(2,1)}, bf16[2,160,256]{2,1,0:T(8,128)(2,1)}, u32[]{:S(2)}, u32[]{:S(2)}) %collective-permute-start.28) | collective-permute-done | bytes 163872 | tf_op jit(solution)/shard_map/ppermute | solution.py:354
  85.8 2.2 %shard_map.112 = (bf16[256,1280]{1,0:T(8,128)(2,1)}, bf16[256,1280]{1,0:T(8,128)(2,1)}) custom-call(bf16[2,160,256]{2,1,0:T(8,128)(2,1)} %get-tuple-element.117.refs_0_, bf16[2,160,256]{2,1,0:T(8,128)(2,1)} %collective-permute-done.26.refs_1_, bf16[2,160,256]{2,1,0:T(8,128)(2,1)} %collective-permute-done.27.refs_2_, ...), custom_call_target="tpu_custom_call", output_to_operand_aliasing={{0}: (4, {}), {1}: (5, {})} | custom-call | flops 3000000000 | bytes 1000000 | tf_op jit(solution)/shard_map/pallas_call | solution.py:494
  (57 shorter events, 14.9 us)
Async XLA Ops:
  3.3 11.0 %collective-permute-start = (bf16[2,160,256]{2,1,0:T(8,128)(2,1)}, bf16[2,160,256]{2,1,0:T(8,128)(2,1)}, u32[]{:S(2)}, u32[]{:S(2)}) collective-permute-start(bf16[2,160,256]{2,1,0:T(8,128)(2,1)} %get-tuple-element.68), channel_id=1, source_target_pairs={{0,1},{1,0},{2,3},{3,2},{4,5},{5,4},{6,7},{7,6},{8,9},{9,8},{10,11... | collective-permute-start | bytes 491528 | tf_op jit(solution)/shard_map/ppermute | solution.py:354
  3.8 10.6 %collective-permute-start.1 = (bf16[2,160,256]{2,1,0:T(8,128)(2,1)}, bf16[2,160,256]{2,1,0:T(8,128)(2,1)}, u32[]{:S(2)}, u32[]{:S(2)}) collective-permute-start(bf16[2,160,256]{2,1,0:T(8,128)(2,1)} %get-tuple-element.69), channel_id=1, source_target_pairs={{0,2},{1,3},{2,0},{3,1},{4,6},{5,7},{6,4},{7,5},{8,10},{9,11},{10,... | collective-permute-start | bytes 491528 | tf_op jit(solution)/shard_map/ppermute | solution.py:354
  6.4 8.3 %collective-permute-start.2 = (bf16[2,160,256]{2,1,0:T(8,128)(2,1)}, bf16[2,160,256]{2,1,0:T(8,128)(2,1)}, u32[]{:S(2)}, u32[]{:S(2)}) collective-permute-start(bf16[2,160,256]{2,1,0:T(8,128)(2,1)} %get-tuple-element.70), channel_id=1, source_target_pairs={{0,3},{1,2},{2,1},{3,0},{4,7},{5,6},{6,5},{7,4},{8,11},{9,10},{10,... | collective-permute-start | bytes 491528 | tf_op jit(solution)/shard_map/ppermute | solution.py:354
  6.5 12.4 %collective-permute-start.11 = (bf16[2,160,256]{2,1,0:T(8,128)(2,1)}, bf16[2,160,256]{2,1,0:T(8,128)(2,1)}, u32[]{:S(2)}, u32[]{:S(2)}) collective-permute-start(bf16[2,160,256]{2,1,0:T(8,128)(2,1)} %get-tuple-element.90), channel_id=1, source_target_pairs={{0,1},{1,0},{2,3},{3,2},{4,5},{5,4},{6,7},{7,6},{8,9},{9,8},{10,11... | collective-permute-start | bytes 491528 | tf_op jit(solution)/shard_map/ppermute | solution.py:354
  6.6 12.4 %collective-permute-start.12 = (bf16[2,160,256]{2,1,0:T(8,128)(2,1)}, bf16[2,160,256]{2,1,0:T(8,128)(2,1)}, u32[]{:S(2)}, u32[]{:S(2)}) collective-permute-start(bf16[2,160,256]{2,1,0:T(8,128)(2,1)} %get-tuple-element.91), channel_id=1, source_target_pairs={{0,2},{1,3},{2,0},{3,1},{4,6},{5,7},{6,4},{7,5},{8,10},{9,11},{10,... | collective-permute-start | bytes 491528 | tf_op jit(solution)/shard_map/ppermute | solution.py:354
  16.8 12.4 %collective-permute-start.6 = (bf16[2,2,160,256]{3,2,1,0:T(8,128)(2,1)}, bf16[2,2,160,256]{3,2,1,0:T(8,128)(2,1)}, u32[]{:S(2)}, u32[]{:S(2)}) collective-permute-start(bf16[2,2,160,256]{3,2,1,0:T(8,128)(2,1)} %get-tuple-element.83), channel_id=1, source_target_pairs={{0,4},{1,5},{2,6},{3,7},{4,0},{5,1},{6,2},{7,3},{8,12},{9,13},{10,... | collective-permute-start | bytes 983048 | tf_op jit(solution)/shard_map/ppermute | solution.py:362
  18.5 12.5 %collective-permute-start.7 = (bf16[2,2,160,256]{3,2,1,0:T(8,128)(2,1)}, bf16[2,2,160,256]{3,2,1,0:T(8,128)(2,1)}, u32[]{:S(2)}, u32[]{:S(2)}) collective-permute-start(bf16[2,2,160,256]{3,2,1,0:T(8,128)(2,1)} %get-tuple-element.84), channel_id=1, source_target_pairs={{0,1},{1,0},{2,3},{3,2},{4,8},{5,9},{6,10},{7,11},{8,4},{9,5},{10,... | collective-permute-start | bytes 983048 | tf_op jit(solution)/shard_map/ppermute | solution.py:362
  25.6 20.5 %collective-permute-start.17 = (bf16[2,2,160,256]{3,2,1,0:T(8,128)(2,1)}, bf16[2,2,160,256]{3,2,1,0:T(8,128)(2,1)}, u32[]{:S(2)}, u32[]{:S(2)}) collective-permute-start(bf16[2,2,160,256]{3,2,1,0:T(8,128)(2,1)} %get-tuple-element.97), channel_id=1, source_target_pairs={{0,4},{1,5},{2,6},{3,7},{4,0},{5,1},{6,2},{7,3},{8,12},{9,13},{10,... | collective-permute-start | bytes 983048 | tf_op jit(solution)/shard_map/ppermute | solution.py:362
  27.2 20.2 %collective-permute-start.18 = (bf16[2,2,160,256]{3,2,1,0:T(8,128)(2,1)}, bf16[2,2,160,256]{3,2,1,0:T(8,128)(2,1)}, u32[]{:S(2)}, u32[]{:S(2)}) collective-permute-start(bf16[2,2,160,256]{3,2,1,0:T(8,128)(2,1)} %get-tuple-element.98), channel_id=1, source_target_pairs={{0,1},{1,0},{2,3},{3,2},{4,8},{5,9},{6,10},{7,11},{8,4},{9,5},{10,... | collective-permute-start | bytes 983048 | tf_op jit(solution)/shard_map/ppermute | solution.py:362
  28.9 13.8 %collective-permute-start.14 = (bf16[2,160,256]{2,1,0:T(8,128)(2,1)}, bf16[2,160,256]{2,1,0:T(8,128)(2,1)}, u32[]{:S(2)}, u32[]{:S(2)}) collective-permute-start(bf16[2,160,256]{2,1,0:T(8,128)(2,1)} %get-tuple-element.76), channel_id=1, source_target_pairs={{0,1},{1,0},{2,3},{3,2},{4,5},{5,4},{6,7},{7,6},{8,9},{9,8},{10,11... | collective-permute-start | bytes 491528 | tf_op jit(solution)/shard_map/ppermute | solution.py:354
  29.2 16.3 %collective-permute-start.15 = (bf16[2,160,256]{2,1,0:T(8,128)(2,1)}, bf16[2,160,256]{2,1,0:T(8,128)(2,1)}, u32[]{:S(2)}, u32[]{:S(2)}) collective-permute-start(bf16[2,160,256]{2,1,0:T(8,128)(2,1)} %get-tuple-element.77), channel_id=1, source_target_pairs={{0,2},{1,3},{2,0},{3,1},{4,6},{5,7},{6,4},{7,5},{8,10},{9,11},{10,... | collective-permute-start | bytes 491528 | tf_op jit(solution)/shard_map/ppermute | solution.py:354
  31.0 14.9 %collective-permute-start.16 = (bf16[2,160,256]{2,1,0:T(8,128)(2,1)}, bf16[2,160,256]{2,1,0:T(8,128)(2,1)}, u32[]{:S(2)}, u32[]{:S(2)}) collective-permute-start(bf16[2,160,256]{2,1,0:T(8,128)(2,1)} %get-tuple-element.78), channel_id=1, source_target_pairs={{0,3},{1,2},{2,1},{3,0},{4,7},{5,6},{6,5},{7,4},{8,11},{9,10},{10,... | collective-permute-start | bytes 491528 | tf_op jit(solution)/shard_map/ppermute | solution.py:354
  42.8 18.6 %collective-permute-start.19 = (bf16[2,2,2,80,256]{4,3,2,1,0:T(8,128)(2,1)}, bf16[2,2,2,80,256]{4,3,2,1,0:T(8,128)(2,1)}, u32[]{:S(2)}, u32[]{:S(2)}) collective-permute-start(bf16[2,2,2,80,256]{4,3,2,1,0:T(8,128)(2,1)} %get-tuple-element.103), channel_id=1, source_target_pairs={{0,4},{1,5},{2,6},{3,7},{4,0},{5,1},{6,2},{7,3},{8,12},{9,13},{10,... | collective-permute-start | bytes 983048 | tf_op jit(solution)/shard_map/ppermute | solution.py:362
  45.5 15.8 %collective-permute-start.20 = (bf16[2,2,2,80,256]{4,3,2,1,0:T(8,128)(2,1)}, bf16[2,2,2,80,256]{4,3,2,1,0:T(8,128)(2,1)}, u32[]{:S(2)}, u32[]{:S(2)}) collective-permute-start(bf16[2,2,2,80,256]{4,3,2,1,0:T(8,128)(2,1)} %get-tuple-element.104), channel_id=1, source_target_pairs={{0,1},{1,0},{2,3},{3,2},{4,8},{5,9},{6,10},{7,11},{8,4},{9,5},{10,... | collective-permute-start | bytes 983048 | tf_op jit(solution)/shard_map/ppermute | solution.py:362
  45.9 13.7 %collective-permute-start.8 = (bf16[2,160,256]{2,1,0:T(8,128)(2,1)}, bf16[2,160,256]{2,1,0:T(8,128)(2,1)}, u32[]{:S(2)}, u32[]{:S(2)}) collective-permute-start(bf16[2,160,256]{2,1,0:T(8,128)(2,1)} %bitcast.40), channel_id=1, source_target_pairs={{0,1},{1,0},{2,3},{3,2},{4,5},{5,4},{6,7},{7,6},{8,9},{9,8},{10,11... | collective-permute-start | bytes 491528 | tf_op jit(solution)/shard_map/ppermute | solution.py:354
  46.1 15.2 %collective-permute-start.9 = (bf16[2,160,256]{2,1,0:T(8,128)(2,1)}, bf16[2,160,256]{2,1,0:T(8,128)(2,1)}, u32[]{:S(2)}, u32[]{:S(2)}) collective-permute-start(bf16[2,160,256]{2,1,0:T(8,128)(2,1)} %bitcast.39), channel_id=1, source_target_pairs={{0,2},{1,3},{2,0},{3,1},{4,6},{5,7},{6,4},{7,5},{8,10},{9,11},{10,... | collective-permute-start | bytes 491528 | tf_op jit(solution)/shard_map/ppermute | solution.py:354
  47.5 13.8 %collective-permute-start.10 = (bf16[2,160,256]{2,1,0:T(8,128)(2,1)}, bf16[2,160,256]{2,1,0:T(8,128)(2,1)}, u32[]{:S(2)}, u32[]{:S(2)}) collective-permute-start(bf16[2,160,256]{2,1,0:T(8,128)(2,1)} %bitcast.38), channel_id=1, source_target_pairs={{0,3},{1,2},{2,1},{3,0},{4,7},{5,6},{6,5},{7,4},{8,11},{9,10},{10,... | collective-permute-start | bytes 491528 | tf_op jit(solution)/shard_map/ppermute | solution.py:354
  59.5 10.5 %collective-permute-start.24 = (bf16[2,2,2,80,256]{4,3,2,1,0:T(8,128)(2,1)}, bf16[2,2,2,80,256]{4,3,2,1,0:T(8,128)(2,1)}, u32[]{:S(2)}, u32[]{:S(2)}) collective-permute-start(bf16[2,2,2,80,256]{4,3,2,1,0:T(8,128)(2,1)} %get-tuple-element.115), channel_id=1, source_target_pairs={{0,4},{1,5},{2,6},{3,7},{4,0},{5,1},{6,2},{7,3},{8,12},{9,13},{10,... | collective-permute-start | bytes 983048 | tf_op jit(solution)/shard_map/ppermute | solution.py:362
  61.2 8.8 %collective-permute-start.25 = (bf16[2,2,2,80,256]{4,3,2,1,0:T(8,128)(2,1)}, bf16[2,2,2,80,256]{4,3,2,1,0:T(8,128)(2,1)}, u32[]{:S(2)}, u32[]{:S(2)}) collective-permute-start(bf16[2,2,2,80,256]{4,3,2,1,0:T(8,128)(2,1)} %get-tuple-element.116), channel_id=1, source_target_pairs={{0,1},{1,0},{2,3},{3,2},{4,8},{5,9},{6,10},{7,11},{8,4},{9,5},{10,... | collective-permute-start | bytes 983048 | tf_op jit(solution)/shard_map/ppermute | solution.py:362
  65.2 8.7 %collective-permute-start.29 = (bf16[2,160,256]{2,1,0:T(8,128)(2,1)}, bf16[2,160,256]{2,1,0:T(8,128)(2,1)}, u32[]{:S(2)}, u32[]{:S(2)}) collective-permute-start(bf16[2,160,256]{2,1,0:T(8,128)(2,1)} %get-tuple-element.121), channel_id=1, source_target_pairs={{0,1},{1,0},{2,3},{3,2},{4,5},{5,4},{6,7},{7,6},{8,9},{9,8},{10,11... | collective-permute-start | bytes 491528 | tf_op jit(solution)/shard_map/ppermute | solution.py:354
  65.2 8.7 %collective-permute-start.30 = (bf16[2,160,256]{2,1,0:T(8,128)(2,1)}, bf16[2,160,256]{2,1,0:T(8,128)(2,1)}, u32[]{:S(2)}, u32[]{:S(2)}) collective-permute-start(bf16[2,160,256]{2,1,0:T(8,128)(2,1)} %get-tuple-element.122), channel_id=1, source_target_pairs={{0,2},{1,3},{2,0},{3,1},{4,6},{5,7},{6,4},{7,5},{8,10},{9,11},{10,... | collective-permute-start | bytes 491528 | tf_op jit(solution)/shard_map/ppermute | solution.py:354
  70.1 8.7 %collective-permute-start.23 = (bf16[2,160,256]{2,1,0:T(8,128)(2,1)}, bf16[2,160,256]{2,1,0:T(8,128)(2,1)}, u32[]{:S(2)}, u32[]{:S(2)}) collective-permute-start(bf16[2,160,256]{2,1,0:T(8,128)(2,1)} %bitcast.36), channel_id=1, source_target_pairs={{0,3},{1,2},{2,1},{3,0},{4,7},{5,6},{6,5},{7,4},{8,11},{9,10},{10,... | collective-permute-start | bytes 491528 | tf_op jit(solution)/shard_map/ppermute | solution.py:354
  73.9 9.2 %collective-permute-start.27 = (bf16[2,160,256]{2,1,0:T(8,128)(2,1)}, bf16[2,160,256]{2,1,0:T(8,128)(2,1)}, u32[]{:S(2)}, u32[]{:S(2)}) collective-permute-start(bf16[2,160,256]{2,1,0:T(8,128)(2,1)} %get-tuple-element.119), channel_id=1, source_target_pairs={{0,2},{1,3},{2,0},{3,1},{4,6},{5,7},{6,4},{7,5},{8,10},{9,11},{10,... | collective-permute-start | bytes 491528 | tf_op jit(solution)/shard_map/ppermute | solution.py:354
  75.2 10.5 %collective-permute-start.28 = (bf16[2,160,256]{2,1,0:T(8,128)(2,1)}, bf16[2,160,256]{2,1,0:T(8,128)(2,1)}, u32[]{:S(2)}, u32[]{:S(2)}) collective-permute-start(bf16[2,160,256]{2,1,0:T(8,128)(2,1)} %get-tuple-element.120), channel_id=1, source_target_pairs={{0,3},{1,2},{2,1},{3,0},{4,7},{5,6},{6,5},{7,4},{8,11},{9,10},{10,... | collective-permute-start | bytes 491528 | tf_op jit(solution)/shard_map/ppermute | solution.py:354
  (10 other events, 64.2 us)

commit v6 on v5

--- a/solution.py
+++ b/solution.py
@@ -14,7 +14,7 @@
 FAR_UP = 2
 WINDOW = 4
 CHAIN = PLANE + FAR_UP + 1
-STRIP = 64
+STRIP = 32
 F32 = jnp.float32
 BF16 = jnp.bfloat16
 HBM = pl.BlockSpec(memory_space=pltpu.HBM)
@@ -68,24 +68,27 @@
         load.start()
     if lists:
         find_limits(*lists_in, refs[count])
+    place = place_of()
+    copies = []
     for index, load in enumerate(loads):
         load.wait()
         turned[index] = rows[index].T
-    place = place_of()
-    copies = []
-    first = 0
-    for number, chunk in enumerate(chunks):
-        span = CHUNKS[chunk] * head_size
-        for hop in range(PLANE):
-            row = pl.multiple_of(first + (place ^ hop) * span, 16)
-            slot = number * PLANE + hop
-            copies.append(
-                pltpu.make_async_copy(
-                    turned.at[:, pl.ds(row, span)], outs[slot], sems.at[slot]
+        first = 0
+        for number, chunk in enumerate(chunks):
+            span = CHUNKS[chunk] * head_size
+            for hop in range(PLANE):
+                row = pl.multiple_of(first + (place ^ hop) * span, 16)
+                slot = number * PLANE + hop
+                copy = pltpu.make_async_copy(
+                    turned.at[index, pl.ds(row, span)],
+                    outs[slot].at[index],
+                    sems.at[index, slot],
                 )
-            )
-        first += PLANE * span
-    run_copies(copies)
+                copy.start()
+                copies.append(copy)
+            first += PLANE * span
+    for copy in copies:
+        copy.wait()
 
 
 def find_limits(local_blocks, far_blocks, counts, out):
@@ -272,30 +275,37 @@
 
 def join_kernel(planes, local, even_in, odd_in, *refs):
     outs = refs[:PLANE]
-    held, sems = refs[PLANE:]
+    held, even, odd, sems = refs[PLANE:]
     place, parity = place_of(), level_of() % 2
     level = level_of()
-    held[...] = local[...]
+    run_copies(
+        [
+            pltpu.make_async_copy(local, held, sems.at[0]),
+            pltpu.make_async_copy(even_in, even, sems.at[1]),
+            pltpu.make_async_copy(odd_in, odd, sems.at[2]),
+        ]
+    )
+
+    def add(unit, part):
+        held[unit] = (held[unit].astype(F32) + part.astype(F32)).astype(BF16)
 
     def take(below, above):
         @pl.when(level > 0)
         def _():
-            held[0] = (held[0].astype(F32) + below[0].astype(F32)).astype(BF16)
+            add(0, below[0])
 
         @pl.when(level < planes - 1)
         def _():
-            for unit in range(2):
-                held[2 + unit] = (held[2 + unit].astype(F32) + above[unit].astype(F32)).astype(
-                    BF16
-                )
+            add(2, above[0])
+            add(3, above[1])
 
     @pl.when(parity == 0)
     def _():
-        take(odd_in, even_in)
+        take(odd, even)
 
     @pl.when(parity == 1)
     def _():
-        take(even_in, odd_in)
+        take(even, odd)
 
     run_copies(
         [
@@ -378,10 +388,10 @@
                 pltpu.VMEM((2, tokens, span), BF16),
                 pltpu.VMEM((2, span, tokens), BF16),
                 pltpu.SemaphoreType.DMA((2,)),
-                pltpu.SemaphoreType.DMA((count,)),
+                pltpu.SemaphoreType.DMA((2, count)),
             ],
             compiler_params=params(),
-            cost_estimate=cost(3),
+            cost_estimate=cost(12),
         )(first, second, *lists)
 
     def spread(parts):
@@ -460,10 +470,12 @@
         return pl.pallas_call(
             lambda *refs: join_kernel(size // PLANE, *refs),
             out_shape=[piece(heads)] * PLANE,
-            in_specs=[VMEM] * 3,
+            in_specs=[HBM] * 3,
             out_specs=[HBM] * PLANE,
             scratch_shapes=[
                 pltpu.VMEM((PLANE,) + flat, BF16),
+                pltpu.VMEM((2,) + flat, BF16),
+                pltpu.VMEM((2,) + flat, BF16),
                 pltpu.SemaphoreType.DMA((PLANE,)),
             ],
             compiler_params=params(),
@@ -504,7 +516,7 @@
             ],
             input_output_aliases={len(parts) + index: index for index in range(len(held))},
             compiler_params=params(),
-            cost_estimate=cost(3),
+            cost_estimate=cost(8),
         )(*parts, *held)
 
     attended, query_grad = finish(query_pieces, every)

time: 88.6 us -> 88.3 us (level)
  no operation moved by 1% of the time
where the time goes in v6:
time: 88.3 us; the launch traced here: 87.8 us
  Pallas kernels  46 us (52%)
  starting transfers between devices  27.5 us (31%)
  waiting for transfers between devices  12 us (14%)
  local copies, waits for them, and re-layouts  1.38 us (2%)
    pallas_call x2, Pallas kernels, main(): pl.pallas_call(lambda *refs: main_kernel(head_size, heads, *refs), out_sh...  23.5 us
    ppermute x24, starting transfers between devices, swap(): return lax.ppermute(array, 'seq', pairs)  18.9 us
    ppermute x24, waiting for transfers between devices, swap(): return lax.ppermute(array, 'seq', pairs)  10.7 us
    ppermute x8, starting transfers between devices, level_swap(): return lax.ppermute(array, 'seq', pairs)  8.64 us
    pallas_call x3, Pallas kernels, finish(): pl.pallas_call(lambda *refs: finish_kernel(head_size, chunks, len(held),...  7.22 us
    pallas_call x2, Pallas kernels, prep(): pl.pallas_call(lambda *refs: prep_kernel(head_size, chunks, len(lists), *...  6.75 us
    pallas_call x2, Pallas kernels, join(): pl.pallas_call(lambda *refs: join_kernel(size // PLANE, *refs), out_shape...  4.46 us
    pallas_call x2, Pallas kernels, body(): pl.pallas_call(pack_kernel, out_shape=[pair, pair], in_specs=[HBM] * PLAN...  4.06 us
  transfers between devices with their start and end apart: 32, of which 9 were waited for; matrix products, arithmetic and copies ran while one was open for 2% of the time, Pallas kernels for 47%

profile of v6, /device:TPU:0, one launch (start us, length us, event | category | flops | bytes accessed | tf_op | source)
XLA Modules:
  0.0 87.8 jit_solution(14300478298195075031)
XLA Ops:
  0.6 2.5 %shard_map.103 = (bf16[2,160,256]{2,1,0:T(8,128)(2,1)}, bf16[2,160,256]{2,1,0:T(8,128)(2,1)}, bf16[2,160,256]{2,1,0:T(8,128)(2,1)}, bf16[2,160,256]{2,1,0:T(8,12...) custom-call(bf16[256,1280]{1,0:T(8,128)(2,1)} %refs_0_.3, ...), custom_call_target="tpu_custom_call" | custom-call | flops 12000000000 | bytes 1000000 | tf_op jit(solution)/shard_map/pallas_call | solution.py:381
  3.7 2.6 %collective-permute-start.1 = (bf16[2,160,256]{2,1,0:T(8,128)(2,1)}, bf16[2,160,256]{2,1,0:T(8,128)(2,1)}, u32[]{:S(2)}, u32[]{:S(2)}) collective-permute-start(bf16[2,160,256]{2,1,0:T(8,128)(2,1)} %get-tuple-element.69), channel_id=1, source_target_pairs={{0,2},{1,3},{2,0},{3,1},{4,6},{5,7},{6,4},{7,5},{8,10},{9,11},{10,... | collective-permute-start | bytes 491528 | tf_op jit(solution)/shard_map/ppermute | solution.py:364
  6.5 1.9 %collective-permute-start.12 = (bf16[2,160,256]{2,1,0:T(8,128)(2,1)}, bf16[2,160,256]{2,1,0:T(8,128)(2,1)}, u32[]{:S(2)}, u32[]{:S(2)}) collective-permute-start(bf16[2,160,256]{2,1,0:T(8,128)(2,1)} %get-tuple-element.91), channel_id=1, source_target_pairs={{0,2},{1,3},{2,0},{3,1},{4,6},{5,7},{6,4},{7,5},{8,10},{9,11},{10,... | collective-permute-start | bytes 491528 | tf_op jit(solution)/shard_map/ppermute | solution.py:364
  9.8 4.2 %shard_map.102 = (bf16[2,160,256]{2,1,0:T(8,128)(2,1)}, bf16[2,160,256]{2,1,0:T(8,128)(2,1)}, bf16[2,160,256]{2,1,0:T(8,128)(2,1)}, bf16[2,160,256]{2,1,0:T(8,12...) custom-call(bf16[256,1280]{1,0:T(8,128)(2,1)} %refs_0_.2, ...), custom_call_target="tpu_custom_call" | custom-call | flops 12000000000 | bytes 1000000 | tf_op jit(solution)/shard_map/pallas_call | solution.py:381
  14.6 2.0 %shard_map.104 = (bf16[2,2,160,256]{3,2,1,0:T(8,128)(2,1)}, bf16[2,2,160,256]{3,2,1,0:T(8,128)(2,1)}) custom-call(bf16[2,160,256]{2,1,0:T(8,128)(2,1)} %get-tuple-element.79.refs_0_, bf16[2,160,256]{2,1,0:T(8,128)(2,1)} %collective-permute-done.refs_1_, bf16[2,160,256]{2,1,0:T(8,128)(2,1)} %collective-permute-done.1.refs_2_, ...), custom_call_target="tpu_custom_call" | custom-call | flops 2000000000 | bytes 1000000 | tf_op jit(solution)/shard_map/pallas_call | solution.py:417
  16.6 1.7 %collective-permute-start.6 = (bf16[2,2,160,256]{3,2,1,0:T(8,128)(2,1)}, bf16[2,2,160,256]{3,2,1,0:T(8,128)(2,1)}, u32[]{:S(2)}, u32[]{:S(2)}) collective-permute-start(bf16[2,2,160,256]{3,2,1,0:T(8,128)(2,1)} %get-tuple-element.83), channel_id=1, source_target_pairs={{0,4},{1,5},{2,6},{3,7},{4,0},{5,1},{6,2},{7,3},{8,12},{9,13},{10,... | collective-permute-start | bytes 983048 | tf_op jit(solution)/shard_map/ppermute | solution.py:372
  18.9 1.8 %collective-permute-start.4 = (bf16[2,160,256]{2,1,0:T(8,128)(2,1)}, bf16[2,160,256]{2,1,0:T(8,128)(2,1)}, u32[]{:S(2)}, u32[]{:S(2)}) collective-permute-start(bf16[2,160,256]{2,1,0:T(8,128)(2,1)} %get-tuple-element.73), channel_id=1, source_target_pairs={{0,2},{1,3},{2,0},{3,1},{4,6},{5,7},{6,4},{7,5},{8,10},{9,11},{10,... | collective-permute-start | bytes 491528 | tf_op jit(solution)/shard_map/ppermute | solution.py:364
  21.6 1.7 %collective-permute-start.5 = (bf16[2,160,256]{2,1,0:T(8,128)(2,1)}, bf16[2,160,256]{2,1,0:T(8,128)(2,1)}, u32[]{:S(2)}, u32[]{:S(2)}) collective-permute-start(bf16[2,160,256]{2,1,0:T(8,128)(2,1)} %get-tuple-element.74), channel_id=1, source_target_pairs={{0,3},{1,2},{2,1},{3,0},{4,7},{5,6},{6,5},{7,4},{8,11},{9,10},{10,... | collective-permute-start | bytes 491528 | tf_op jit(solution)/shard_map/ppermute | solution.py:364
  23.4 2.0 %shard_map.106 = (bf16[2,2,160,256]{3,2,1,0:T(8,128)(2,1)}, bf16[2,2,160,256]{3,2,1,0:T(8,128)(2,1)}) custom-call(bf16[2,160,256]{2,1,0:T(8,128)(2,1)} %get-tuple-element.93.refs_0_, bf16[2,160,256]{2,1,0:T(8,128)(2,1)} %collective-permute-done.11.refs_1_, bf16[2,160,256]{2,1,0:T(8,128)(2,1)} %collective-permute-done.12.refs_2_, ...), custom_call_target="tpu_custom_call" | custom-call | flops 2000000000 | bytes 1000000 | tf_op jit(solution)/shard_map/pallas_call | solution.py:417
  25.5 1.6 %collective-permute-start.17 = (bf16[2,2,160,256]{3,2,1,0:T(8,128)(2,1)}, bf16[2,2,160,256]{3,2,1,0:T(8,128)(2,1)}, u32[]{:S(2)}, u32[]{:S(2)}) collective-permute-start(bf16[2,2,160,256]{3,2,1,0:T(8,128)(2,1)} %get-tuple-element.97), channel_id=1, source_target_pairs={{0,4},{1,5},{2,6},{3,7},{4,0},{5,1},{6,2},{7,3},{8,12},{9,13},{10,... | collective-permute-start | bytes 983048 | tf_op jit(solution)/shard_map/ppermute | solution.py:372
  27.1 1.7 %collective-permute-done.5 = bf16[2,160,256]{2,1,0:T(8,128)(2,1)} collective-permute-done((bf16[2,160,256]{2,1,0:T(8,128)(2,1)}, bf16[2,160,256]{2,1,0:T(8,128)(2,1)}, u32[]{:S(2)}, u32[]{:S(2)}) %collective-permute-start.5) | collective-permute-done | bytes 163872 | tf_op jit(solution)/shard_map/ppermute | solution.py:364
  29.1 1.8 %collective-permute-start.15 = (bf16[2,160,256]{2,1,0:T(8,128)(2,1)}, bf16[2,160,256]{2,1,0:T(8,128)(2,1)}, u32[]{:S(2)}, u32[]{:S(2)}) collective-permute-start(bf16[2,160,256]{2,1,0:T(8,128)(2,1)} %get-tuple-element.77), channel_id=1, source_target_pairs={{0,2},{1,3},{2,0},{3,1},{4,6},{5,7},{6,4},{7,5},{8,10},{9,11},{10,... | collective-permute-start | bytes 491528 | tf_op jit(solution)/shard_map/ppermute | solution.py:364
  30.9 11.7 %shard_map.105 = (bf16[2,2,80,256]{3,2,1,0:T(8,128)(2,1)}, bf16[2,2,80,256]{3,2,1,0:T(8,128)(2,1)}, bf16[2,2,80,256]{3,2,1,0:T(8,128)(2,1)}, bf16[2,2,80,256]{3,...) custom-call(s32[64]{0:T(128)} %get-tuple-element.66.refs_0_, ...), custom_call_target="tpu_custom_call" | custom-call | flops 2000000000 | bytes 1000000 | tf_op jit(solution)/shard_map/pallas_call | solution.py:435
  42.6 2.8 %collective-permute-start.19 = (bf16[2,2,2,80,256]{4,3,2,1,0:T(8,128)(2,1)}, bf16[2,2,2,80,256]{4,3,2,1,0:T(8,128)(2,1)}, u32[]{:S(2)}, u32[]{:S(2)}) collective-permute-start(bf16[2,2,2,80,256]{4,3,2,1,0:T(8,128)(2,1)} %get-tuple-element.103), channel_id=1, source_target_pairs={{0,4},{1,5},{2,6},{3,7},{4,0},{5,1},{6,2},{7,3},{8,12},{9,13},{10,... | collective-permute-start | bytes 983048 | tf_op jit(solution)/shard_map/ppermute | solution.py:372
  47.6 11.8 %shard_map.107 = (bf16[2,2,80,256]{3,2,1,0:T(8,128)(2,1)}, bf16[2,2,80,256]{3,2,1,0:T(8,128)(2,1)}, bf16[2,2,80,256]{3,2,1,0:T(8,128)(2,1)}, bf16[2,2,80,256]{3,...) custom-call(s32[64]{0:T(128)} %get-tuple-element.66.refs_0_, ...), custom_call_target="tpu_custom_call" | custom-call | flops 2000000000 | bytes 1000000 | tf_op jit(solution)/shard_map/pallas_call | solution.py:435
  59.4 1.7 %collective-permute-start.24 = (bf16[2,2,2,80,256]{4,3,2,1,0:T(8,128)(2,1)}, bf16[2,2,2,80,256]{4,3,2,1,0:T(8,128)(2,1)}, u32[]{:S(2)}, u32[]{:S(2)}) collective-permute-start(bf16[2,2,2,80,256]{4,3,2,1,0:T(8,128)(2,1)} %get-tuple-element.115), channel_id=1, source_target_pairs={{0,4},{1,5},{2,6},{3,7},{4,0},{5,1},{6,2},{7,3},{8,12},{9,13},{10,... | collective-permute-start | bytes 983048 | tf_op jit(solution)/shard_map/ppermute | solution.py:372
  62.7 2.2 %shard_map.109 = (bf16[2,160,256]{2,1,0:T(8,128)(2,1)}, bf16[2,160,256]{2,1,0:T(8,128)(2,1)}, bf16[2,160,256]{2,1,0:T(8,128)(2,1)}, bf16[2,160,256]{2,1,0:T(8,128)(2,1)}) custom-call(bf16[4,2,160,256]{3,2,1,0:T(8,128)(2,1)} %bitcast.34, bf16[2,2,160,256]{3,2,1,0:T(8,128)(2,1)} %bitcast.29.refs_1_, bf16[2,2,160,256]{3,2,1,0:T(8,128)(2,1)} %bitcast.30.refs_2_), custom_call_target="tpu_custom_call" | custom-call | tf_op jit(solution)/shard_map/pallas_call | solution.py:470
  65.7 2.4 %collective-permute-done.22.refs_6_ = bf16[2,160,256]{2,1,0:T(8,128)(2,1)} collective-permute-done((bf16[2,160,256]{2,1,0:T(8,128)(2,1)}, bf16[2,160,256]{2,1,0:T(8,128)(2,1)}, u32[]{:S(2)}, u32[]{:S(2)}) %collective-permute-start.22) | collective-permute-done | bytes 163872 | tf_op jit(solution)/shard_map/ppermute | solution.py:364
  71.4 2.2 %shard_map.110 = (bf16[2,160,256]{2,1,0:T(8,128)(2,1)}, bf16[2,160,256]{2,1,0:T(8,128)(2,1)}, bf16[2,160,256]{2,1,0:T(8,128)(2,1)}, bf16[2,160,256]{2,1,0:T(8,128)(2,1)}) custom-call(bf16[4,2,160,256]{3,2,1,0:T(8,128)(2,1)} %bitcast.35, bf16[2,2,160,256]{3,2,1,0:T(8,128)(2,1)} %bitcast.32.refs_1_, bf16[2,2,160,256]{3,2,1,0:T(8,128)(2,1)} %bitcast.33.refs_2_), custom_call_target="tpu_custom_call" | custom-call | tf_op jit(solution)/shard_map/pallas_call | solution.py:470
  75.9 2.2 %shard_map.111 = (bf16[256,1280]{1,0:T(8,128)(2,1)}, bf16[256,1280]{1,0:T(8,128)(2,1)}) custom-call(bf16[2,160,256]{2,1,0:T(8,128)(2,1)} %get-tuple-element.113.refs_0_, bf16[2,160,256]{2,1,0:T(8,128)(2,1)} %collective-permute-done.29.refs_1_, bf16[2,160,256]{2,1,0:T(8,128)(2,1)} %collective-permute-done.30.refs_2_, ...), custom_call_target="tpu_custom_call" | custom-call | flops 8000000000 | bytes 1000000 | tf_op jit(solution)/shard_map/pallas_call | solution.py:506
  78.5 2.8 %shard_map.108 = (bf16[256,1280]{1,0:T(8,128)(2,1)}, bf16[256,1280]{1,0:T(8,128)(2,1)}) custom-call(bf16[2,160,256]{2,1,0:T(8,128)(2,1)} %bitcast.43, bf16[2,160,256]{2,1,0:T(8,128)(2,1)} %collective-permute-done.8.refs_1_, bf16[2,160,256]{2,1,0:T(8,128)(2,1)} %collective-permute-done.9.refs_2_, bf16[2,160,256]{2,1,0:T(8,128)(2,1)} %collective-permute-done.10.refs_3_, ...), custom_call_target="tpu_custom_call" | custom-call | flops 8000000000 | bytes 1000000 | tf_op jit(solution)/shard_map/pallas_call | solution.py:506
  81.3 1.6 %collective-permute-done.27.refs_2_ = bf16[2,160,256]{2,1,0:T(8,128)(2,1)} collective-permute-done((bf16[2,160,256]{2,1,0:T(8,128)(2,1)}, bf16[2,160,256]{2,1,0:T(8,128)(2,1)}, u32[]{:S(2)}, u32[]{:S(2)}) %collective-permute-start.27) | collective-permute-done | bytes 163872 | tf_op jit(solution)/shard_map/ppermute | solution.py:364
  82.9 2.6 %collective-permute-done.28.refs_3_ = bf16[2,160,256]{2,1,0:T(8,128)(2,1)} collective-permute-done((bf16[2,160,256]{2,1,0:T(8,128)(2,1)}, bf16[2,160,256]{2,1,0:T(8,128)(2,1)}, u32[]{:S(2)}, u32[]{:S(2)}) %collective-permute-start.28) | collective-permute-done | bytes 163872 | tf_op jit(solution)/shard_map/ppermute | solution.py:364
  85.5 2.2 %shard_map.112 = (bf16[256,1280]{1,0:T(8,128)(2,1)}, bf16[256,1280]{1,0:T(8,128)(2,1)}) custom-call(bf16[2,160,256]{2,1,0:T(8,128)(2,1)} %get-tuple-element.117.refs_0_, bf16[2,160,256]{2,1,0:T(8,128)(2,1)} %collective-permute-done.26.refs_1_, bf16[2,160,256]{2,1,0:T(8,128)(2,1)} %collective-permute-done.27.refs_2_, ...), custom_call_target="tpu_custom_call", output_to_operand_aliasing={{0}: (4, {}), {1}: (5, {})} | custom-call | flops 8000000000 | bytes 1000000 | tf_op jit(solution)/shard_map/pallas_call | solution.py:506
  (57 shorter events, 15.1 us)
Async XLA Ops:
  3.2 10.9 %collective-permute-start = (bf16[2,160,256]{2,1,0:T(8,128)(2,1)}, bf16[2,160,256]{2,1,0:T(8,128)(2,1)}, u32[]{:S(2)}, u32[]{:S(2)}) collective-permute-start(bf16[2,160,256]{2,1,0:T(8,128)(2,1)} %get-tuple-element.68), channel_id=1, source_target_pairs={{0,1},{1,0},{2,3},{3,2},{4,5},{5,4},{6,7},{7,6},{8,9},{9,8},{10,11... | collective-permute-start | bytes 491528 | tf_op jit(solution)/shard_map/ppermute | solution.py:364
  3.7 10.5 %collective-permute-start.1 = (bf16[2,160,256]{2,1,0:T(8,128)(2,1)}, bf16[2,160,256]{2,1,0:T(8,128)(2,1)}, u32[]{:S(2)}, u32[]{:S(2)}) collective-permute-start(bf16[2,160,256]{2,1,0:T(8,128)(2,1)} %get-tuple-element.69), channel_id=1, source_target_pairs={{0,2},{1,3},{2,0},{3,1},{4,6},{5,7},{6,4},{7,5},{8,10},{9,11},{10,... | collective-permute-start | bytes 491528 | tf_op jit(solution)/shard_map/ppermute | solution.py:364
  6.3 8.3 %collective-permute-start.2 = (bf16[2,160,256]{2,1,0:T(8,128)(2,1)}, bf16[2,160,256]{2,1,0:T(8,128)(2,1)}, u32[]{:S(2)}, u32[]{:S(2)}) collective-permute-start(bf16[2,160,256]{2,1,0:T(8,128)(2,1)} %get-tuple-element.70), channel_id=1, source_target_pairs={{0,3},{1,2},{2,1},{3,0},{4,7},{5,6},{6,5},{7,4},{8,11},{9,10},{10,... | collective-permute-start | bytes 491528 | tf_op jit(solution)/shard_map/ppermute | solution.py:364
  6.3 12.4 %collective-permute-start.11 = (bf16[2,160,256]{2,1,0:T(8,128)(2,1)}, bf16[2,160,256]{2,1,0:T(8,128)(2,1)}, u32[]{:S(2)}, u32[]{:S(2)}) collective-permute-start(bf16[2,160,256]{2,1,0:T(8,128)(2,1)} %get-tuple-element.90), channel_id=1, source_target_pairs={{0,1},{1,0},{2,3},{3,2},{4,5},{5,4},{6,7},{7,6},{8,9},{9,8},{10,11... | collective-permute-start | bytes 491528 | tf_op jit(solution)/shard_map/ppermute | solution.py:364
  6.5 12.4 %collective-permute-start.12 = (bf16[2,160,256]{2,1,0:T(8,128)(2,1)}, bf16[2,160,256]{2,1,0:T(8,128)(2,1)}, u32[]{:S(2)}, u32[]{:S(2)}) collective-permute-start(bf16[2,160,256]{2,1,0:T(8,128)(2,1)} %get-tuple-element.91), channel_id=1, source_target_pairs={{0,2},{1,3},{2,0},{3,1},{4,6},{5,7},{6,4},{7,5},{8,10},{9,11},{10,... | collective-permute-start | bytes 491528 | tf_op jit(solution)/shard_map/ppermute | solution.py:364
  16.6 12.4 %collective-permute-start.6 = (bf16[2,2,160,256]{3,2,1,0:T(8,128)(2,1)}, bf16[2,2,160,256]{3,2,1,0:T(8,128)(2,1)}, u32[]{:S(2)}, u32[]{:S(2)}) collective-permute-start(bf16[2,2,160,256]{3,2,1,0:T(8,128)(2,1)} %get-tuple-element.83), channel_id=1, source_target_pairs={{0,4},{1,5},{2,6},{3,7},{4,0},{5,1},{6,2},{7,3},{8,12},{9,13},{10,... | collective-permute-start | bytes 983048 | tf_op jit(solution)/shard_map/ppermute | solution.py:372
  18.3 12.5 %collective-permute-start.7 = (bf16[2,2,160,256]{3,2,1,0:T(8,128)(2,1)}, bf16[2,2,160,256]{3,2,1,0:T(8,128)(2,1)}, u32[]{:S(2)}, u32[]{:S(2)}) collective-permute-start(bf16[2,2,160,256]{3,2,1,0:T(8,128)(2,1)} %get-tuple-element.84), channel_id=1, source_target_pairs={{0,1},{1,0},{2,3},{3,2},{4,8},{5,9},{6,10},{7,11},{8,4},{9,5},{10,... | collective-permute-start | bytes 983048 | tf_op jit(solution)/shard_map/ppermute | solution.py:372
  25.5 20.5 %collective-permute-start.17 = (bf16[2,2,160,256]{3,2,1,0:T(8,128)(2,1)}, bf16[2,2,160,256]{3,2,1,0:T(8,128)(2,1)}, u32[]{:S(2)}, u32[]{:S(2)}) collective-permute-start(bf16[2,2,160,256]{3,2,1,0:T(8,128)(2,1)} %get-tuple-element.97), channel_id=1, source_target_pairs={{0,4},{1,5},{2,6},{3,7},{4,0},{5,1},{6,2},{7,3},{8,12},{9,13},{10,... | collective-permute-start | bytes 983048 | tf_op jit(solution)/shard_map/ppermute | solution.py:372
  27.1 20.2 %collective-permute-start.18 = (bf16[2,2,160,256]{3,2,1,0:T(8,128)(2,1)}, bf16[2,2,160,256]{3,2,1,0:T(8,128)(2,1)}, u32[]{:S(2)}, u32[]{:S(2)}) collective-permute-start(bf16[2,2,160,256]{3,2,1,0:T(8,128)(2,1)} %get-tuple-element.98), channel_id=1, source_target_pairs={{0,1},{1,0},{2,3},{3,2},{4,8},{5,9},{6,10},{7,11},{8,4},{9,5},{10,... | collective-permute-start | bytes 983048 | tf_op jit(solution)/shard_map/ppermute | solution.py:372
  28.8 13.8 %collective-permute-start.14 = (bf16[2,160,256]{2,1,0:T(8,128)(2,1)}, bf16[2,160,256]{2,1,0:T(8,128)(2,1)}, u32[]{:S(2)}, u32[]{:S(2)}) collective-permute-start(bf16[2,160,256]{2,1,0:T(8,128)(2,1)} %get-tuple-element.76), channel_id=1, source_target_pairs={{0,1},{1,0},{2,3},{3,2},{4,5},{5,4},{6,7},{7,6},{8,9},{9,8},{10,11... | collective-permute-start | bytes 491528 | tf_op jit(solution)/shard_map/ppermute | solution.py:364
  29.1 16.3 %collective-permute-start.15 = (bf16[2,160,256]{2,1,0:T(8,128)(2,1)}, bf16[2,160,256]{2,1,0:T(8,128)(2,1)}, u32[]{:S(2)}, u32[]{:S(2)}) collective-permute-start(bf16[2,160,256]{2,1,0:T(8,128)(2,1)} %get-tuple-element.77), channel_id=1, source_target_pairs={{0,2},{1,3},{2,0},{3,1},{4,6},{5,7},{6,4},{7,5},{8,10},{9,11},{10,... | collective-permute-start | bytes 491528 | tf_op jit(solution)/shard_map/ppermute | solution.py:364
  30.9 14.9 %collective-permute-start.16 = (bf16[2,160,256]{2,1,0:T(8,128)(2,1)}, bf16[2,160,256]{2,1,0:T(8,128)(2,1)}, u32[]{:S(2)}, u32[]{:S(2)}) collective-permute-start(bf16[2,160,256]{2,1,0:T(8,128)(2,1)} %get-tuple-element.78), channel_id=1, source_target_pairs={{0,3},{1,2},{2,1},{3,0},{4,7},{5,6},{6,5},{7,4},{8,11},{9,10},{10,... | collective-permute-start | bytes 491528 | tf_op jit(solution)/shard_map/ppermute | solution.py:364
  42.6 18.5 %collective-permute-start.19 = (bf16[2,2,2,80,256]{4,3,2,1,0:T(8,128)(2,1)}, bf16[2,2,2,80,256]{4,3,2,1,0:T(8,128)(2,1)}, u32[]{:S(2)}, u32[]{:S(2)}) collective-permute-start(bf16[2,2,2,80,256]{4,3,2,1,0:T(8,128)(2,1)} %get-tuple-element.103), channel_id=1, source_target_pairs={{0,4},{1,5},{2,6},{3,7},{4,0},{5,1},{6,2},{7,3},{8,12},{9,13},{10,... | collective-permute-start | bytes 983048 | tf_op jit(solution)/shard_map/ppermute | solution.py:372
  45.4 15.8 %collective-permute-start.20 = (bf16[2,2,2,80,256]{4,3,2,1,0:T(8,128)(2,1)}, bf16[2,2,2,80,256]{4,3,2,1,0:T(8,128)(2,1)}, u32[]{:S(2)}, u32[]{:S(2)}) collective-permute-start(bf16[2,2,2,80,256]{4,3,2,1,0:T(8,128)(2,1)} %get-tuple-element.104), channel_id=1, source_target_pairs={{0,1},{1,0},{2,3},{3,2},{4,8},{5,9},{6,10},{7,11},{8,4},{9,5},{10,... | collective-permute-start | bytes 983048 | tf_op jit(solution)/shard_map/ppermute | solution.py:372
  45.7 13.7 %collective-permute-start.8 = (bf16[2,160,256]{2,1,0:T(8,128)(2,1)}, bf16[2,160,256]{2,1,0:T(8,128)(2,1)}, u32[]{:S(2)}, u32[]{:S(2)}) collective-permute-start(bf16[2,160,256]{2,1,0:T(8,128)(2,1)} %bitcast.40), channel_id=1, source_target_pairs={{0,1},{1,0},{2,3},{3,2},{4,5},{5,4},{6,7},{7,6},{8,9},{9,8},{10,11... | collective-permute-start | bytes 491528 | tf_op jit(solution)/shard_map/ppermute | solution.py:364
  45.9 15.2 %collective-permute-start.9 = (bf16[2,160,256]{2,1,0:T(8,128)(2,1)}, bf16[2,160,256]{2,1,0:T(8,128)(2,1)}, u32[]{:S(2)}, u32[]{:S(2)}) collective-permute-start(bf16[2,160,256]{2,1,0:T(8,128)(2,1)} %bitcast.39), channel_id=1, source_target_pairs={{0,2},{1,3},{2,0},{3,1},{4,6},{5,7},{6,4},{7,5},{8,10},{9,11},{10,... | collective-permute-start | bytes 491528 | tf_op jit(solution)/shard_map/ppermute | solution.py:364
  47.3 13.8 %collective-permute-start.10 = (bf16[2,160,256]{2,1,0:T(8,128)(2,1)}, bf16[2,160,256]{2,1,0:T(8,128)(2,1)}, u32[]{:S(2)}, u32[]{:S(2)}) collective-permute-start(bf16[2,160,256]{2,1,0:T(8,128)(2,1)} %bitcast.38), channel_id=1, source_target_pairs={{0,3},{1,2},{2,1},{3,0},{4,7},{5,6},{6,5},{7,4},{8,11},{9,10},{10,... | collective-permute-start | bytes 491528 | tf_op jit(solution)/shard_map/ppermute | solution.py:364
  59.4 10.4 %collective-permute-start.24 = (bf16[2,2,2,80,256]{4,3,2,1,0:T(8,128)(2,1)}, bf16[2,2,2,80,256]{4,3,2,1,0:T(8,128)(2,1)}, u32[]{:S(2)}, u32[]{:S(2)}) collective-permute-start(bf16[2,2,2,80,256]{4,3,2,1,0:T(8,128)(2,1)} %get-tuple-element.115), channel_id=1, source_target_pairs={{0,4},{1,5},{2,6},{3,7},{4,0},{5,1},{6,2},{7,3},{8,12},{9,13},{10,... | collective-permute-start | bytes 983048 | tf_op jit(solution)/shard_map/ppermute | solution.py:372
  61.1 8.9 %collective-permute-start.25 = (bf16[2,2,2,80,256]{4,3,2,1,0:T(8,128)(2,1)}, bf16[2,2,2,80,256]{4,3,2,1,0:T(8,128)(2,1)}, u32[]{:S(2)}, u32[]{:S(2)}) collective-permute-start(bf16[2,2,2,80,256]{4,3,2,1,0:T(8,128)(2,1)} %get-tuple-element.116), channel_id=1, source_target_pairs={{0,1},{1,0},{2,3},{3,2},{4,8},{5,9},{6,10},{7,11},{8,4},{9,5},{10,... | collective-permute-start | bytes 983048 | tf_op jit(solution)/shard_map/ppermute | solution.py:372
  64.9 8.7 %collective-permute-start.29 = (bf16[2,160,256]{2,1,0:T(8,128)(2,1)}, bf16[2,160,256]{2,1,0:T(8,128)(2,1)}, u32[]{:S(2)}, u32[]{:S(2)}) collective-permute-start(bf16[2,160,256]{2,1,0:T(8,128)(2,1)} %get-tuple-element.121), channel_id=1, source_target_pairs={{0,1},{1,0},{2,3},{3,2},{4,5},{5,4},{6,7},{7,6},{8,9},{9,8},{10,11... | collective-permute-start | bytes 491528 | tf_op jit(solution)/shard_map/ppermute | solution.py:364
  65.0 8.7 %collective-permute-start.30 = (bf16[2,160,256]{2,1,0:T(8,128)(2,1)}, bf16[2,160,256]{2,1,0:T(8,128)(2,1)}, u32[]{:S(2)}, u32[]{:S(2)}) collective-permute-start(bf16[2,160,256]{2,1,0:T(8,128)(2,1)} %get-tuple-element.122), channel_id=1, source_target_pairs={{0,2},{1,3},{2,0},{3,1},{4,6},{5,7},{6,4},{7,5},{8,10},{9,11},{10,... | collective-permute-start | bytes 491528 | tf_op jit(solution)/shard_map/ppermute | solution.py:364
  70.0 8.5 %collective-permute-start.23 = (bf16[2,160,256]{2,1,0:T(8,128)(2,1)}, bf16[2,160,256]{2,1,0:T(8,128)(2,1)}, u32[]{:S(2)}, u32[]{:S(2)}) collective-permute-start(bf16[2,160,256]{2,1,0:T(8,128)(2,1)} %bitcast.36), channel_id=1, source_target_pairs={{0,3},{1,2},{2,1},{3,0},{4,7},{5,6},{6,5},{7,4},{8,11},{9,10},{10,... | collective-permute-start | bytes 491528 | tf_op jit(solution)/shard_map/ppermute | solution.py:364
  73.7 9.2 %collective-permute-start.27 = (bf16[2,160,256]{2,1,0:T(8,128)(2,1)}, bf16[2,160,256]{2,1,0:T(8,128)(2,1)}, u32[]{:S(2)}, u32[]{:S(2)}) collective-permute-start(bf16[2,160,256]{2,1,0:T(8,128)(2,1)} %get-tuple-element.119), channel_id=1, source_target_pairs={{0,2},{1,3},{2,0},{3,1},{4,6},{5,7},{6,4},{7,5},{8,10},{9,11},{10,... | collective-permute-start | bytes 491528 | tf_op jit(solution)/shard_map/ppermute | solution.py:364
  75.0 10.5 %collective-permute-start.28 = (bf16[2,160,256]{2,1,0:T(8,128)(2,1)}, bf16[2,160,256]{2,1,0:T(8,128)(2,1)}, u32[]{:S(2)}, u32[]{:S(2)}) collective-permute-start(bf16[2,160,256]{2,1,0:T(8,128)(2,1)} %get-tuple-element.120), channel_id=1, source_target_pairs={{0,3},{1,2},{2,1},{3,0},{4,7},{5,6},{6,5},{7,4},{8,11},{9,10},{10,... | collective-permute-start | bytes 491528 | tf_op jit(solution)/shard_map/ppermute | solution.py:364
  (10 other events, 64.2 us)

commit v7 on v5

--- a/solution.py
+++ b/solution.py
@@ -14,7 +14,7 @@
 FAR_UP = 2
 WINDOW = 4
 CHAIN = PLANE + FAR_UP + 1
-STRIP = 64
+STRIP = 32
 F32 = jnp.float32
 BF16 = jnp.bfloat16
 HBM = pl.BlockSpec(memory_space=pltpu.HBM)

time: 88.6 us -> 88.6 us (level)
  no operation moved by 1% of the time
where the time goes in v7:
time: 88.6 us; the launch traced here: 88 us
  Pallas kernels  46.4 us (52%)
  starting transfers between devices  27.5 us (31%)
  waiting for transfers between devices  11.9 us (13%)
  local copies, waits for them, and re-layouts  1.38 us (2%)
    pallas_call x2, Pallas kernels, main(): pl.pallas_call(lambda *refs: main_kernel(head_size, heads, *refs), out_sh...  23.5 us
    ppermute x24, starting transfers between devices, swap(): return lax.ppermute(array, 'seq', pairs)  18.8 us
    ppermute x24, waiting for transfers between devices, swap(): return lax.ppermute(array, 'seq', pairs)  10.6 us
    ppermute x8, starting transfers between devices, level_swap(): return lax.ppermute(array, 'seq', pairs)  8.67 us
    pallas_call x3, Pallas kernels, finish(): pl.pallas_call(lambda *refs: finish_kernel(head_size, chunks, len(held),...  7.22 us
    pallas_call x2, Pallas kernels, prep(): pl.pallas_call(lambda *refs: prep_kernel(head_size, chunks, len(lists), *...  7.04 us
    pallas_call x2, Pallas kernels, join(): pl.pallas_call(lambda *refs: join_kernel(size // PLANE, *refs), out_shape...  4.56 us
    pallas_call x2, Pallas kernels, body(): pl.pallas_call(pack_kernel, out_shape=[pair, pair], in_specs=[HBM] * PLAN...  4.06 us
  transfers between devices with their start and end apart: 32, of which 9 were waited for; matrix products, arithmetic and copies ran while one was open for 2% of the time, Pallas kernels for 47%

profile of v7, /device:TPU:0, one launch (start us, length us, event | category | flops | bytes accessed | tf_op | source)
XLA Modules:
  0.0 88.0 jit_solution(17112593391148824772)
XLA Ops:
  0.6 2.7 %shard_map.103 = (bf16[2,160,256]{2,1,0:T(8,128)(2,1)}, bf16[2,160,256]{2,1,0:T(8,128)(2,1)}, bf16[2,160,256]{2,1,0:T(8,128)(2,1)}, bf16[2,160,256]{2,1,0:T(8,12...) custom-call(bf16[256,1280]{1,0:T(8,128)(2,1)} %refs_0_.3, ...), custom_call_target="tpu_custom_call" | custom-call | flops 3000000000 | bytes 1000000 | tf_op jit(solution)/shard_map/pallas_call | solution.py:371
  3.8 2.6 %collective-permute-start.1 = (bf16[2,160,256]{2,1,0:T(8,128)(2,1)}, bf16[2,160,256]{2,1,0:T(8,128)(2,1)}, u32[]{:S(2)}, u32[]{:S(2)}) collective-permute-start(bf16[2,160,256]{2,1,0:T(8,128)(2,1)} %get-tuple-element.69), channel_id=1, source_target_pairs={{0,2},{1,3},{2,0},{3,1},{4,6},{5,7},{6,4},{7,5},{8,10},{9,11},{10,... | collective-permute-start | bytes 491528 | tf_op jit(solution)/shard_map/ppermute | solution.py:354
  6.6 1.9 %collective-permute-start.12 = (bf16[2,160,256]{2,1,0:T(8,128)(2,1)}, bf16[2,160,256]{2,1,0:T(8,128)(2,1)}, u32[]{:S(2)}, u32[]{:S(2)}) collective-permute-start(bf16[2,160,256]{2,1,0:T(8,128)(2,1)} %get-tuple-element.91), channel_id=1, source_target_pairs={{0,2},{1,3},{2,0},{3,1},{4,6},{5,7},{6,4},{7,5},{8,10},{9,11},{10,... | collective-permute-start | bytes 491528 | tf_op jit(solution)/shard_map/ppermute | solution.py:354
  9.9 4.4 %shard_map.102 = (bf16[2,160,256]{2,1,0:T(8,128)(2,1)}, bf16[2,160,256]{2,1,0:T(8,128)(2,1)}, bf16[2,160,256]{2,1,0:T(8,128)(2,1)}, bf16[2,160,256]{2,1,0:T(8,12...) custom-call(bf16[256,1280]{1,0:T(8,128)(2,1)} %refs_0_.2, ...), custom_call_target="tpu_custom_call" | custom-call | flops 3000000000 | bytes 1000000 | tf_op jit(solution)/shard_map/pallas_call | solution.py:371
  14.8 2.0 %shard_map.104 = (bf16[2,2,160,256]{3,2,1,0:T(8,128)(2,1)}, bf16[2,2,160,256]{3,2,1,0:T(8,128)(2,1)}) custom-call(bf16[2,160,256]{2,1,0:T(8,128)(2,1)} %get-tuple-element.79.refs_0_, bf16[2,160,256]{2,1,0:T(8,128)(2,1)} %collective-permute-done.refs_1_, bf16[2,160,256]{2,1,0:T(8,128)(2,1)} %collective-permute-done.1.refs_2_, ...), custom_call_target="tpu_custom_call" | custom-call | flops 2000000000 | bytes 1000000 | tf_op jit(solution)/shard_map/pallas_call | solution.py:407
  16.8 1.7 %collective-permute-start.6 = (bf16[2,2,160,256]{3,2,1,0:T(8,128)(2,1)}, bf16[2,2,160,256]{3,2,1,0:T(8,128)(2,1)}, u32[]{:S(2)}, u32[]{:S(2)}) collective-permute-start(bf16[2,2,160,256]{3,2,1,0:T(8,128)(2,1)} %get-tuple-element.83), channel_id=1, source_target_pairs={{0,4},{1,5},{2,6},{3,7},{4,0},{5,1},{6,2},{7,3},{8,12},{9,13},{10,... | collective-permute-start | bytes 983048 | tf_op jit(solution)/shard_map/ppermute | solution.py:362
  19.0 1.8 %collective-permute-start.4 = (bf16[2,160,256]{2,1,0:T(8,128)(2,1)}, bf16[2,160,256]{2,1,0:T(8,128)(2,1)}, u32[]{:S(2)}, u32[]{:S(2)}) collective-permute-start(bf16[2,160,256]{2,1,0:T(8,128)(2,1)} %get-tuple-element.73), channel_id=1, source_target_pairs={{0,2},{1,3},{2,0},{3,1},{4,6},{5,7},{6,4},{7,5},{8,10},{9,11},{10,... | collective-permute-start | bytes 491528 | tf_op jit(solution)/shard_map/ppermute | solution.py:354
  21.8 1.7 %collective-permute-start.5 = (bf16[2,160,256]{2,1,0:T(8,128)(2,1)}, bf16[2,160,256]{2,1,0:T(8,128)(2,1)}, u32[]{:S(2)}, u32[]{:S(2)}) collective-permute-start(bf16[2,160,256]{2,1,0:T(8,128)(2,1)} %get-tuple-element.74), channel_id=1, source_target_pairs={{0,3},{1,2},{2,1},{3,0},{4,7},{5,6},{6,5},{7,4},{8,11},{9,10},{10,... | collective-permute-start | bytes 491528 | tf_op jit(solution)/shard_map/ppermute | solution.py:354
  23.5 2.0 %shard_map.106 = (bf16[2,2,160,256]{3,2,1,0:T(8,128)(2,1)}, bf16[2,2,160,256]{3,2,1,0:T(8,128)(2,1)}) custom-call(bf16[2,160,256]{2,1,0:T(8,128)(2,1)} %get-tuple-element.93.refs_0_, bf16[2,160,256]{2,1,0:T(8,128)(2,1)} %collective-permute-done.11.refs_1_, bf16[2,160,256]{2,1,0:T(8,128)(2,1)} %collective-permute-done.12.refs_2_, ...), custom_call_target="tpu_custom_call" | custom-call | flops 2000000000 | bytes 1000000 | tf_op jit(solution)/shard_map/pallas_call | solution.py:407
  25.6 1.6 %collective-permute-start.17 = (bf16[2,2,160,256]{3,2,1,0:T(8,128)(2,1)}, bf16[2,2,160,256]{3,2,1,0:T(8,128)(2,1)}, u32[]{:S(2)}, u32[]{:S(2)}) collective-permute-start(bf16[2,2,160,256]{3,2,1,0:T(8,128)(2,1)} %get-tuple-element.97), channel_id=1, source_target_pairs={{0,4},{1,5},{2,6},{3,7},{4,0},{5,1},{6,2},{7,3},{8,12},{9,13},{10,... | collective-permute-start | bytes 983048 | tf_op jit(solution)/shard_map/ppermute | solution.py:362
  27.3 1.7 %collective-permute-done.5 = bf16[2,160,256]{2,1,0:T(8,128)(2,1)} collective-permute-done((bf16[2,160,256]{2,1,0:T(8,128)(2,1)}, bf16[2,160,256]{2,1,0:T(8,128)(2,1)}, u32[]{:S(2)}, u32[]{:S(2)}) %collective-permute-start.5) | collective-permute-done | bytes 163872 | tf_op jit(solution)/shard_map/ppermute | solution.py:354
  29.2 1.8 %collective-permute-start.15 = (bf16[2,160,256]{2,1,0:T(8,128)(2,1)}, bf16[2,160,256]{2,1,0:T(8,128)(2,1)}, u32[]{:S(2)}, u32[]{:S(2)}) collective-permute-start(bf16[2,160,256]{2,1,0:T(8,128)(2,1)} %get-tuple-element.77), channel_id=1, source_target_pairs={{0,2},{1,3},{2,0},{3,1},{4,6},{5,7},{6,4},{7,5},{8,10},{9,11},{10,... | collective-permute-start | bytes 491528 | tf_op jit(solution)/shard_map/ppermute | solution.py:354
  31.0 11.7 %shard_map.105 = (bf16[2,2,80,256]{3,2,1,0:T(8,128)(2,1)}, bf16[2,2,80,256]{3,2,1,0:T(8,128)(2,1)}, bf16[2,2,80,256]{3,2,1,0:T(8,128)(2,1)}, bf16[2,2,80,256]{3,...) custom-call(s32[64]{0:T(128)} %get-tuple-element.66.refs_0_, ...), custom_call_target="tpu_custom_call" | custom-call | flops 2000000000 | bytes 1000000 | tf_op jit(solution)/shard_map/pallas_call | solution.py:425
  42.8 2.8 %collective-permute-start.19 = (bf16[2,2,2,80,256]{4,3,2,1,0:T(8,128)(2,1)}, bf16[2,2,2,80,256]{4,3,2,1,0:T(8,128)(2,1)}, u32[]{:S(2)}, u32[]{:S(2)}) collective-permute-start(bf16[2,2,2,80,256]{4,3,2,1,0:T(8,128)(2,1)} %get-tuple-element.103), channel_id=1, source_target_pairs={{0,4},{1,5},{2,6},{3,7},{4,0},{5,1},{6,2},{7,3},{8,12},{9,13},{10,... | collective-permute-start | bytes 983048 | tf_op jit(solution)/shard_map/ppermute | solution.py:362
  47.7 11.8 %shard_map.107 = (bf16[2,2,80,256]{3,2,1,0:T(8,128)(2,1)}, bf16[2,2,80,256]{3,2,1,0:T(8,128)(2,1)}, bf16[2,2,80,256]{3,2,1,0:T(8,128)(2,1)}, bf16[2,2,80,256]{3,...) custom-call(s32[64]{0:T(128)} %get-tuple-element.66.refs_0_, ...), custom_call_target="tpu_custom_call" | custom-call | flops 2000000000 | bytes 1000000 | tf_op jit(solution)/shard_map/pallas_call | solution.py:425
  59.5 1.7 %collective-permute-start.24 = (bf16[2,2,2,80,256]{4,3,2,1,0:T(8,128)(2,1)}, bf16[2,2,2,80,256]{4,3,2,1,0:T(8,128)(2,1)}, u32[]{:S(2)}, u32[]{:S(2)}) collective-permute-start(bf16[2,2,2,80,256]{4,3,2,1,0:T(8,128)(2,1)} %get-tuple-element.115), channel_id=1, source_target_pairs={{0,4},{1,5},{2,6},{3,7},{4,0},{5,1},{6,2},{7,3},{8,12},{9,13},{10,... | collective-permute-start | bytes 983048 | tf_op jit(solution)/shard_map/ppermute | solution.py:362
  62.9 2.3 %shard_map.109 = (bf16[2,160,256]{2,1,0:T(8,128)(2,1)}, bf16[2,160,256]{2,1,0:T(8,128)(2,1)}, bf16[2,160,256]{2,1,0:T(8,128)(2,1)}, bf16[2,160,256]{2,1,0:T(8,128)(2,1)}) custom-call(bf16[4,2,160,256]{3,2,1,0:T(8,128)(2,1)} %bitcast.34, bf16[2,2,160,256]{3,2,1,0:T(8,128)(2,1)} %bitcast.29.refs_1_, bf16[2,2,160,256]{3,2,1,0:T(8,128)(2,1)} %bitcast.30.refs_2_), custom_call_target="tpu_custom_call" | custom-call | tf_op jit(solution)/shard_map/pallas_call | solution.py:460
  65.9 2.3 %collective-permute-done.22.refs_6_ = bf16[2,160,256]{2,1,0:T(8,128)(2,1)} collective-permute-done((bf16[2,160,256]{2,1,0:T(8,128)(2,1)}, bf16[2,160,256]{2,1,0:T(8,128)(2,1)}, u32[]{:S(2)}, u32[]{:S(2)}) %collective-permute-start.22) | collective-permute-done | bytes 163872 | tf_op jit(solution)/shard_map/ppermute | solution.py:354
  71.5 2.3 %shard_map.110 = (bf16[2,160,256]{2,1,0:T(8,128)(2,1)}, bf16[2,160,256]{2,1,0:T(8,128)(2,1)}, bf16[2,160,256]{2,1,0:T(8,128)(2,1)}, bf16[2,160,256]{2,1,0:T(8,128)(2,1)}) custom-call(bf16[4,2,160,256]{3,2,1,0:T(8,128)(2,1)} %bitcast.35, bf16[2,2,160,256]{3,2,1,0:T(8,128)(2,1)} %bitcast.32.refs_1_, bf16[2,2,160,256]{3,2,1,0:T(8,128)(2,1)} %bitcast.33.refs_2_), custom_call_target="tpu_custom_call" | custom-call | tf_op jit(solution)/shard_map/pallas_call | solution.py:460
  76.1 2.2 %shard_map.111 = (bf16[256,1280]{1,0:T(8,128)(2,1)}, bf16[256,1280]{1,0:T(8,128)(2,1)}) custom-call(bf16[2,160,256]{2,1,0:T(8,128)(2,1)} %get-tuple-element.113.refs_0_, bf16[2,160,256]{2,1,0:T(8,128)(2,1)} %collective-permute-done.29.refs_1_, bf16[2,160,256]{2,1,0:T(8,128)(2,1)} %collective-permute-done.30.refs_2_, ...), custom_call_target="tpu_custom_call" | custom-call | flops 3000000000 | bytes 1000000 | tf_op jit(solution)/shard_map/pallas_call | solution.py:494
  78.7 2.8 %shard_map.108 = (bf16[256,1280]{1,0:T(8,128)(2,1)}, bf16[256,1280]{1,0:T(8,128)(2,1)}) custom-call(bf16[2,160,256]{2,1,0:T(8,128)(2,1)} %bitcast.43, bf16[2,160,256]{2,1,0:T(8,128)(2,1)} %collective-permute-done.8.refs_1_, bf16[2,160,256]{2,1,0:T(8,128)(2,1)} %collective-permute-done.9.refs_2_, bf16[2,160,256]{2,1,0:T(8,128)(2,1)} %collective-permute-done.10.refs_3_, ...), custom_call_target="tpu_custom_call" | custom-call | flops 3000000000 | bytes 1000000 | tf_op jit(solution)/shard_map/pallas_call | solution.py:494
  81.5 1.6 %collective-permute-done.27.refs_2_ = bf16[2,160,256]{2,1,0:T(8,128)(2,1)} collective-permute-done((bf16[2,160,256]{2,1,0:T(8,128)(2,1)}, bf16[2,160,256]{2,1,0:T(8,128)(2,1)}, u32[]{:S(2)}, u32[]{:S(2)}) %collective-permute-start.27) | collective-permute-done | bytes 163872 | tf_op jit(solution)/shard_map/ppermute | solution.py:354
  83.1 2.6 %collective-permute-done.28.refs_3_ = bf16[2,160,256]{2,1,0:T(8,128)(2,1)} collective-permute-done((bf16[2,160,256]{2,1,0:T(8,128)(2,1)}, bf16[2,160,256]{2,1,0:T(8,128)(2,1)}, u32[]{:S(2)}, u32[]{:S(2)}) %collective-permute-start.28) | collective-permute-done | bytes 163872 | tf_op jit(solution)/shard_map/ppermute | solution.py:354
  85.8 2.2 %shard_map.112 = (bf16[256,1280]{1,0:T(8,128)(2,1)}, bf16[256,1280]{1,0:T(8,128)(2,1)}) custom-call(bf16[2,160,256]{2,1,0:T(8,128)(2,1)} %get-tuple-element.117.refs_0_, bf16[2,160,256]{2,1,0:T(8,128)(2,1)} %collective-permute-done.26.refs_1_, bf16[2,160,256]{2,1,0:T(8,128)(2,1)} %collective-permute-done.27.refs_2_, ...), custom_call_target="tpu_custom_call", output_to_operand_aliasing={{0}: (4, {}), {1}: (5, {})} | custom-call | flops 3000000000 | bytes 1000000 | tf_op jit(solution)/shard_map/pallas_call | solution.py:494
  (57 shorter events, 14.9 us)
Async XLA Ops:
  3.3 11.0 %collective-permute-start = (bf16[2,160,256]{2,1,0:T(8,128)(2,1)}, bf16[2,160,256]{2,1,0:T(8,128)(2,1)}, u32[]{:S(2)}, u32[]{:S(2)}) collective-permute-start(bf16[2,160,256]{2,1,0:T(8,128)(2,1)} %get-tuple-element.68), channel_id=1, source_target_pairs={{0,1},{1,0},{2,3},{3,2},{4,5},{5,4},{6,7},{7,6},{8,9},{9,8},{10,11... | collective-permute-start | bytes 491528 | tf_op jit(solution)/shard_map/ppermute | solution.py:354
  3.8 10.6 %collective-permute-start.1 = (bf16[2,160,256]{2,1,0:T(8,128)(2,1)}, bf16[2,160,256]{2,1,0:T(8,128)(2,1)}, u32[]{:S(2)}, u32[]{:S(2)}) collective-permute-start(bf16[2,160,256]{2,1,0:T(8,128)(2,1)} %get-tuple-element.69), channel_id=1, source_target_pairs={{0,2},{1,3},{2,0},{3,1},{4,6},{5,7},{6,4},{7,5},{8,10},{9,11},{10,... | collective-permute-start | bytes 491528 | tf_op jit(solution)/shard_map/ppermute | solution.py:354
  6.5 12.4 %collective-permute-start.11 = (bf16[2,160,256]{2,1,0:T(8,128)(2,1)}, bf16[2,160,256]{2,1,0:T(8,128)(2,1)}, u32[]{:S(2)}, u32[]{:S(2)}) collective-permute-start(bf16[2,160,256]{2,1,0:T(8,128)(2,1)} %get-tuple-element.90), channel_id=1, source_target_pairs={{0,1},{1,0},{2,3},{3,2},{4,5},{5,4},{6,7},{7,6},{8,9},{9,8},{10,11... | collective-permute-start | bytes 491528 | tf_op jit(solution)/shard_map/ppermute | solution.py:354
  6.6 12.4 %collective-permute-start.12 = (bf16[2,160,256]{2,1,0:T(8,128)(2,1)}, bf16[2,160,256]{2,1,0:T(8,128)(2,1)}, u32[]{:S(2)}, u32[]{:S(2)}) collective-permute-start(bf16[2,160,256]{2,1,0:T(8,128)(2,1)} %get-tuple-element.91), channel_id=1, source_target_pairs={{0,2},{1,3},{2,0},{3,1},{4,6},{5,7},{6,4},{7,5},{8,10},{9,11},{10,... | collective-permute-start | bytes 491528 | tf_op jit(solution)/shard_map/ppermute | solution.py:354
  16.8 12.4 %collective-permute-start.6 = (bf16[2,2,160,256]{3,2,1,0:T(8,128)(2,1)}, bf16[2,2,160,256]{3,2,1,0:T(8,128)(2,1)}, u32[]{:S(2)}, u32[]{:S(2)}) collective-permute-start(bf16[2,2,160,256]{3,2,1,0:T(8,128)(2,1)} %get-tuple-element.83), channel_id=1, source_target_pairs={{0,4},{1,5},{2,6},{3,7},{4,0},{5,1},{6,2},{7,3},{8,12},{9,13},{10,... | collective-permute-start | bytes 983048 | tf_op jit(solution)/shard_map/ppermute | solution.py:362
  18.5 12.5 %collective-permute-start.7 = (bf16[2,2,160,256]{3,2,1,0:T(8,128)(2,1)}, bf16[2,2,160,256]{3,2,1,0:T(8,128)(2,1)}, u32[]{:S(2)}, u32[]{:S(2)}) collective-permute-start(bf16[2,2,160,256]{3,2,1,0:T(8,128)(2,1)} %get-tuple-element.84), channel_id=1, source_target_pairs={{0,1},{1,0},{2,3},{3,2},{4,8},{5,9},{6,10},{7,11},{8,4},{9,5},{10,... | collective-permute-start | bytes 983048 | tf_op jit(solution)/shard_map/ppermute | solution.py:362
  25.6 20.4 %collective-permute-start.17 = (bf16[2,2,160,256]{3,2,1,0:T(8,128)(2,1)}, bf16[2,2,160,256]{3,2,1,0:T(8,128)(2,1)}, u32[]{:S(2)}, u32[]{:S(2)}) collective-permute-start(bf16[2,2,160,256]{3,2,1,0:T(8,128)(2,1)} %get-tuple-element.97), channel_id=1, source_target_pairs={{0,4},{1,5},{2,6},{3,7},{4,0},{5,1},{6,2},{7,3},{8,12},{9,13},{10,... | collective-permute-start | bytes 983048 | tf_op jit(solution)/shard_map/ppermute | solution.py:362
  27.2 20.2 %collective-permute-start.18 = (bf16[2,2,160,256]{3,2,1,0:T(8,128)(2,1)}, bf16[2,2,160,256]{3,2,1,0:T(8,128)(2,1)}, u32[]{:S(2)}, u32[]{:S(2)}) collective-permute-start(bf16[2,2,160,256]{3,2,1,0:T(8,128)(2,1)} %get-tuple-element.98), channel_id=1, source_target_pairs={{0,1},{1,0},{2,3},{3,2},{4,8},{5,9},{6,10},{7,11},{8,4},{9,5},{10,... | collective-permute-start | bytes 983048 | tf_op jit(solution)/shard_map/ppermute | solution.py:362
  28.9 13.8 %collective-permute-start.14 = (bf16[2,160,256]{2,1,0:T(8,128)(2,1)}, bf16[2,160,256]{2,1,0:T(8,128)(2,1)}, u32[]{:S(2)}, u32[]{:S(2)}) collective-permute-start(bf16[2,160,256]{2,1,0:T(8,128)(2,1)} %get-tuple-element.76), channel_id=1, source_target_pairs={{0,1},{1,0},{2,3},{3,2},{4,5},{5,4},{6,7},{7,6},{8,9},{9,8},{10,11... | collective-permute-start | bytes 491528 | tf_op jit(solution)/shard_map/ppermute | solution.py:354
  29.2 16.3 %collective-permute-start.15 = (bf16[2,160,256]{2,1,0:T(8,128)(2,1)}, bf16[2,160,256]{2,1,0:T(8,128)(2,1)}, u32[]{:S(2)}, u32[]{:S(2)}) collective-permute-start(bf16[2,160,256]{2,1,0:T(8,128)(2,1)} %get-tuple-element.77), channel_id=1, source_target_pairs={{0,2},{1,3},{2,0},{3,1},{4,6},{5,7},{6,4},{7,5},{8,10},{9,11},{10,... | collective-permute-start | bytes 491528 | tf_op jit(solution)/shard_map/ppermute | solution.py:354
  31.0 14.9 %collective-permute-start.16 = (bf16[2,160,256]{2,1,0:T(8,128)(2,1)}, bf16[2,160,256]{2,1,0:T(8,128)(2,1)}, u32[]{:S(2)}, u32[]{:S(2)}) collective-permute-start(bf16[2,160,256]{2,1,0:T(8,128)(2,1)} %get-tuple-element.78), channel_id=1, source_target_pairs={{0,3},{1,2},{2,1},{3,0},{4,7},{5,6},{6,5},{7,4},{8,11},{9,10},{10,... | collective-permute-start | bytes 491528 | tf_op jit(solution)/shard_map/ppermute | solution.py:354
  42.8 18.6 %collective-permute-start.19 = (bf16[2,2,2,80,256]{4,3,2,1,0:T(8,128)(2,1)}, bf16[2,2,2,80,256]{4,3,2,1,0:T(8,128)(2,1)}, u32[]{:S(2)}, u32[]{:S(2)}) collective-permute-start(bf16[2,2,2,80,256]{4,3,2,1,0:T(8,128)(2,1)} %get-tuple-element.103), channel_id=1, source_target_pairs={{0,4},{1,5},{2,6},{3,7},{4,0},{5,1},{6,2},{7,3},{8,12},{9,13},{10,... | collective-permute-start | bytes 983048 | tf_op jit(solution)/shard_map/ppermute | solution.py:362
  45.5 15.8 %collective-permute-start.20 = (bf16[2,2,2,80,256]{4,3,2,1,0:T(8,128)(2,1)}, bf16[2,2,2,80,256]{4,3,2,1,0:T(8,128)(2,1)}, u32[]{:S(2)}, u32[]{:S(2)}) collective-permute-start(bf16[2,2,2,80,256]{4,3,2,1,0:T(8,128)(2,1)} %get-tuple-element.104), channel_id=1, source_target_pairs={{0,1},{1,0},{2,3},{3,2},{4,8},{5,9},{6,10},{7,11},{8,4},{9,5},{10,... | collective-permute-start | bytes 983048 | tf_op jit(solution)/shard_map/ppermute | solution.py:362
  45.9 13.7 %collective-permute-start.8 = (bf16[2,160,256]{2,1,0:T(8,128)(2,1)}, bf16[2,160,256]{2,1,0:T(8,128)(2,1)}, u32[]{:S(2)}, u32[]{:S(2)}) collective-permute-start(bf16[2,160,256]{2,1,0:T(8,128)(2,1)} %bitcast.40), channel_id=1, source_target_pairs={{0,1},{1,0},{2,3},{3,2},{4,5},{5,4},{6,7},{7,6},{8,9},{9,8},{10,11... | collective-permute-start | bytes 491528 | tf_op jit(solution)/shard_map/ppermute | solution.py:354
  46.1 15.2 %collective-permute-start.9 = (bf16[2,160,256]{2,1,0:T(8,128)(2,1)}, bf16[2,160,256]{2,1,0:T(8,128)(2,1)}, u32[]{:S(2)}, u32[]{:S(2)}) collective-permute-start(bf16[2,160,256]{2,1,0:T(8,128)(2,1)} %bitcast.39), channel_id=1, source_target_pairs={{0,2},{1,3},{2,0},{3,1},{4,6},{5,7},{6,4},{7,5},{8,10},{9,11},{10,... | collective-permute-start | bytes 491528 | tf_op jit(solution)/shard_map/ppermute | solution.py:354
  47.5 13.8 %collective-permute-start.10 = (bf16[2,160,256]{2,1,0:T(8,128)(2,1)}, bf16[2,160,256]{2,1,0:T(8,128)(2,1)}, u32[]{:S(2)}, u32[]{:S(2)}) collective-permute-start(bf16[2,160,256]{2,1,0:T(8,128)(2,1)} %bitcast.38), channel_id=1, source_target_pairs={{0,3},{1,2},{2,1},{3,0},{4,7},{5,6},{6,5},{7,4},{8,11},{9,10},{10,... | collective-permute-start | bytes 491528 | tf_op jit(solution)/shard_map/ppermute | solution.py:354
  59.5 10.4 %collective-permute-start.24 = (bf16[2,2,2,80,256]{4,3,2,1,0:T(8,128)(2,1)}, bf16[2,2,2,80,256]{4,3,2,1,0:T(8,128)(2,1)}, u32[]{:S(2)}, u32[]{:S(2)}) collective-permute-start(bf16[2,2,2,80,256]{4,3,2,1,0:T(8,128)(2,1)} %get-tuple-element.115), channel_id=1, source_target_pairs={{0,4},{1,5},{2,6},{3,7},{4,0},{5,1},{6,2},{7,3},{8,12},{9,13},{10,... | collective-permute-start | bytes 983048 | tf_op jit(solution)/shard_map/ppermute | solution.py:362
  61.2 8.8 %collective-permute-start.25 = (bf16[2,2,2,80,256]{4,3,2,1,0:T(8,128)(2,1)}, bf16[2,2,2,80,256]{4,3,2,1,0:T(8,128)(2,1)}, u32[]{:S(2)}, u32[]{:S(2)}) collective-permute-start(bf16[2,2,2,80,256]{4,3,2,1,0:T(8,128)(2,1)} %get-tuple-element.116), channel_id=1, source_target_pairs={{0,1},{1,0},{2,3},{3,2},{4,8},{5,9},{6,10},{7,11},{8,4},{9,5},{10,... | collective-permute-start | bytes 983048 | tf_op jit(solution)/shard_map/ppermute | solution.py:362
  65.2 8.7 %collective-permute-start.29 = (bf16[2,160,256]{2,1,0:T(8,128)(2,1)}, bf16[2,160,256]{2,1,0:T(8,128)(2,1)}, u32[]{:S(2)}, u32[]{:S(2)}) collective-permute-start(bf16[2,160,256]{2,1,0:T(8,128)(2,1)} %get-tuple-element.121), channel_id=1, source_target_pairs={{0,1},{1,0},{2,3},{3,2},{4,5},{5,4},{6,7},{7,6},{8,9},{9,8},{10,11... | collective-permute-start | bytes 491528 | tf_op jit(solution)/shard_map/ppermute | solution.py:354
  65.2 8.7 %collective-permute-start.30 = (bf16[2,160,256]{2,1,0:T(8,128)(2,1)}, bf16[2,160,256]{2,1,0:T(8,128)(2,1)}, u32[]{:S(2)}, u32[]{:S(2)}) collective-permute-start(bf16[2,160,256]{2,1,0:T(8,128)(2,1)} %get-tuple-element.122), channel_id=1, source_target_pairs={{0,2},{1,3},{2,0},{3,1},{4,6},{5,7},{6,4},{7,5},{8,10},{9,11},{10,... | collective-permute-start | bytes 491528 | tf_op jit(solution)/shard_map/ppermute | solution.py:354
  70.0 8.4 %collective-permute-start.21 = (bf16[2,160,256]{2,1,0:T(8,128)(2,1)}, bf16[2,160,256]{2,1,0:T(8,128)(2,1)}, u32[]{:S(2)}, u32[]{:S(2)}) collective-permute-start(bf16[2,160,256]{2,1,0:T(8,128)(2,1)} %bitcast.37), channel_id=1, source_target_pairs={{0,1},{1,0},{2,3},{3,2},{4,5},{5,4},{6,7},{7,6},{8,9},{9,8},{10,11... | collective-permute-start | bytes 491528 | tf_op jit(solution)/shard_map/ppermute | solution.py:354
  70.1 8.6 %collective-permute-start.23 = (bf16[2,160,256]{2,1,0:T(8,128)(2,1)}, bf16[2,160,256]{2,1,0:T(8,128)(2,1)}, u32[]{:S(2)}, u32[]{:S(2)}) collective-permute-start(bf16[2,160,256]{2,1,0:T(8,128)(2,1)} %bitcast.36), channel_id=1, source_target_pairs={{0,3},{1,2},{2,1},{3,0},{4,7},{5,6},{6,5},{7,4},{8,11},{9,10},{10,... | collective-permute-start | bytes 491528 | tf_op jit(solution)/shard_map/ppermute | solution.py:354
  73.9 9.2 %collective-permute-start.27 = (bf16[2,160,256]{2,1,0:T(8,128)(2,1)}, bf16[2,160,256]{2,1,0:T(8,128)(2,1)}, u32[]{:S(2)}, u32[]{:S(2)}) collective-permute-start(bf16[2,160,256]{2,1,0:T(8,128)(2,1)} %get-tuple-element.119), channel_id=1, source_target_pairs={{0,2},{1,3},{2,0},{3,1},{4,6},{5,7},{6,4},{7,5},{8,10},{9,11},{10,... | collective-permute-start | bytes 491528 | tf_op jit(solution)/shard_map/ppermute | solution.py:354
  75.2 10.5 %collective-permute-start.28 = (bf16[2,160,256]{2,1,0:T(8,128)(2,1)}, bf16[2,160,256]{2,1,0:T(8,128)(2,1)}, u32[]{:S(2)}, u32[]{:S(2)}) collective-permute-start(bf16[2,160,256]{2,1,0:T(8,128)(2,1)} %get-tuple-element.120), channel_id=1, source_target_pairs={{0,3},{1,2},{2,1},{3,0},{4,7},{5,6},{6,5},{7,4},{8,11},{9,10},{10,... | collective-permute-start | bytes 491528 | tf_op jit(solution)/shard_map/ppermute | solution.py:354
  (10 other events, 64.2 us)
